TPU v7x, 512 devices: a whole 4x4x16 slice. The times are simulated.
512 devices in a mesh: slab: 128 (over y, z, core), sub: 4 (over x).
Axes of the slice: x: 4, y: 4, z: 16, core: 2. Of those that a mesh axis runs over, the one named last changes fastest.
Arguments:
- covariates: bfloat16 [1048576, 128], P(('slab', 'sub')), may hold values from -6 to 6
- partition_slot: int32 [2, 1048576], P(None, ('slab', 'sub')), may hold values from 0 to 2047, as said below
- in_weight: bfloat16 [128, 256], replicated, may hold values from -0.5 to 0.5
- in_bias: float32 [256], replicated, may hold values from -3 to 3
- out_weight: bfloat16 [3, 256], replicated, may hold values from -0.375 to 0.375
- out_bias: float32 [3], replicated, may hold values from -2.5 to 2.5
- gradients: float32 [2, 2, 1048576], P(None, None, ('slab', 'sub')), may hold values from -6 to 6
- areas: float32 [1048576], P(('slab', 'sub')), may hold values from 0.02 to 0.2
- corners: int32 [2, 3, 1048576], P(None, None, ('slab', 'sub')), may hold values from 0 to 127, as said below
- tile_rows: int32 [8192], P(('slab', 'sub')), may hold values from 0 to 2047, as said below
- tile_cols: int32 [8192], P(('slab', 'sub')), may hold values from 0 to 2047, as said below
- probe: bfloat16 [64, 262144], P(None, ('slab', 'sub')), may hold values from -6 to 6
Outputs:
- applied: float32 [64, 262144], P(None, ('slab', 'sub'))
Inputs may be any that keep to these rules, and one draw needn't show every extreme that they name: The pairs (2048 * partition_slot[0,r] + partition_slot[1,r]) form a permutation of the rows; of the 2048 raster rows of each device, equally many go to every device; partition_slot[0] is below the number of devices and partition_slot[1] below 2048. `corners`: an element's three row positions are distinct, and so are its three column positions. `tile_rows`: the 16 tiles of a device name row blocks of devices with its own slab index; at most 8 of them name blocks of any one device, and in every slab exactly 8 of the tiles of each device name blocks of one common device. `tile_cols`: each tile names a column block of a device whose slab index differs from that of the tile's device by at most one.
All inputs are finite; a program needn't handle non-finite values.
Results may differ from a plain program's by a relative error of at most 0.0053.
Values may be sent and summed in bfloat16 or wider, within the bound.
No kernel may reach another device: no remote copies, remote signals or barrier semaphores. Data moves between devices by JAX's collectives and lax.ppermute only.
A program may use at most 64 MiB of HBM per device.

v0:
```python
import jax
import jax.numpy as jnp
from jax import lax
from jax.sharding import PartitionSpec as P

BLK = 128


def padded(shard, sides, width):
    for axis, dim in sides:
        size, length = (lax.axis_size(axis), shard.shape[dim])
        up = [(i, (i + 1) % size) for i in range(size - 1)]
        down = [(j, i) for i, j in up]
        last = lax.slice_in_dim(shard, length - width, length, axis=dim)
        initial = lax.slice_in_dim(shard, 0, width, axis=dim)
        before = lax.ppermute(last, axis, up)
        after = lax.ppermute(initial, axis, down)
        shard = jnp.concatenate([before, shard, after], axis=dim)
    return shard


def features_to_params(feature_rows, in_weight, in_bias, out_weight, out_bias):
    pre_act = jnp.dot(feature_rows, in_weight, preferred_element_type=jnp.float32) + in_bias
    hidden = jax.nn.gelu(pre_act, approximate=True).astype(jnp.bfloat16)
    outputs = lax.dot_general(
        out_weight, hidden, (((1,), (1,)), ((), ())), preferred_element_type=jnp.float32
    )
    return outputs + out_bias[:, None]


def element_matrices(params, gradients, areas):
    kappa_sq = jnp.exp(params[0])
    aniso_scale = jnp.exp(params[1])
    coupling = 0.9 * jnp.tanh(params[2])
    grad_x = [gradients[0, 0], gradients[0, 1], -(gradients[0, 0] + gradients[0, 1])]
    grad_y = [gradients[1, 0], gradients[1, 1], -(gradients[1, 0] + gradients[1, 1])]
    rows_out = []
    for corner_a in range(3):
        matrix_row = []
        for corner_b in range(3):
            stiffness = grad_x[corner_a] * grad_x[corner_b] + grad_y[corner_a] * grad_y[corner_b]
            stiffness = stiffness + coupling * (
                grad_x[corner_a] * grad_y[corner_b] + grad_y[corner_a] * grad_x[corner_b]
            )
            mass_term = kappa_sq * (2.0 if corner_a == corner_b else 1.0)
            matrix_row.append(areas * (aniso_scale * stiffness + mass_term))
        rows_out.append(jnp.stack(matrix_row))
    return jnp.stack(rows_out).astype(jnp.bfloat16)


def build_tiles(element_k, row_pos, col_pos, tile_count):
    positions = lax.broadcasted_iota(jnp.int32, (1, 1, BLK), 2)
    row_hit = row_pos[:, :, None] == positions
    col_hot = (col_pos[:, :, None] == positions).astype(jnp.bfloat16)
    zero_value = jnp.zeros((), jnp.bfloat16)
    weighted = []
    for corner_b in range(3):
        column_sum = jnp.zeros(row_hit.shape[1:], jnp.bfloat16)
        for corner_a in range(3):
            column_sum = column_sum + jnp.where(
                row_hit[corner_a], element_k[corner_a, corner_b][:, None], zero_value
            )
        weighted.append(column_sum)
    per_tile = row_pos.shape[1] // tile_count
    weighted = jnp.stack(weighted).reshape(3, tile_count, per_tile, BLK)
    col_hot = col_hot.reshape(3, tile_count, per_tile, BLK)
    return jnp.einsum(
        "btei,btej->tij", weighted, col_hot, preferred_element_type=jnp.float32
    ).astype(jnp.bfloat16)


def apply_tiles(tile_mats, column_blocks, xblocks):
    picked = xblocks[:, column_blocks, :]
    return jnp.einsum("csk,sik->csi", picked, tile_mats, preferred_element_type=jnp.float32)


def collect_rows(contrib, local_block, blk_dev):
    block_hot = (local_block[:, None] == jnp.arange(blk_dev, dtype=jnp.int32)[None, :]).astype(
        jnp.float32
    )
    summed = jnp.einsum("csi,sl->cli", contrib, block_hot, precision=lax.Precision.HIGHEST)
    return summed.reshape(contrib.shape[0], blk_dev * contrib.shape[2])


def local(
    covariates,
    partition_slot,
    in_weight,
    in_bias,
    out_weight,
    out_bias,
    gradients,
    areas,
    corners,
    tile_rows,
    tile_cols,
    probe,
):
    slab_count = lax.axis_size("slab")
    sub_count = lax.axis_size("sub")
    elem_dev = partition_slot.shape[1]
    per_peer = elem_dev // (slab_count * sub_count)
    sort_key = partition_slot[0] * elem_dev + partition_slot[1]
    by_slot = jnp.argsort(sort_key)
    dest_local = partition_slot[1][by_slot].reshape(slab_count, sub_count, per_peer)
    outgoing = covariates[by_slot].reshape(slab_count, sub_count, per_peer, covariates.shape[1])
    arrived, arrived_local = (
        lax.all_to_all(
            lax.all_to_all(outgoing, "slab", split_axis=0, concat_axis=0, tiled=True),
            "sub",
            split_axis=1,
            concat_axis=1,
            tiled=True,
        ),
        lax.all_to_all(
            lax.all_to_all(dest_local, "slab", split_axis=0, concat_axis=0, tiled=True),
            "sub",
            split_axis=1,
            concat_axis=1,
            tiled=True,
        ),
    )
    placed = (
        jnp.zeros_like(covariates)
        .at[arrived_local.reshape(-1)]
        .set(arrived.reshape(elem_dev, covariates.shape[1]))
    )
    params = features_to_params(placed, in_weight, in_bias, out_weight, out_bias)
    element_k = element_matrices(params, gradients, areas)
    tile_count = tile_rows.shape[0]
    capacity = tile_count // 2
    blk_dev = probe.shape[1] // BLK
    slab_index = lax.axis_index("slab")
    owner_sub = tile_rows // blk_dev % sub_count
    local_block = tile_rows % blk_dev
    sub_hits = (owner_sub[:, None] == jnp.arange(sub_count, dtype=jnp.int32)[None, :]).astype(
        jnp.int32
    )
    before = jnp.sum((jnp.cumsum(sub_hits, axis=0) - sub_hits) * sub_hits, axis=1)
    slot_of = owner_sub * capacity + before
    slot_count = sub_count * capacity
    slot_match = slot_of[None, :] == jnp.arange(slot_count, dtype=jnp.int32)[:, None]
    filled = jnp.any(slot_match, axis=1)
    source = jnp.sum(
        slot_match.astype(jnp.int32) * jnp.arange(tile_count, dtype=jnp.int32)[None, :], axis=1
    )
    slot_block = jnp.where(filled, local_block[source], -1)
    slot_column = jnp.where(filled, tile_cols[source], 0)
    base_block = (slab_index - 1) * sub_count * blk_dev
    grouped = lax.all_gather(probe, "sub", axis=1, tiled=True)
    widened = padded(grouped, (("slab", 1),), grouped.shape[1])
    xblocks = widened.reshape(widened.shape[0], -1, BLK)
    zero_value = jnp.zeros((), jnp.bfloat16)
    tile_mats = build_tiles(element_k, corners[0], corners[1], tile_count)
    outgoing_tiles = jnp.where(filled[:, None, None], tile_mats[source], zero_value).reshape(
        sub_count, capacity, BLK, BLK
    )
    slot_info = (
        jnp.stack([slot_block, slot_column]).reshape(2, sub_count, capacity).transpose(1, 0, 2)
    )
    got_tiles, got_info = (
        lax.all_to_all(outgoing_tiles, "sub", split_axis=0, concat_axis=0, tiled=True),
        lax.all_to_all(slot_info, "sub", split_axis=0, concat_axis=0, tiled=True),
    )
    arrived_block = got_info[:, 0, :].reshape(-1)
    arrived_column = got_info[:, 1, :].reshape(-1)
    column_local = jnp.where(arrived_block >= 0, arrived_column - base_block, 0)
    contrib = apply_tiles(got_tiles.reshape(slot_count, BLK, BLK), column_local, xblocks)
    return collect_rows(contrib, arrived_block, blk_dev)


def solution(mesh):
    placed = (
        P(("slab", "sub"), None),
        P(None, ("slab", "sub")),
        P(),
        P(),
        P(),
        P(),
        P(None, None, ("slab", "sub")),
        P(("slab", "sub")),
        P(None, None, ("slab", "sub")),
        P(("slab", "sub")),
        P(("slab", "sub")),
        P(None, ("slab", "sub")),
    )
    return jax.shard_map(
        local, mesh=mesh, in_specs=placed, out_specs=P(None, ("slab", "sub")), check_vma=False
    )
```

profile of v0, /device:TPU:1, one launch (start us, length us, event | category | flops | bytes accessed | tf_op | source)
XLA Modules:
  0.0 184.8 jit_solution(560233252852476157)
XLA Ops:
  0.0 0.8 slice_multiply_fusion
  0.8 5.0 %sort.17 = (s32[2048]{0:T(1024)}, s32[2048]{0:T(1024)S(1)}) sort(s32[2048]{0:T(1024)S(1)} %add.203, s32[2048]{0:T(1024)S(1)} %iota.24), dimensions={0}, to_apply=%region_4.5 | sort | flops 22528 | bytes 32768 | tf_op jit(solution)/shard_map/jit(argsort)/sort | solution.py:104
  5.9 11.8 %gather_fusion.2 = s32[2048]{0:T(1024)S(1)} fusion(s32[2048]{0:T(1024)S(1)} %bitcast.65, s32[2048]{0:T(1024)S(1)} %fusion.38), kind=kCustom, calls=%fused_computation.2 | custom fusion | bytes 24576 | tf_op jit(solution)/shard_map/gather | solution.py:105
  17.7 1.1 reshape.243
  18.7 20.6 %all-to-all-start.1 = ((s32[128,4,4]{2,1,0:T(4,128)}), s32[128,4,4]{2,1,0:T(4,128)S(1)}, u32[]{:S(2)}, u32[]{:S(2)}) async-start(s32[128,4,4]{2,1,0:T(4,128)} %reshape.243), calls=%async_computation.1 | async-start | bytes 524288 | tf_op jit(solution)/shard_map/all_to_all | solution.py:116
  39.4 22.4 %all-to-all-done.1 = s32[128,4,4]{2,1,0:T(4,128)S(1)} async-done(((s32[128,4,4]{2,1,0:T(4,128)}), s32[128,4,4]{2,1,0:T(4,128)S(1)}, u32[]{:S(2)}, u32[]{:S(2)}) %all-to-all-start.1) | async-done | bytes 8224 | tf_op jit(solution)/shard_map/all_to_all | solution.py:116
  61.8 0.7 copy.57
  62.5 4.0 %all-to-all-start.2 = ((s32[128,4,4]{0,2,1:T(4,128)}), s32[128,4,4]{0,2,1:T(4,128)S(1)}, u32[]{:S(2)}, u32[]{:S(2)}) async-start(s32[128,4,4]{0,2,1:T(4,128)} %copy.57), calls=%async_computation.2 | async-start | bytes 16384 | tf_op jit(solution)/shard_map/all_to_all | solution.py:115
  66.6 8.0 %gather_fusion.3 = bf16[2048,128]{1,0:T(8,128)(2,1)} fusion(bf16[2048,128]{1,0:T(8,128)(2,1)S(1)} %copy-done, s32[2048]{0:T(1024)S(1)} %fusion.38), kind=kCustom, calls=%fused_computation.3 | custom fusion | bytes 1056768 | tf_op jit(solution)/shard_map/gather | solution.py:106
  74.6 7.6 %all-to-all-start.3 = ((bf16[128,4,4,128]{3,2,1,0:T(4,128)(2,1)}), bf16[128,4,4,128]{3,2,1,0:T(4,128)(2,1)S(1)}, u32[]{:S(2)}, u32[]{:S(2)}) async-start(bf16[128,4,4,128]{3,2,1,0:T(4,128)(2,1)} %bitcast.7), calls=%async_computation.3 | async-start | bytes 1048576 | tf_op jit(solution)/shard_map/all_to_all | solution.py:109
  82.7 0.7 gather_fusion
  83.4 0.7 gather_fusion.1
  85.0 1.1 iota_compare_fusion.1
  86.6 29.0 %all-to-all-done.3 = bf16[128,4,4,128]{3,2,1,0:T(4,128)(2,1)S(1)} async-done(((bf16[128,4,4,128]{3,2,1,0:T(4,128)(2,1)}), bf16[128,4,4,128]{3,2,1,0:T(4,128)(2,1)S(1)}, u32[]{:S(2)}, u32[]{:S(2)}) %all-to-all-start.3) | async-done | bytes 524320 | tf_op jit(solution)/shard_map/all_to_all | solution.py:109
  115.5 1.0 copy.59
  116.5 4.5 %all-to-all-start.4 = ((bf16[128,4,4,128]{3,2,0,1:T(4,128)(2,1)}), bf16[128,4,4,128]{3,2,0,1:T(4,128)(2,1)S(1)}, u32[]{:S(2)}, u32[]{:S(2)}) async-start(bf16[128,4,4,128]{3,2,0,1:T(4,128)(2,1)} %copy.59), calls=%async_computation.4 | async-start | bytes 1048576 | tf_op jit(solution)/shard_map/all_to_all | solution.py:108
  121.1 7.7 %all-to-all-done.4 = bf16[128,4,4,128]{3,2,0,1:T(4,128)(2,1)S(1)} async-done(((bf16[128,4,4,128]{3,2,0,1:T(4,128)(2,1)}), bf16[128,4,4,128]{3,2,0,1:T(4,128)(2,1)S(1)}, u32[]{:S(2)}, u32[]{:S(2)}) %all-to-all-start.4) | async-done | bytes 524320 | tf_op jit(solution)/shard_map/all_to_all | solution.py:108
  128.8 3.2 %all-to-all-start = ((s32[4,2,8]{2,1,0:T(2,128)}), s32[4,2,8]{2,1,0:T(2,128)S(1)}, u32[]{:S(2)}, u32[]{:S(2)}) async-start(s32[4,2,8]{2,1,0:T(2,128)} %copy.56), calls=%async_computation | async-start | bytes 8192 | tf_op jit(solution)/shard_map/all_to_all | solution.py:163
  132.2 6.0 %scatter_custom_fusion = bf16[2048,128]{1,0:T(8,128)(2,1)S(1)} fusion(s32[2048]{0:T(1024)S(1)} %bitcast.83, bf16[2048,128]{1,0:T(8,128)(2,1)S(1)} %bitcast.72, bf16[]{:T(256)} %constant.65.clone.1), kind=kCustom, calls=%fused_computation.57 | custom fusion | bytes 524290 | tf_op jit(solution)/shard_map/scatter | solution.py:126
  138.3 1.0 fusion.1
  139.8 3.1 %fusion.30 = (bf16[1,2048,128]{2,1,0:T(8,128)(2,1)S(1)}, bf16[1,2048,128]{2,1,0:T(8,128)(2,1)S(1)}, bf16[1,2048,128]{2,1,0:T(8,128)(2,1)S(1)}) fusion(pred[3,2048,128]{2,1,0:T(8,128)(4,1)S(1)} %iota_compare_fusion.1, bf16[2048]{0:T(1024)(128)(2,1)S(1)} %get-tuple-element.13, bf16[2048]{0:T(1024)(128)(2,1)S(1)} %get-tuple-element.47, ...), kind=kLoop, calls=%fused_computation.51 | loop fusion | flops 3932160 | bytes 2396160 | tf_op jit(solution)/shard_map/add | solution.py:60
  143.8 1.8 fusion.19
  145.6 0.7 gather_fusion.4
  146.3 1.1 broadcast_select_fusion
  147.5 4.3 %all-to-all-start.5 = ((bf16[4,8,128,128]{3,2,1,0:T(8,128)(2,1)}), bf16[4,8,128,128]{3,2,1,0:T(8,128)(2,1)S(1)}, u32[]{:S(2)}, u32[]{:S(2)}) async-start(bf16[4,8,128,128]{3,2,1,0:T(8,128)(2,1)} %broadcast_select_fusion), calls=%async_computation.5 | async-start | bytes 2097152 | tf_op jit(solution)/shard_map/all_to_all | solution.py:162
  151.8 17.2 %all_gather.3 = bf16[64,2048]{1,0:T(8,128)(2,1)S(1)} all-gather(bf16[64,512]{1,0:T(8,128)(2,1)S(1)} %copy-done.2), channel_id=1, replica_groups=mesh['slab'=128,'sub'=4] {'sub'}, dimensions={1}, use_global_device_ids=true | all-gather | bytes 327680 | tf_op jit(solution)/shard_map/all_gather | solution.py:150
  169.0 7.2 %collective-permute-start.1 = (bf16[64,2048]{1,0:T(8,128)(2,1)S(1)}, bf16[64,2048]{1,0:T(8,128)(2,1)S(1)}, u32[]{:S(2)}, u32[]{:S(2)}) collective-permute-start(bf16[64,2048]{1,0:T(8,128)(2,1)S(1)} %all_gather.3), channel_id=1, source_target_pairs={{4,0},{8,4},{12,8},{16,12},{20,16},{24,20},{28,24},{32,28},{36,32}... | collective-permute-start | bytes 786440 | tf_op jit(solution)/shard_map/ppermute | solution.py:17
  176.1 1.9 %collective-permute-start = (bf16[64,2048]{1,0:T(8,128)(2,1)S(1)}, bf16[64,2048]{1,0:T(8,128)(2,1)S(1)}, u32[]{:S(2)}, u32[]{:S(2)}) collective-permute-start(bf16[64,2048]{1,0:T(8,128)(2,1)S(1)} %all_gather.3), channel_id=1, source_target_pairs={{0,4},{4,8},{8,12},{12,16},{16,20},{20,24},{24,28},{28,32},{32,36}... | collective-permute-start | bytes 786440 | tf_op jit(solution)/shard_map/ppermute | solution.py:16
  178.3 1.7 collective-permute-done.1
  180.0 1.4 collective-permute-done
  182.3 0.8 convolution_bitcast_fusion
  183.1 1.0 fusion.22
  (73 shorter events, 5.2 us)
Async XLA Ops:
  0.0 66.6 %copy-start = (bf16[2048,128]{1,0:T(8,128)(2,1)S(1)}, bf16[2048,128]{1,0:T(8,128)(2,1)}, u32[]{:S(2)}) copy-start(bf16[2048,128]{1,0:T(8,128)(2,1)} %param.12) | copy-start | bytes 1572868
  5.9 33.4 %copy-start.3 = (s32[2,3,2048]{2,0,1:T(2,128)S(1)}, s32[2,3,2048]{2,0,1:T(2,128)}, u32[]{:S(2)}) copy-start(s32[2,3,2048]{2,0,1:T(2,128)} %param.20) | copy-start | bytes 147460
  5.9 33.5 %copy-start.9 = (s32[16]{0:T(128)S(1)}, s32[16]{0:T(128)}, u32[]{:S(2)}) copy-start(s32[16]{0:T(128)} %param.21) | copy-start | bytes 196
  18.7 43.1 %all-to-all-start.1 = ((s32[128,4,4]{2,1,0:T(4,128)}), s32[128,4,4]{2,1,0:T(4,128)S(1)}, u32[]{:S(2)}, u32[]{:S(2)}) async-start(s32[128,4,4]{2,1,0:T(4,128)} %reshape.243), calls=%async_computation.1 | async-start | bytes 524288 | tf_op jit(solution)/shard_map/all_to_all | solution.py:116
  62.5 12.1 %all-to-all-start.2 = ((s32[128,4,4]{0,2,1:T(4,128)}), s32[128,4,4]{0,2,1:T(4,128)S(1)}, u32[]{:S(2)}, u32[]{:S(2)}) async-start(s32[128,4,4]{0,2,1:T(4,128)} %copy.57), calls=%async_computation.2 | async-start | bytes 16384 | tf_op jit(solution)/shard_map/all_to_all | solution.py:115
  74.6 8.9 %copy-start.1 = (s32[16]{0:T(128)S(1)}, s32[16]{0:T(128)}, u32[]{:S(2)}) copy-start(s32[16]{0:T(128)} %param.22) | copy-start | bytes 196
  74.6 10.3 %copy-start.4 = (f32[2,2,2048]{2,1,0:T(2,128)S(1)}, f32[2,2,2048]{2,1,0:T(2,128)}, u32[]{:S(2)}) copy-start(f32[2,2,2048]{2,1,0:T(2,128)} %param.18) | copy-start | bytes 98308
  74.6 40.9 %all-to-all-start.3 = ((bf16[128,4,4,128]{3,2,1,0:T(4,128)(2,1)}), bf16[128,4,4,128]{3,2,1,0:T(4,128)(2,1)S(1)}, u32[]{:S(2)}, u32[]{:S(2)}) async-start(bf16[128,4,4,128]{3,2,1,0:T(4,128)(2,1)} %bitcast.7), calls=%async_computation.3 | async-start | bytes 1048576 | tf_op jit(solution)/shard_map/all_to_all | solution.py:109
  116.5 12.3 %all-to-all-start.4 = ((bf16[128,4,4,128]{3,2,0,1:T(4,128)(2,1)}), bf16[128,4,4,128]{3,2,0,1:T(4,128)(2,1)S(1)}, u32[]{:S(2)}, u32[]{:S(2)}) async-start(bf16[128,4,4,128]{3,2,0,1:T(4,128)(2,1)} %copy.59), calls=%async_computation.4 | async-start | bytes 1048576 | tf_op jit(solution)/shard_map/all_to_all | solution.py:108
  121.0 17.2 %copy-start.6 = (bf16[128,256]{1,0:T(8,128)(2,1)S(1)}, bf16[128,256]{1,0:T(8,128)(2,1)}, u32[]{:S(2)}) copy-start(bf16[128,256]{1,0:T(8,128)(2,1)} %param.14) | copy-start | bytes 196612
  121.0 17.2 %copy-start.7 = (bf16[3,256]{1,0:T(4,128)(2,1)S(1)}, bf16[3,256]{1,0:T(4,128)(2,1)}, u32[]{:S(2)}) copy-start(bf16[3,256]{1,0:T(4,128)(2,1)} %param.16) | copy-start | bytes 4612
  121.0 17.3 %copy-start.8 = (f32[256]{0:T(256)S(1)}, f32[256]{0:T(256)}, u32[]{:S(2)}) copy-start(f32[256]{0:T(256)} %param.15) | copy-start | bytes 3076
  121.0 17.3 %copy-start.10 = (f32[3]{0:T(128)S(1)}, f32[3]{0:T(128)}, u32[]{:S(2)}) copy-start(f32[3]{0:T(128)} %param.17) | copy-start | bytes 40
  128.8 18.7 %all-to-all-start = ((s32[4,2,8]{2,1,0:T(2,128)}), s32[4,2,8]{2,1,0:T(2,128)S(1)}, u32[]{:S(2)}, u32[]{:S(2)}) async-start(s32[4,2,8]{2,1,0:T(2,128)} %copy.56), calls=%async_computation | async-start | bytes 8192 | tf_op jit(solution)/shard_map/all_to_all | solution.py:163
  138.3 1.0 copy-start.5
  147.5 4.3 %copy-start.2 = (bf16[64,512]{1,0:T(8,128)(2,1)S(1)}, bf16[64,512]{1,0:T(8,128)(2,1)}, u32[]{:S(2)}) copy-start(bf16[64,512]{1,0:T(8,128)(2,1)} %param.23) | copy-start | bytes 196612
  147.5 34.8 %all-to-all-start.5 = ((bf16[4,8,128,128]{3,2,1,0:T(8,128)(2,1)}), bf16[4,8,128,128]{3,2,1,0:T(8,128)(2,1)S(1)}, u32[]{:S(2)}, u32[]{:S(2)}) async-start(bf16[4,8,128,128]{3,2,1,0:T(8,128)(2,1)} %broadcast_select_fusion), calls=%async_computation.5 | async-start | bytes 2097152 | tf_op jit(solution)/shard_map/all_to_all | solution.py:162
  169.0 11.0 %collective-permute-start.1 = (bf16[64,2048]{1,0:T(8,128)(2,1)S(1)}, bf16[64,2048]{1,0:T(8,128)(2,1)S(1)}, u32[]{:S(2)}, u32[]{:S(2)}) collective-permute-start(bf16[64,2048]{1,0:T(8,128)(2,1)S(1)} %all_gather.3), channel_id=1, source_target_pairs={{4,0},{8,4},{12,8},{16,12},{20,16},{24,20},{28,24},{32,28},{36,32}... | collective-permute-start | bytes 786440 | tf_op jit(solution)/shard_map/ppermute | solution.py:17
  176.1 5.2 %collective-permute-start = (bf16[64,2048]{1,0:T(8,128)(2,1)S(1)}, bf16[64,2048]{1,0:T(8,128)(2,1)S(1)}, u32[]{:S(2)}, u32[]{:S(2)}) collective-permute-start(bf16[64,2048]{1,0:T(8,128)(2,1)S(1)} %all_gather.3), channel_id=1, source_target_pairs={{0,4},{4,8},{8,12},{12,16},{16,20},{20,24},{24,28},{28,32},{32,36}... | collective-permute-start | bytes 786440 | tf_op jit(solution)/shard_map/ppermute | solution.py:16
where the time goes:
time: 188 us; the launch traced here: 185 us
  waiting for transfers between devices  62.2 us (33%)
  starting transfers between devices  53.4 us (28%)
  local copies, waits for them, and re-layouts  34.9 us (19%)
  blocking collectives  17.2 us (9%)
  other arithmetic  12.2 us (6%)
  matrix products  4.61 us (2%)
    all_to_all x1, waiting for transfers between devices, local(): lax.all_to_all(outgoing, 'slab', split_axis=0, concat_axis=0, tiled=True)  29 us
    all_to_all x1, waiting for transfers between devices, local(): lax.all_to_all(dest_local, 'slab', split_axis=0, concat_axis=0, tiled=True)  22.4 us
    all_to_all x1, starting transfers between devices, local(): lax.all_to_all(dest_local, 'slab', split_axis=0, concat_axis=0, tiled=True)  20.6 us
    all_gather x1, blocking collectives, local(): grouped = lax.all_gather(probe, 'sub', axis=1, tiled=True)  17.2 us
    gather x1, local copies, waits for them, and re-layouts, local(): partition_slot[1][by_slot].reshape(slab_count, sub_count, per_peer)  11.8 us
    gather x1, local copies, waits for them, and re-layouts, local(): covariates[by_slot]  7.97 us
    all_to_all x1, waiting for transfers between devices, local(): lax.all_to_all(lax.all_to_all(outgoing, 'slab', split_axis=0, concat_axis...  7.69 us
    all_to_all x1, starting transfers between devices, local(): lax.all_to_all(outgoing, 'slab', split_axis=0, concat_axis=0, tiled=True)  7.58 us
  transfers between devices with their start and end apart: 8, of which 5 were waited for; matrix products, arithmetic and copies ran while one was open for 16% of the time, Pallas kernels for 0%

commit v1 on v0

v1 whole, which is shorter than its diff:
```python
import jax
import jax.numpy as jnp
from jax import lax
from jax.experimental import pallas as pl
from jax.experimental.pallas import tpu as pltpu
from jax.sharding import PartitionSpec as P

BLK = 128
CHUNKS = 16
RANKS = 16
FIELDS = 8
SLOTS = 32
TILES_SLAB = 64
SUBS = 4
BLK_DEV = 4
COLS = 64
PAIRS = ((0, 0), (0, 1), (0, 2), (1, 1), (1, 2), (2, 2))
PAIR_OF = {(a, b): PAIRS.index((min(a, b), max(a, b))) for a in range(3) for b in range(3)}
NT = (((1,), (1,)), ((), ()))
VMEM = pl.BlockSpec(memory_space=pltpu.VMEM)
SMEM = pl.BlockSpec(memory_space=pltpu.SMEM)
F32 = jnp.float32
BF16 = jnp.bfloat16


def call(kernel, out_shape, in_specs, out_specs, scratch, flops, nbytes):
    return pl.pallas_call(
        kernel,
        out_shape=out_shape,
        in_specs=in_specs,
        out_specs=out_specs,
        scratch_shapes=scratch,
        compiler_params=pltpu.CompilerParams(vmem_limit_bytes=40 * 1024 * 1024),
        cost_estimate=pl.CostEstimate(flops=flops, bytes_accessed=nbytes, transcendentals=0),
    )


def lanes(chunk):
    return slice(chunk * BLK, (chunk + 1) * BLK)


def pack_kernel(grad_ref, area_ref, corner_ref, rows_ref, cols_ref, out_ref):
    out_ref[0:1, :] = grad_ref[0, 0:1, :]
    out_ref[1:2, :] = grad_ref[0, 1:2, :]
    out_ref[2:3, :] = grad_ref[1, 0:1, :]
    out_ref[3:4, :] = grad_ref[1, 1:2, :]
    out_ref[4:5, :] = area_ref[...]
    for side in range(2):
        packed = (
            corner_ref[side, 0:1, :]
            + corner_ref[side, 1:2, :] * BLK
            + corner_ref[side, 2:3, :] * (BLK * BLK)
        )
        out_ref[5 + side : 6 + side, :] = packed.astype(F32)
    out_ref[7:8, :] = jnp.zeros((1, out_ref.shape[1]), F32)
    out_ref[7:8, 0:16] = rows_ref[...].astype(F32)
    out_ref[7:8, 16:32] = cols_ref[...].astype(F32)


def route_kernel(cov_ref, slot_ref, w1_ref, b1_ref, w2_ref, b2_ref, out_ref, hot_ref, val_ref, par_ref):
    rows = 256
    for part in range(cov_ref.shape[0] // rows):
        here = slice(part * rows, (part + 1) * rows)
        pre_act = (
            jnp.dot(cov_ref[here, :], w1_ref[...], preferred_element_type=F32) + b1_ref[...]
        )
        hidden = jax.nn.gelu(pre_act, approximate=True).astype(BF16)
        par_ref[:, here] = (
            lax.dot_general(w2_ref[...], hidden, NT, preferred_element_type=F32) + b2_ref[...]
        )
    slab_iota = lax.broadcasted_iota(jnp.int32, (BLK, BLK), 0)
    lane_iota = lax.broadcasted_iota(jnp.int32, (BLK, BLK), 1)
    for chunk in range(CHUNKS):
        slab = slot_ref[0:1, lanes(chunk)] >> 2
        hot_ref[:, lanes(chunk)] = jnp.where(slab_iota == slab, 1.0, 0.0).astype(BF16)
    earlier = jnp.concatenate(
        [jnp.where(slab_iota < lane_iota, 1.0, 0.0).astype(BF16), jnp.ones((BLK, BLK), BF16)], axis=1
    )
    rank_iota = lax.broadcasted_iota(jnp.int32, (RANKS, BLK), 0).astype(F32)
    seen = jnp.zeros((BLK, BLK), F32)
    for chunk in range(CHUNKS):
        hot = hot_ref[:, lanes(chunk)]
        counts = jnp.dot(hot, earlier, preferred_element_type=F32)
        rank = jnp.sum(hot.astype(F32) * (counts[:, :BLK] + seen), axis=0, keepdims=True)
        seen = seen + counts[:, BLK:]
        params = par_ref[:, lanes(chunk)]
        high = params.astype(BF16).astype(F32)
        low = params - high
        device = slot_ref[0:1, lanes(chunk)]
        place = slot_ref[1:2, lanes(chunk)]
        tile = ((device & 3) * 16 + (place >> 7)).astype(F32)
        lane = (place & 127).astype(F32)
        values = []
        for f in range(3):
            values += [high[f : f + 1], low[f : f + 1]]
        values += [tile, lane]
        mine = rank_iota == rank
        val_ref[:, lanes(chunk)] = jnp.concatenate(
            [jnp.where(mine, v, 0.0).astype(BF16) for v in values], axis=0
        )
    out_ref[...] = lax.dot_general(hot_ref[...], val_ref[...], NT, preferred_element_type=F32)


def window_kernel(meta_ref, elem_ref, before_ref, own_ref, after_ref, tid_ref, geo_ref, pos_ref, xg_ref, info_ref, raw_ref):
    me = lax.axis_index("sub")
    base = (lax.axis_index("slab") - 1) * (SUBS * BLK_DEV)
    tid_ref[...] = jnp.full(tid_ref.shape, -1.0, F32)

    def find(t, n):
        u, k = t // 16, t % 16
        row = meta_ref[u, k]
        owned = (row // BLK_DEV) % SUBS == me

        @pl.when(owned)
        def _():
            info_ref[0, n] = row % BLK_DEV
            info_ref[1, n] = meta_ref[u, 16 + k] - base
            info_ref[2, n] = t
            tid_ref[pl.ds(n, 1), :] = jnp.full((1, BLK), t, jnp.int32).astype(F32)

        return n + owned.astype(jnp.int32)

    count = lax.fori_loop(0, TILES_SLAB, find, jnp.int32(0))
    info_ref[0, SLOTS] = count
    node_iota = lax.broadcasted_iota(jnp.int32, (BLK, BLK), 0)

    def gather(n, carry):
        t, col = info_ref[2, n], info_ref[1, n]
        u, k = t // 16, t % 16
        rows = elem_ref[u, :, pl.ds(pl.multiple_of(k * BLK, BLK), BLK)]
        for f in range(7):
            raw_ref[f, pl.ds(n, 1), :] = rows[f : f + 1]
        packed = rows[6:7].astype(jnp.int32)
        hot = jnp.concatenate(
            [
                jnp.where(node_iota == ((packed >> (7 * b)) & 127), 1.0, 0.0).astype(BF16)
                for b in range(3)
            ],
            axis=1,
        )
        step, s, blk = col // 16, (col // 4) % 4, col % 4
        where = pl.ds(pl.multiple_of(blk * BLK, BLK), BLK)

        def store(ref):
            def _():
                xg_ref[n] = jnp.dot(ref[s, :, where], hot, preferred_element_type=F32).astype(BF16)

            return _

        pl.when(step == 0)(store(before_ref))
        pl.when(step == 1)(store(own_ref))
        pl.when(step == 2)(store(after_ref))
        return carry

    lax.fori_loop(0, count, gather, jnp.int32(0))
    grad_x = [raw_ref[0], raw_ref[1]]
    grad_x.append(-(grad_x[0] + grad_x[1]))
    grad_y = [raw_ref[2], raw_ref[3]]
    grad_y.append(-(grad_y[0] + grad_y[1]))
    for i, (a, b) in enumerate(PAIRS):
        geo_ref[i] = grad_x[a] * grad_x[b] + grad_y[a] * grad_y[b]
        geo_ref[6 + i] = grad_x[a] * grad_y[b] + grad_y[a] * grad_x[b]
    geo_ref[12] = raw_ref[4]
    row_packed = raw_ref[5].astype(jnp.int32)
    for a in range(3):
        pos_ref[a] = (row_packed >> (7 * a)) & 127


def apply_kernel(info_ref, got_ref, tid_ref, geo_ref, pos_ref, xg_ref, out_ref, hot_ref, val_ref, k_ref, turned_ref):
    lane_iota = lax.broadcasted_iota(jnp.int32, (BLK, BLK), 0).astype(F32)
    tiles = tid_ref[...]
    found = jnp.zeros((6 * SLOTS, BLK), F32)
    for u in range(SUBS):
        turned_ref[...] = got_ref[u].T
        for k in range(RANKS):
            rows = [turned_ref[f * RANKS + k : f * RANKS + k + 1, :] for f in range(FIELDS)]
            mine = tiles == rows[6]
            val_ref[:, lanes(k)] = jnp.concatenate(
                [jnp.where(mine, rows[f], 0.0).astype(BF16) for f in range(6)], axis=0
            )
            hot_ref[:, lanes(k)] = jnp.where(lane_iota == rows[7], 1.0, 0.0).astype(BF16)
        found = found + lax.dot_general(val_ref[...], hot_ref[...], NT, preferred_element_type=F32)
    params = [
        found[2 * f * SLOTS : (2 * f + 1) * SLOTS] + found[(2 * f + 1) * SLOTS : (2 * f + 2) * SLOTS]
        for f in range(3)
    ]
    kappa_sq = jnp.exp(params[0])
    scale = jnp.exp(params[1])
    coupling = 0.9 * jnp.tanh(params[2])
    area = geo_ref[12]
    for i, (a, b) in enumerate(PAIRS):
        mass = kappa_sq * (2.0 if a == b else 1.0)
        stiffness = scale * (geo_ref[i] + coupling * geo_ref[6 + i])
        k_ref[i] = (area * (stiffness + mass)).astype(BF16).astype(F32)
    out_ref[...] = jnp.zeros(out_ref.shape, F32)
    node_iota = lax.broadcasted_iota(jnp.int32, (BLK, BLK), 0)

    def add(n, carry):
        k = [k_ref[i, pl.ds(n, 1), :] for i in range(6)]
        x = xg_ref[n].astype(F32)
        xs = [x[:, lanes(b)] for b in range(3)]
        ys = []
        hots = []
        for a in range(3):
            y = k[PAIR_OF[a, 0]] * xs[0] + k[PAIR_OF[a, 1]] * xs[1] + k[PAIR_OF[a, 2]] * xs[2]
            ys.append(y.astype(BF16))
            hots.append(jnp.where(node_iota == pos_ref[a, pl.ds(n, 1), :], 1.0, 0.0).astype(BF16))
        part = lax.dot_general(
            jnp.concatenate(ys, axis=1), jnp.concatenate(hots, axis=1), NT, preferred_element_type=F32
        )
        where = pl.ds(pl.multiple_of(info_ref[0, n] * BLK, BLK), BLK)
        out_ref[:, where] = out_ref[:, where] + part
        return carry

    lax.fori_loop(0, info_ref[0, SLOTS], add, jnp.int32(0))


def shared(block):
    copies = jnp.broadcast_to(block[None], (SUBS, *block.shape))
    return lax.all_to_all(copies, "sub", split_axis=0, concat_axis=0, tiled=True)


def local(
    covariates,
    partition_slot,
    in_weight,
    in_bias,
    out_weight,
    out_bias,
    gradients,
    areas,
    corners,
    tile_rows,
    tile_cols,
    probe,
):
    elements = areas.shape[0]
    slabs = lax.axis_size("slab")
    sds = jax.ShapeDtypeStruct
    packed = call(
        pack_kernel, sds((8, elements), F32), [VMEM] * 5, VMEM, (), 10000, 200000
    )(gradients, areas[None], corners, tile_rows[None], tile_cols[None])
    routed = call(
        route_kernel,
        sds((BLK, BLK), F32),
        [VMEM] * 6,
        VMEM,
        [pltpu.VMEM((BLK, elements), BF16), pltpu.VMEM((BLK, elements), BF16), pltpu.VMEM((3, elements), F32)],
        400_000_000,
        1_000_000,
    )(covariates, partition_slot, in_weight, in_bias[None], out_weight, out_bias[:, None])
    arrived = lax.all_to_all(routed, "slab", split_axis=0, concat_axis=0, tiled=True)

    elem = shared(packed)
    own = shared(probe)
    up = [(i, i + 1) for i in range(slabs - 1)]
    before = lax.ppermute(own, "slab", up)
    after = lax.ppermute(own, "slab", [(j, i) for i, j in up])
    meta = elem[:, 7, :32].astype(jnp.int32)
    tid, geo, pos, xg, info = call(
        window_kernel,
        (
            sds((SLOTS, BLK), F32),
            sds((13, SLOTS, BLK), F32),
            sds((3, SLOTS, BLK), jnp.int32),
            sds((SLOTS, COLS, 3 * BLK), BF16),
            sds((3, SLOTS + 1), jnp.int32),
        ),
        [SMEM, VMEM, VMEM, VMEM, VMEM],
        (VMEM, VMEM, VMEM, VMEM, SMEM),
        [pltpu.VMEM((7, SLOTS, BLK), F32)],
        400_000_000,
        3_000_000,
    )(meta, elem, before, own, after)
    got = shared(arrived.astype(BF16)).astype(F32)
    return call(
        apply_kernel,
        sds((COLS, probe.shape[1]), F32),
        [SMEM] + [VMEM] * 5,
        VMEM,
        [
            pltpu.VMEM((BLK, RANKS * BLK), BF16),
            pltpu.VMEM((6 * SLOTS, RANKS * BLK), BF16),
            pltpu.VMEM((6, SLOTS, BLK), F32),
            pltpu.VMEM((BLK, BLK), F32),
        ],
        1_000_000_000,
        3_000_000,
    )(info, got, tid, geo, pos, xg)


def solution(mesh):
    placed = (
        P(("slab", "sub"), None),
        P(None, ("slab", "sub")),
        P(),
        P(),
        P(),
        P(),
        P(None, None, ("slab", "sub")),
        P(("slab", "sub")),
        P(None, None, ("slab", "sub")),
        P(("slab", "sub")),
        P(("slab", "sub")),
        P(None, ("slab", "sub")),
    )
    return jax.shard_map(
        local, mesh=mesh, in_specs=placed, out_specs=P(None, ("slab", "sub")), check_vma=False
    )
```

time: 188 us -> 86.9 us (0.46)
  the two profiles are of different devices: /device:TPU:1 before, /device:TPU:64 now
where the time goes in v1:
time: 86.9 us; the launch traced here: 86.2 us
  starting transfers between devices  36.7 us (42%)
  waiting for transfers between devices  20.9 us (24%)
  Pallas kernels  20.7 us (24%)
  local copies, waits for them, and re-layouts  7.76 us (9%)
    all_to_all x1, starting transfers between devices, local(): lax.all_to_all(routed, 'slab', split_axis=0, concat_axis=0, tiled=True)  18.7 us
    all_to_all x3, waiting for transfers between devices, shared(): lax.all_to_all(copies, 'sub', split_axis=0, concat_axis=0, tiled=True)  12.7 us
    all_to_all x3, starting transfers between devices, shared(): lax.all_to_all(copies, 'sub', split_axis=0, concat_axis=0, tiled=True)  12.4 us
    pallas_call x1, Pallas kernels, local(): call(window_kernel, (sds((SLOTS, BLK), F32), sds((13, SLOTS, BLK), F32),...  9.32 us
    pallas_call x1, Pallas kernels, local(): call(apply_kernel, sds((COLS, probe.shape[1]), F32), [SMEM] + [VMEM] * 5,...  8.67 us
    all_to_all x1, waiting for transfers between devices, local(): lax.all_to_all(routed, 'slab', split_axis=0, concat_axis=0, tiled=True)  8.15 us
    unnamed x21, local copies, waits for them, and re-layouts  4.01 us
    ppermute x1, starting transfers between devices, local(): after = lax.ppermute(own, 'slab', [(j, i) for i, j in up])  3.51 us
  transfers between devices with their start and end apart: 6, of which 3 were waited for; matrix products, arithmetic and copies ran while one was open for 3% of the time, Pallas kernels for 3%

profile of v1, /device:TPU:64, one launch (start us, length us, event | category | flops | bytes accessed | tf_op | source)
XLA Modules:
  0.0 86.2 jit_solution(4670328499619768177)
XLA Ops:
  0.0 0.0 copy-start.3
  0.0 0.0 copy-start
  0.0 1.6 %broadcast_in_dim.37 = bf16[4,64,512]{2,1,0:T(8,128)(2,1)} broadcast(bf16[64,512]{1,0:T(8,128)(2,1)} %param.23), dimensions={1,2} | broadcast | bytes 327680 | tf_op jit(solution)/shard_map/broadcast_in_dim | solution.py:219
  1.6 4.3 %all-to-all-start.1 = ((bf16[4,64,512]{2,1,0:T(8,128)(2,1)}), bf16[4,64,512]{2,1,0:T(8,128)(2,1)S(1)}, u32[]{:S(2)}, u32[]{:S(2)}) async-start(bf16[4,64,512]{2,1,0:T(8,128)(2,1)} %broadcast_in_dim.37), calls=%async_computation.1 | async-start | bytes 524288 | tf_op jit(solution)/shard_map/all_to_all | solution.py:220
  5.9 0.7 copy.19.b2_ref
  6.7 1.0 %copy-done.4 = bf16[2048,128]{1,0:T(8,128)(2,1)S(1)} copy-done((bf16[2048,128]{1,0:T(8,128)(2,1)S(1)}, bf16[2048,128]{1,0:T(8,128)(2,1)}, u32[]{:S(2)}) %copy-start.4) | copy-done | bytes 524312
  7.7 0.8 copy-done.5
  8.6 0.7 copy-done.6
  9.3 0.7 copy-done.7
  10.0 0.7 copy-done.8
  10.6 2.6 %shard_map.120 = f32[128,128]{1,0:T(8,128)} custom-call(bf16[2048,128]{1,0:T(8,128)(2,1)S(1)} %copy-done.4, s32[2,2048]{1,0:T(2,128)S(1)} %copy-done.6, bf16[128,256]{1,0:T(8,128)(2,1)S(1)} %copy-done.5, f32[1,256]{1,0:T(1,128)S(1)} %bitcast.16, bf16[3,256]{1,0:T(4,128)(2,1)S(1)} %copy-done.7, f32[3,1]{1,0:T(4,128)S(1)} %copy.19.b2_ref), custom_call_target="tpu_custom_call" | custom-call | flops 400000000 | bytes 1000000 | tf_op jit(solution)/shard_map/pallas_call | solution.py:243
  13.3 0.0 all-to-all-done.1.own_ref
  13.3 18.7 %all-to-all-start.2 = ((f32[128,1,128]{2,1,0:T(1,128)}), f32[128,1,128]{2,1,0:T(1,128)S(1)}, u32[]{:S(2)}, u32[]{:S(2)}) async-start(f32[128,1,128]{2,1,0:T(1,128)} %bitcast.7), calls=%async_computation.2 | async-start | bytes 131072 | tf_op jit(solution)/shard_map/all_to_all | solution.py:252
  32.0 0.0 copy-done.9
  32.0 0.0 copy-done.1
  32.1 0.0 copy-done.2
  32.1 0.0 copy-done.3
  32.1 0.0 copy-done
  32.1 0.1 shard_map.118
  32.2 2.0 %collective-permute-start = (bf16[4,64,512]{2,1,0:T(8,128)(2,1)S(1)}, bf16[4,64,512]{2,1,0:T(8,128)(2,1)S(1)}, u32[]{:S(2)}, u32[]{:S(2)}) collective-permute-start(bf16[4,64,512]{2,1,0:T(8,128)(2,1)S(1)} %all-to-all-done.1.own_ref), channel_id=1, source_target_pairs={{0,4},{4,8},{8,12},{12,16},{16,20},{20,24},{24,28},{28,32},{32,36}... | collective-permute-start | bytes 786440 | tf_op jit(solution)/shard_map/ppermute | solution.py:257
  34.2 3.5 %collective-permute-start.1 = (bf16[4,64,512]{2,1,0:T(8,128)(2,1)S(1)}, bf16[4,64,512]{2,1,0:T(8,128)(2,1)S(1)}, u32[]{:S(2)}, u32[]{:S(2)}) collective-permute-start(bf16[4,64,512]{2,1,0:T(8,128)(2,1)S(1)} %all-to-all-done.1.own_ref), channel_id=1, source_target_pairs={{4,0},{8,4},{12,8},{16,12},{20,16},{24,20},{28,24},{32,28},{36,32}... | collective-permute-start | bytes 786440 | tf_op jit(solution)/shard_map/ppermute | solution.py:258
  37.7 8.2 %all-to-all-done.2 = f32[128,1,128]{2,1,0:T(1,128)S(1)} async-done(((f32[128,1,128]{2,1,0:T(1,128)}), f32[128,1,128]{2,1,0:T(1,128)S(1)}, u32[]{:S(2)}, u32[]{:S(2)}) %all-to-all-start.2) | async-done | bytes 65568 | tf_op jit(solution)/shard_map/all_to_all | solution.py:252
  45.9 0.7 broadcast_in_dim.36
  46.6 4.8 %all-to-all-start = ((f32[4,8,2048]{2,1,0:T(8,128)}), f32[4,8,2048]{2,1,0:T(8,128)S(1)}, u32[]{:S(2)}, u32[]{:S(2)}) async-start(f32[4,8,2048]{2,1,0:T(8,128)} %broadcast_in_dim.36), calls=%async_computation | async-start | bytes 524288 | tf_op jit(solution)/shard_map/all_to_all | solution.py:220
  51.4 6.8 %all-to-all-done.elem_ref = f32[4,8,2048]{2,1,0:T(8,128)S(1)} async-done(((f32[4,8,2048]{2,1,0:T(8,128)}), f32[4,8,2048]{2,1,0:T(8,128)S(1)}, u32[]{:S(2)}, u32[]{:S(2)}) %all-to-all-start) | async-done | bytes 262176 | tf_op jit(solution)/shard_map/all_to_all | solution.py:220
  58.2 0.7 broadcast_in_dim.40
  58.9 3.3 %all-to-all-start.3 = ((bf16[4,128,128]{2,1,0:T(8,128)(2,1)}), bf16[4,128,128]{2,1,0:T(8,128)(2,1)S(1)}, u32[]{:S(2)}, u32[]{:S(2)}) async-start(bf16[4,128,128]{2,1,0:T(8,128)(2,1)} %broadcast_in_dim.40), calls=%async_computation.3 | async-start | bytes 262144 | tf_op jit(solution)/shard_map/all_to_all | solution.py:220
  62.2 5.9 %all-to-all-done.3 = bf16[4,128,128]{2,1,0:T(8,128)(2,1)S(1)} async-done(((bf16[4,128,128]{2,1,0:T(8,128)(2,1)}), bf16[4,128,128]{2,1,0:T(8,128)(2,1)S(1)}, u32[]{:S(2)}, u32[]{:S(2)}) %all-to-all-start.3) | async-done | bytes 131104 | tf_op jit(solution)/shard_map/all_to_all | solution.py:220
  68.1 0.0 collective-permute-done.before_ref
  68.2 0.0 collective-permute-done.1.after_ref
  68.2 9.3 %shard_map.119 = (f32[32,128]{1,0:T(8,128)S(1)}, f32[13,32,128]{2,1,0:T(8,128)S(1)}, s32[3,32,128]{2,1,0:T(8,128)S(1)}, bf16[32,64,384]{2,1,0:T(8,128)(2,1)S(1)}, s32[3,33]{1,0:T(4,128)S(1)}) custom-call(s32[4,32]{1,0:T(4,128)S(1)} %bitcast.13, f32[4,8,2048]{2,1,0:T(8,128)S(1)} %all-to-all-done.elem_ref, ...), custom_call_target="tpu_custom_call" | custom-call | flops 400000000 | bytes 3000000 | tf_op jit(solution)/shard_map/pallas_call | solution.py:260
  77.5 8.7 %shard_map.121 = f32[64,512]{1,0:T(8,128)} custom-call(s32[3,33]{1,0:T(4,128)S(1)} %get-tuple-element.10.info_ref, f32[4,128,128]{2,1,0:T(8,128)S(1)} %convert_element_type.22.got_ref, f32[32,128]{1,0:T(8,128)S(1)} %get-tuple-element.11.tid_ref, f32[13,32,128]{2,1,0:T(8,128)S(1)} %get-tuple-element.12.geo_ref, s32[3,32,128]{2,1,0:T(8,128)S(1)} %get-tuple-element.13.pos_ref, ...), custom_call_target="tpu_custom_call" | custom-call | flops 1000000000 | bytes 3000000 | tf_op jit(solution)/shard_map/pallas_call | solution.py:276
  (12 shorter events, 0.1 us)
Async XLA Ops:
  0.0 32.0 %copy-start.9 = (s32[2,3,2048]{2,0,1:T(2,128)S(1)}, s32[2,3,2048]{2,0,1:T(2,128)}, u32[]{:S(2)}) copy-start(s32[2,3,2048]{2,0,1:T(2,128)} %param.20) | copy-start | bytes 147460
  0.0 32.0 %copy-start.1 = (f32[2048]{0:T(1024)S(1)}, f32[2048]{0:T(1024)}, u32[]{:S(2)}) copy-start(f32[2048]{0:T(1024)} %param.19) | copy-start | bytes 24580
  0.0 32.1 %copy-start.2 = (s32[16]{0:T(128)S(1)}, s32[16]{0:T(128)}, u32[]{:S(2)}) copy-start(s32[16]{0:T(128)} %param.21) | copy-start | bytes 196
  0.0 32.1 %copy-start.3 = (s32[16]{0:T(128)S(1)}, s32[16]{0:T(128)}, u32[]{:S(2)}) copy-start(s32[16]{0:T(128)} %param.22) | copy-start | bytes 196
  0.0 32.1 %copy-start = (f32[2,2,2048]{2,1,0:T(2,128)S(1)}, f32[2,2,2048]{2,1,0:T(2,128)}, u32[]{:S(2)}) copy-start(f32[2,2,2048]{2,1,0:T(2,128)} %grad_ref.1) | copy-start | bytes 98308
  1.6 11.6 %all-to-all-start.1 = ((bf16[4,64,512]{2,1,0:T(8,128)(2,1)}), bf16[4,64,512]{2,1,0:T(8,128)(2,1)S(1)}, u32[]{:S(2)}, u32[]{:S(2)}) async-start(bf16[4,64,512]{2,1,0:T(8,128)(2,1)} %broadcast_in_dim.37), calls=%async_computation.1 | async-start | bytes 524288 | tf_op jit(solution)/shard_map/all_to_all | solution.py:220
  6.7 1.0 %copy-start.4 = (bf16[2048,128]{1,0:T(8,128)(2,1)S(1)}, bf16[2048,128]{1,0:T(8,128)(2,1)}, u32[]{:S(2)}) copy-start(bf16[2048,128]{1,0:T(8,128)(2,1)} %cov_ref.1) | copy-start | bytes 1572868
  7.7 0.8 copy-start.5
  8.6 0.7 copy-start.6
  9.3 0.7 copy-start.7
  10.0 0.7 copy-start.8
  13.3 32.6 %all-to-all-start.2 = ((f32[128,1,128]{2,1,0:T(1,128)}), f32[128,1,128]{2,1,0:T(1,128)S(1)}, u32[]{:S(2)}, u32[]{:S(2)}) async-start(f32[128,1,128]{2,1,0:T(1,128)} %bitcast.7), calls=%async_computation.2 | async-start | bytes 131072 | tf_op jit(solution)/shard_map/all_to_all | solution.py:252
  32.2 36.0 %collective-permute-start = (bf16[4,64,512]{2,1,0:T(8,128)(2,1)S(1)}, bf16[4,64,512]{2,1,0:T(8,128)(2,1)S(1)}, u32[]{:S(2)}, u32[]{:S(2)}) collective-permute-start(bf16[4,64,512]{2,1,0:T(8,128)(2,1)S(1)} %all-to-all-done.1.own_ref), channel_id=1, source_target_pairs={{0,4},{4,8},{8,12},{12,16},{16,20},{20,24},{24,28},{28,32},{32,36}... | collective-permute-start | bytes 786440 | tf_op jit(solution)/shard_map/ppermute | solution.py:257
  34.2 33.9 %collective-permute-start.1 = (bf16[4,64,512]{2,1,0:T(8,128)(2,1)S(1)}, bf16[4,64,512]{2,1,0:T(8,128)(2,1)S(1)}, u32[]{:S(2)}, u32[]{:S(2)}) collective-permute-start(bf16[4,64,512]{2,1,0:T(8,128)(2,1)S(1)} %all-to-all-done.1.own_ref), channel_id=1, source_target_pairs={{4,0},{8,4},{12,8},{16,12},{20,16},{24,20},{28,24},{32,28},{36,32}... | collective-permute-start | bytes 786440 | tf_op jit(solution)/shard_map/ppermute | solution.py:258
  46.6 11.6 %all-to-all-start = ((f32[4,8,2048]{2,1,0:T(8,128)}), f32[4,8,2048]{2,1,0:T(8,128)S(1)}, u32[]{:S(2)}, u32[]{:S(2)}) async-start(f32[4,8,2048]{2,1,0:T(8,128)} %broadcast_in_dim.36), calls=%async_computation | async-start | bytes 524288 | tf_op jit(solution)/shard_map/all_to_all | solution.py:220
  58.9 9.3 %all-to-all-start.3 = ((bf16[4,128,128]{2,1,0:T(8,128)(2,1)}), bf16[4,128,128]{2,1,0:T(8,128)(2,1)S(1)}, u32[]{:S(2)}, u32[]{:S(2)}) async-start(bf16[4,128,128]{2,1,0:T(8,128)(2,1)} %broadcast_in_dim.40), calls=%async_computation.3 | async-start | bytes 262144 | tf_op jit(solution)/shard_map/all_to_all | solution.py:220

commit v2 on v1

v2 whole, which is shorter than its diff:
```python
import jax
import jax.numpy as jnp
from jax import lax
from jax.experimental import pallas as pl
from jax.experimental.pallas import tpu as pltpu
from jax.sharding import PartitionSpec as P

BLK = 128
CHUNKS = 16
RANKS = 16
FIELDS = 8
SLOTS = 32
TILES_SLAB = 64
TILE_DEV = 16
SUBS = 4
BLK_DEV = 4
COLS = 64
PAIRS = ((0, 0), (0, 1), (0, 2), (1, 1), (1, 2), (2, 2))
PAIR_OF = {(a, b): PAIRS.index((min(a, b), max(a, b))) for a in range(3) for b in range(3)}
NT = (((1,), (1,)), ((), ()))
VMEM = pl.BlockSpec(memory_space=pltpu.VMEM)
SMEM = pl.BlockSpec(memory_space=pltpu.SMEM)
F32 = jnp.float32
BF16 = jnp.bfloat16


HBM = pl.BlockSpec(memory_space=pltpu.HBM)
ANY = pl.BlockSpec(memory_space=pl.ANY)
ELEM_FIELDS = 32
SEND_ROWS = 256


def call(kernel, out_shape, in_specs, out_specs, scratch, flops, nbytes, vmem=40):
    return pl.pallas_call(
        kernel,
        out_shape=out_shape,
        in_specs=in_specs,
        out_specs=out_specs,
        scratch_shapes=scratch,
        compiler_params=pltpu.CompilerParams(vmem_limit_bytes=vmem * 1024 * 1024),
        cost_estimate=pl.CostEstimate(flops=flops, bytes_accessed=nbytes, transcendentals=0),
    )


def lanes(chunk):
    return slice(chunk * BLK, (chunk + 1) * BLK)


def parts(x, n):
    out = []
    for _ in range(n - 1):
        out.append(x.astype(BF16).astype(F32))
        x = x - out[-1]
    return out + [x]


def pack_elements(grad_ref, area_ref, corner_ref, rows_ref, cols_ref, send_ref, meta_ref):
    meta_ref[...] = jnp.zeros(meta_ref.shape, F32)
    for i, ref in enumerate((rows_ref, cols_ref)):
        meta_ref[2 * i : 2 * i + 1, 0:TILE_DEV] = (ref[...] >> 4).astype(F32)
        meta_ref[2 * i + 1 : 2 * i + 2, 0:TILE_DEV] = (ref[...] & 15).astype(F32)
    for q in range(4):
        here = slice(q * 512, (q + 1) * 512)
        fields = []
        for i in range(2):
            for j in range(2):
                fields += parts(grad_ref[i, j : j + 1, here], 3)
        fields += parts(area_ref[:, here], 3)
        for side in range(2):
            for a in range(3):
                fields.append(corner_ref[a, side : side + 1, here].astype(F32))
        fields += [meta_ref[...], jnp.zeros((ELEM_FIELDS - 29, 512), F32)]
        top = COLS + q * ELEM_FIELDS
        send_ref[top : top + ELEM_FIELDS, :] = jnp.concatenate(fields, axis=0).astype(BF16)


def route_kernel(
    cov_hbm, slot_hbm, w1_hbm, b1_hbm, w2_hbm, b2_ref, grad_hbm, area_hbm, corner_hbm, probe_hbm, rows_ref, cols_ref,
    out_ref, send_ref,
    cov_ref, slot_ref, w1_ref, b1_ref, w2_ref, grad_ref, area_ref, corner_ref, hot_ref, count_ref, val_ref, par_ref, meta_ref, sem,
):
    pairs = (
        (slot_hbm, slot_ref), (cov_hbm, cov_ref), (w1_hbm, w1_ref), (b1_hbm, b1_ref), (w2_hbm, w2_ref),
        (grad_hbm, grad_ref), (area_hbm, area_ref), (corner_hbm, corner_ref),
        (probe_hbm, send_ref.at[0:COLS]),
    )
    copies = [pltpu.make_async_copy(s, d, sem.at[i]) for i, (s, d) in enumerate(pairs)]
    for c in copies:
        c.start()
    slab_iota = lax.broadcasted_iota(jnp.int32, (BLK, BLK), 0)
    lane_iota = lax.broadcasted_iota(jnp.int32, (BLK, BLK), 1)
    earlier = jnp.concatenate(
        [jnp.where(slab_iota < lane_iota, 1.0, 0.0).astype(BF16), jnp.ones((BLK, BLK), BF16)], axis=1
    )
    copies[0].wait()
    for chunk in range(CHUNKS):
        slab = slot_ref[0:1, lanes(chunk)] >> 2
        hot_ref[:, lanes(chunk)] = jnp.where(slab_iota == slab, 1.0, 0.0).astype(BF16)
    rank_iota = lax.broadcasted_iota(jnp.int32, (RANKS, BLK), 0).astype(F32)
    seen = jnp.zeros((BLK, BLK), F32)
    for chunk in range(CHUNKS):
        hot = hot_ref[:, lanes(chunk)]
        counts = jnp.dot(hot, earlier, preferred_element_type=F32)
        rank = jnp.sum(hot.astype(F32) * (counts[:, :BLK] + seen), axis=0, keepdims=True)
        seen = seen + counts[:, BLK:]
        count_ref[:, lanes(chunk)] = rank
    for c in copies[1:5]:
        c.wait()
    rows = 256
    for part in range(cov_ref.shape[0] // rows):
        here = slice(part * rows, (part + 1) * rows)
        pre_act = jnp.dot(cov_ref[here, :], w1_ref[...], preferred_element_type=F32) + b1_ref[...]
        hidden = jax.nn.gelu(pre_act, approximate=True).astype(BF16)
        par_ref[:, here] = lax.dot_general(w2_ref[...], hidden, NT, preferred_element_type=F32)
    for chunk in range(CHUNKS):
        device = slot_ref[0:1, lanes(chunk)]
        place = slot_ref[1:2, lanes(chunk)]
        tile = ((device & 3) * 16 + (place >> 7)).astype(F32)
        lane = (place & 127).astype(F32)
        values = []
        for f in range(3):
            values += parts(par_ref[f : f + 1, lanes(chunk)] + b2_ref[f], 2)
        values += [tile, lane]
        mine = rank_iota == count_ref[:, lanes(chunk)]
        val_ref[:, lanes(chunk)] = jnp.concatenate(
            [jnp.where(mine, v, 0.0).astype(BF16) for v in values], axis=0
        )
    out_ref[...] = lax.dot_general(hot_ref[...], val_ref[...], NT, preferred_element_type=F32).astype(out_ref.dtype)
    for c in copies[5:]:
        c.wait()
    send_ref[COLS + 4 * ELEM_FIELDS :, :] = jnp.zeros((SEND_ROWS - COLS - 4 * ELEM_FIELDS, 512), BF16)
    pack_elements(grad_ref, area_ref, corner_ref, rows_ref, cols_ref, send_ref, meta_ref)


def list_kernel(all_ref, tid_ref, geo_ref, pos_ref, info_ref, raw_ref, ints_ref, meta_ref, sem):
    me = lax.axis_index("sub")
    base = (lax.axis_index("slab") - 1) * (SUBS * BLK_DEV)
    for u in range(SUBS):
        coded = all_ref[u, COLS : COLS + ELEM_FIELDS, 0:BLK].astype(F32)
        for i in range(2):
            whole = coded[21 + 2 * i : 22 + 2 * i] * 16.0 + coded[22 + 2 * i : 23 + 2 * i]
            ints_ref[4 * i + u : 4 * i + u + 1, :] = whole.astype(jnp.int32)
    copy = pltpu.make_async_copy(ints_ref, meta_ref, sem.at[0])
    copy.start()
    tid_ref[...] = jnp.full(tid_ref.shape, -1.0, F32)
    raw_ref[...] = jnp.zeros(raw_ref.shape, F32)
    for n in range(SLOTS):
        info_ref[0, n] = 0
        info_ref[1, n] = SUBS * BLK_DEV

    copy.wait()

    def find(t, n):
        u, k = t // 16, t % 16
        row = meta_ref[u, k]
        owned = (row // BLK_DEV) % SUBS == me

        @pl.when(owned)
        def _():
            info_ref[0, n] = row % BLK_DEV
            info_ref[1, n] = meta_ref[4 + u, k] - base
            tid_ref[pl.ds(n, 1), :] = jnp.full((1, BLK), t, jnp.int32).astype(F32)
            top = pl.ds(pl.multiple_of(COLS + (k // 4) * ELEM_FIELDS, 32), ELEM_FIELDS)
            here = pl.ds(pl.multiple_of((k % 4) * BLK, BLK), BLK)
            rows = all_ref[u, top, here].astype(F32)
            for f in range(5):
                raw_ref[f, pl.ds(n, 1), :] = rows[3 * f : 3 * f + 1] + rows[3 * f + 1 : 3 * f + 2] + rows[3 * f + 2 : 3 * f + 3]
            for f in range(6):
                raw_ref[5 + f, pl.ds(n, 1), :] = rows[15 + f : 16 + f]

        return n + owned.astype(jnp.int32)

    info_ref[0, SLOTS] = lax.fori_loop(0, TILES_SLAB, find, jnp.int32(0))
    grad_x = [raw_ref[0], raw_ref[1]]
    grad_x.append(-(grad_x[0] + grad_x[1]))
    grad_y = [raw_ref[2], raw_ref[3]]
    grad_y.append(-(grad_y[0] + grad_y[1]))
    for i, (a, b) in enumerate(PAIRS):
        geo_ref[i] = grad_x[a] * grad_x[b] + grad_y[a] * grad_y[b]
        geo_ref[6 + i] = grad_x[a] * grad_y[b] + grad_y[a] * grad_x[b]
    geo_ref[12] = raw_ref[4]
    for a in range(6):
        pos_ref[a] = raw_ref[5 + a].astype(jnp.int32)


def apply_kernel(
    info_ref, got_ref, tid_ref, geo_ref, pos_ref, before_hbm, own_hbm, after_hbm,
    out_ref, hot_ref, val_ref, k_ref, turned_ref, x_ref, acc_ref, sem,
):
    copies = [
        pltpu.make_async_copy(src, x_ref.at[4 * i : 4 * i + 4], sem.at[i])
        for i, src in enumerate((before_hbm, own_hbm, after_hbm))
    ]
    for c in copies:
        c.start()
    lane_iota = lax.broadcasted_iota(jnp.int32, (BLK, BLK), 0).astype(F32).astype(BF16)
    one, zero = jnp.ones((), BF16), jnp.zeros((), BF16)
    tiles = tid_ref[...].astype(BF16)
    found = jnp.zeros((6 * SLOTS, BLK), F32)
    for u in range(SUBS):
        turned_ref[...] = got_ref[u].astype(F32).T
        for k in range(RANKS):
            rows = [
                jnp.broadcast_to(turned_ref[f * RANKS + k : f * RANKS + k + 1, :], (16, BLK)).astype(BF16)
                for f in range(FIELDS)
            ]
            twice = [jnp.concatenate([r, r], axis=0) for r in rows[:7]]
            mine = tiles == twice[6]
            val_ref[:, lanes(k)] = jnp.concatenate([jnp.where(mine, twice[f], zero) for f in range(6)], axis=0)
            hot_ref[:, lanes(k)] = jnp.where(lane_iota == jnp.concatenate([rows[7]] * 8, axis=0), one, zero)
        found = found + lax.dot_general(val_ref[...], hot_ref[...], NT, preferred_element_type=F32)
    params = [
        found[2 * f * SLOTS : (2 * f + 1) * SLOTS] + found[(2 * f + 1) * SLOTS : (2 * f + 2) * SLOTS]
        for f in range(3)
    ]
    kappa_sq = jnp.exp(params[0])
    scale = jnp.exp(params[1])
    coupling = 0.9 * jnp.tanh(params[2])
    area = geo_ref[12]
    for i, (a, b) in enumerate(PAIRS):
        mass = kappa_sq * (2.0 if a == b else 1.0)
        stiffness = scale * (geo_ref[i] + coupling * geo_ref[6 + i])
        k_ref[i] = (area * (stiffness + mass)).astype(BF16).astype(F32)
    acc_ref[...] = jnp.zeros(acc_ref.shape, F32)
    for c in copies:
        c.wait()

    def tile_part(n):
        col = info_ref[1, n]
        where = pl.ds(pl.multiple_of((col % 4) * BLK, BLK), BLK)
        x = x_ref[col // 4, :, where].astype(F32)
        k = [k_ref[i, pl.ds(n, 1), :] for i in range(6)]
        xs = [
            jnp.take_along_axis(x, jnp.broadcast_to(pos_ref[3 + b, pl.ds(n, 1), :], (COLS, BLK)), axis=1)
            for b in range(3)
        ]
        ys = []
        hots = []
        for a in range(3):
            y = k[PAIR_OF[a, 0]] * xs[0] + k[PAIR_OF[a, 1]] * xs[1] + k[PAIR_OF[a, 2]] * xs[2]
            ys.append(y.astype(BF16))
            row = jnp.broadcast_to(pos_ref[a, pl.ds(n, 1), :].astype(F32), (16, BLK)).astype(BF16)
            hots.append(jnp.where(lane_iota == jnp.concatenate([row] * 8, axis=0), one, zero))
        return lax.dot_general(
            jnp.concatenate(ys, axis=1), jnp.concatenate(hots, axis=1), NT, preferred_element_type=F32
        )

    def add(group, carry):
        done = [tile_part(group * UNROLL + i) for i in range(UNROLL)]
        for i in range(UNROLL):
            block = info_ref[0, group * UNROLL + i]
            acc_ref[block] = acc_ref[block] + done[i]
        return carry

    lax.fori_loop(0, (info_ref[0, SLOTS] + UNROLL - 1) // UNROLL, add, jnp.int32(0))
    for block in range(BLK_DEV):
        out_ref[:, lanes(block)] = acc_ref[block]


UNROLL = 4


def shared(block):
    copies = jnp.broadcast_to(block[None], (SUBS, *block.shape))
    return lax.all_to_all(copies, "sub", split_axis=0, concat_axis=0, tiled=True)


def local(
    covariates,
    partition_slot,
    in_weight,
    in_bias,
    out_weight,
    out_bias,
    gradients,
    areas,
    corners,
    tile_rows,
    tile_cols,
    probe,
):
    elements = areas.shape[0]
    slabs = lax.axis_size("slab")
    sds = jax.ShapeDtypeStruct
    vm = pltpu.VMEM
    routed, send = call(
        route_kernel,
        (sds((BLK, BLK), F32), sds((SEND_ROWS, 512), BF16)),
        [HBM] * 5 + [SMEM] + [HBM] * 4 + [VMEM] * 2,
        (VMEM, VMEM),
        [
            vm(covariates.shape, BF16),
            vm(partition_slot.shape, jnp.int32),
            vm(in_weight.shape, BF16),
            vm((1, in_bias.shape[0]), F32),
            vm(out_weight.shape, BF16),
            vm(gradients.shape, F32),
            vm((1, elements), F32),
            vm((3, 2, elements), jnp.int32),
            vm((BLK, elements), BF16),
            vm((1, elements), F32),
            vm((BLK, elements), BF16),
            vm((3, elements), F32),
            vm((8, 512), F32),
            pltpu.SemaphoreType.DMA((9,)),
        ],
        400_000_000,
        1_000_000,
        60,
    )(
        covariates, partition_slot, in_weight, in_bias[None], out_weight, out_bias,
        gradients, areas[None], corners.transpose(1, 0, 2), probe, tile_rows[None], tile_cols[None],
    )
    everything = lax.all_gather(send, "sub")
    arrived = lax.all_to_all(routed, "slab", split_axis=0, concat_axis=0, tiled=True)
    own = everything[:, :COLS]
    up = [(i, i + 1) for i in range(slabs - 1)]
    before = lax.ppermute(own, "slab", up)
    after = lax.ppermute(own, "slab", [(j, i) for i, j in up])
    tid, geo, pos, info = call(
        list_kernel,
        (
            sds((SLOTS, BLK), F32),
            sds((13, SLOTS, BLK), F32),
            sds((6, SLOTS, BLK), jnp.int32),
            sds((2, SLOTS + 1), jnp.int32),
        ),
        [VMEM],
        (VMEM, VMEM, VMEM, SMEM),
        [
            vm((11, SLOTS, BLK), F32),
            vm((8, BLK), jnp.int32),
            pltpu.SMEM((8, BLK), jnp.int32),
            pltpu.SemaphoreType.DMA((1,)),
        ],
        10_000_000,
        1_000_000,
    )(everything)
    got = shared(arrived.astype(BF16))
    return call(
        apply_kernel,
        sds((COLS, probe.shape[1]), F32),
        [SMEM] + [VMEM] * 4 + [ANY] * 3,
        VMEM,
        [
            vm((BLK, RANKS * BLK), BF16),
            vm((6 * SLOTS, RANKS * BLK), BF16),
            vm((6, SLOTS, BLK), F32),
            vm((BLK, BLK), F32),
            vm((3 * SUBS, COLS, probe.shape[1]), BF16),
            vm((BLK_DEV, COLS, BLK), F32),
            pltpu.SemaphoreType.DMA((3,)),
        ],
        1_000_000_000,
        3_000_000,
    )(info, got, tid, geo, pos, before, own, after)


def solution(mesh):
    placed = (
        P(("slab", "sub"), None),
        P(None, ("slab", "sub")),
        P(),
        P(),
        P(),
        P(),
        P(None, None, ("slab", "sub")),
        P(("slab", "sub")),
        P(None, None, ("slab", "sub")),
        P(("slab", "sub")),
        P(("slab", "sub")),
        P(None, ("slab", "sub")),
    )
    return jax.shard_map(
        local, mesh=mesh, in_specs=placed, out_specs=P(None, ("slab", "sub")), check_vma=False
    )
```

time: 86.9 us -> 78.9 us (0.908)
  the two profiles are of different devices: /device:TPU:64 before, /device:TPU:10 now
where the time goes in v2:
time: 78.9 us; the launch traced here: 78.6 us
  starting transfers between devices  32.4 us (41%)
  waiting for transfers between devices  15.9 us (20%)
  Pallas kernels  15 us (19%)
  between operations  13.5 us (17%)
  local copies, waits for them, and re-layouts  1.73 us (2%)
    all_to_all x1, starting transfers between devices, local(): lax.all_to_all(routed, 'slab', split_axis=0, concat_axis=0, tiled=True)  19.6 us
    all_gather x1, waiting for transfers between devices, local(): everything = lax.all_gather(send, 'sub')  15.3 us
    pallas_call x1, Pallas kernels, local(): call(apply_kernel, sds((COLS, probe.shape[1]), F32), [SMEM] + [VMEM] * 4...  5.93 us
    ppermute x1, starting transfers between devices, local(): after = lax.ppermute(own, 'slab', [(j, i) for i, j in up])  5.75 us
    pallas_call x1, Pallas kernels, local(): call(route_kernel, (sds((BLK, BLK), F32), sds((SEND_ROWS, 512), BF16)), [...  5.24 us
    all_to_all x1, starting transfers between devices, shared(): lax.all_to_all(copies, 'sub', split_axis=0, concat_axis=0, tiled=True)  5.11 us
    pallas_call x1, Pallas kernels, local(): call(list_kernel, (sds((SLOTS, BLK), F32), sds((13, SLOTS, BLK), F32), sd...  3.87 us
    ppermute x1, starting transfers between devices, local(): before = lax.ppermute(own, 'slab', up)  1.92 us
  transfers between devices with their start and end apart: 5, of which 2 were waited for; matrix products, arithmetic and copies ran while one was open for 2% of the time, Pallas kernels for 5%

profile of v2, /device:TPU:10, one launch (start us, length us, event | category | flops | bytes accessed | tf_op | source)
XLA Modules:
  0.0 78.6 jit_solution(2190144931552217822)
XLA Ops:
  6.5 0.0 all-gather.3.cloned.1.call-start
  6.5 5.2 %shard_map.118 = (f32[128,128]{1,0:T(8,128)}, bf16[256,512]{1,0:T(8,128)(2,1)}) custom-call(bf16[2048,128]{1,0:T(8,128)(2,1)} %cov_hbm.1, s32[2,2048]{1,0:T(2,128)} %slot_hbm.1, bf16[128,256]{1,0:T(8,128)(2,1)} %w1_hbm.1, f32[1,256]{1,0:T(1,128)} %bitcast.17, bf16[3,256]{1,0:T(4,128)(2,1)} %w2_hbm.1, f32[3]{0:T(128)} %b2_ref.1, f32[2,2,2048]{2,1,0:T(2,128)} %grad_hbm.1, ...), custom_call_target="tpu_custom_call" | custom-call | flops 400000000 | bytes 1000000 | tf_op jit(solution)/shard_map/pallas_call | solution.py:286
  11.8 0.0 all-gather.3.cloned.1.call-update
  11.8 19.6 %all-to-all-start = ((f32[128,1,128]{2,1,0:T(1,128)}), f32[128,1,128]{2,1,0:T(1,128)S(1)}, u32[]{:S(2)}, u32[]{:S(2)}) async-start(f32[128,1,128]{2,1,0:T(1,128)} %bitcast.7), calls=%async_computation | async-start | bytes 131072 | tf_op jit(solution)/shard_map/all_to_all | solution.py:315
  31.4 15.3 %all-gather.3.cloned.1.call-done = bf16[1024,512]{1,0:T(8,128)(2,1)} async-done(((bf16[256,512]{1,0:T(8,128)(2,1)}), bf16[1024,512]{1,0:T(8,128)(2,1)}) %all-gather.3.cloned.1.call-update) | async-done | bytes 1048592 | tf_op jit(solution)/shard_map/all_gather | solution.py:314
  46.7 0.0 copy-start
  46.7 1.1 %slice.4.own_hbm = bf16[4,64,512]{2,1,0:T(8,128)(2,1)S(1)} slice(bf16[4,256,512]{2,1,0:T(8,128)(2,1)} %bitcast.12), slice={[0:4], [0:64], [0:512]} | slice | bytes 524288 | tf_op jit(solution)/shard_map/slice | solution.py:316
  47.8 1.9 %collective-permute-start = (bf16[4,64,512]{2,1,0:T(8,128)(2,1)S(1)}, bf16[4,64,512]{2,1,0:T(8,128)(2,1)S(1)}, u32[]{:S(2)}, u32[]{:S(2)}) collective-permute-start(bf16[4,64,512]{2,1,0:T(8,128)(2,1)S(1)} %slice.4.own_hbm), channel_id=1, source_target_pairs={{0,4},{4,8},{8,12},{12,16},{16,20},{20,24},{24,28},{28,32},{32,36}... | collective-permute-start | bytes 786440 | tf_op jit(solution)/shard_map/ppermute | solution.py:318
  49.7 5.8 %collective-permute-start.1 = (bf16[4,64,512]{2,1,0:T(8,128)(2,1)S(1)}, bf16[4,64,512]{2,1,0:T(8,128)(2,1)S(1)}, u32[]{:S(2)}, u32[]{:S(2)}) collective-permute-start(bf16[4,64,512]{2,1,0:T(8,128)(2,1)S(1)} %slice.4.own_hbm), channel_id=1, source_target_pairs={{4,0},{8,4},{12,8},{16,12},{20,16},{24,20},{28,24},{32,28},{36,32}... | collective-permute-start | bytes 786440 | tf_op jit(solution)/shard_map/ppermute | solution.py:319
  55.5 0.0 all-to-all-done
  55.5 0.7 broadcast_in_dim.22
  56.2 5.1 %all-to-all-start.1 = ((bf16[4,128,128]{2,1,0:T(8,128)(2,1)}), bf16[4,128,128]{2,1,0:T(8,128)(2,1)S(1)}, u32[]{:S(2)}, u32[]{:S(2)}) async-start(bf16[4,128,128]{2,1,0:T(8,128)(2,1)} %broadcast_in_dim.22), calls=%async_computation.1 | async-start | bytes 262144 | tf_op jit(solution)/shard_map/all_to_all | solution.py:265
  61.3 0.0 copy-done
  61.3 3.9 %shard_map.119 = (f32[32,128]{1,0:T(8,128)S(1)}, f32[13,32,128]{2,1,0:T(8,128)S(1)}, s32[6,32,128]{2,1,0:T(8,128)S(1)}, s32[2,33]{1,0:T(2,128)S(1)}) custom-call(bf16[4,256,512]{2,1,0:T(8,128)(2,1)S(1)} %bitcast.13), custom_call_target="tpu_custom_call" | custom-call | flops 10000000 | bytes 1000000 | tf_op jit(solution)/shard_map/pallas_call | solution.py:320
  65.1 0.6 all-to-all-done.1.got_ref
  65.8 0.0 collective-permute-done.before_hbm
  65.8 0.0 collective-permute-done.1.after_hbm
  65.8 5.9 %shard_map.120 = f32[64,512]{1,0:T(8,128)} custom-call(s32[2,33]{1,0:T(2,128)S(1)} %get-tuple-element.12.info_ref, bf16[4,128,128]{2,1,0:T(8,128)(2,1)S(1)} %all-to-all-done.1.got_ref, f32[32,128]{1,0:T(8,128)S(1)} %get-tuple-element.14.tid_ref, f32[13,32,128]{2,1,0:T(8,128)S(1)} %get-tuple-element.15.geo_ref, s32[6,32,128]{2,1,0:T(8,128)S(1)} %get-tuple-element.16.pos_ref, ...), custom_call_target="tpu_custom_call" | custom-call | flops 1000000000 | bytes 3000000 | tf_op jit(solution)/shard_map/pallas_call | solution.py:340
  (1 shorter events, 0.0 us)
Async XLA Ops:
  6.5 40.2 %all-gather.3.cloned.1.call-start = ((), (), s32[]{:S(2)}) async-start(), calls=%async_computation.2 | async-start | bytes 1310720 | tf_op jit(solution)/shard_map/all_gather | solution.py:314
  11.8 43.7 %all-to-all-start = ((f32[128,1,128]{2,1,0:T(1,128)}), f32[128,1,128]{2,1,0:T(1,128)S(1)}, u32[]{:S(2)}, u32[]{:S(2)}) async-start(f32[128,1,128]{2,1,0:T(1,128)} %bitcast.7), calls=%async_computation | async-start | bytes 131072 | tf_op jit(solution)/shard_map/all_to_all | solution.py:315
  46.7 14.6 %copy-start = (bf16[1024,512]{1,0:T(8,128)(2,1)S(1)}, bf16[1024,512]{1,0:T(8,128)(2,1)}, u32[]{:S(2)}) copy-start(bf16[1024,512]{1,0:T(8,128)(2,1)} %all-gather.3.cloned.1.call-done) | copy-start | bytes 3145732
  47.8 18.0 %collective-permute-start = (bf16[4,64,512]{2,1,0:T(8,128)(2,1)S(1)}, bf16[4,64,512]{2,1,0:T(8,128)(2,1)S(1)}, u32[]{:S(2)}, u32[]{:S(2)}) collective-permute-start(bf16[4,64,512]{2,1,0:T(8,128)(2,1)S(1)} %slice.4.own_hbm), channel_id=1, source_target_pairs={{0,4},{4,8},{8,12},{12,16},{16,20},{20,24},{24,28},{28,32},{32,36}... | collective-permute-start | bytes 786440 | tf_op jit(solution)/shard_map/ppermute | solution.py:318
  49.7 16.1 %collective-permute-start.1 = (bf16[4,64,512]{2,1,0:T(8,128)(2,1)S(1)}, bf16[4,64,512]{2,1,0:T(8,128)(2,1)S(1)}, u32[]{:S(2)}, u32[]{:S(2)}) collective-permute-start(bf16[4,64,512]{2,1,0:T(8,128)(2,1)S(1)} %slice.4.own_hbm), channel_id=1, source_target_pairs={{4,0},{8,4},{12,8},{16,12},{20,16},{24,20},{28,24},{32,28},{36,32}... | collective-permute-start | bytes 786440 | tf_op jit(solution)/shard_map/ppermute | solution.py:319
  56.2 9.6 %all-to-all-start.1 = ((bf16[4,128,128]{2,1,0:T(8,128)(2,1)}), bf16[4,128,128]{2,1,0:T(8,128)(2,1)S(1)}, u32[]{:S(2)}, u32[]{:S(2)}) async-start(bf16[4,128,128]{2,1,0:T(8,128)(2,1)} %broadcast_in_dim.22), calls=%async_computation.1 | async-start | bytes 262144 | tf_op jit(solution)/shard_map/all_to_all | solution.py:265
Sparse Core Ops, SparseCore 0:
  11.9 34.7 all-gather.2

commit v3 on v2

v3 whole, which is shorter than its diff:
```python
import jax
import jax.numpy as jnp
from jax import lax
from jax.experimental import pallas as pl
from jax.experimental.pallas import tpu as pltpu
from jax.sharding import PartitionSpec as P

BLK = 128
CHUNKS = 16
RANKS = 16
FIELDS = 8
SLOTS = 32
TILES_SLAB = 64
TILE_DEV = 16
SUBS = 4
BLK_DEV = 4
COLS = 64
PAIRS = ((0, 0), (0, 1), (0, 2), (1, 1), (1, 2), (2, 2))
PAIR_OF = {(a, b): PAIRS.index((min(a, b), max(a, b))) for a in range(3) for b in range(3)}
NT = (((1,), (1,)), ((), ()))
VMEM = pl.BlockSpec(memory_space=pltpu.VMEM)
SMEM = pl.BlockSpec(memory_space=pltpu.SMEM)
F32 = jnp.float32
BF16 = jnp.bfloat16
HBM = pl.BlockSpec(memory_space=pltpu.HBM)
ANY = pl.BlockSpec(memory_space=pl.ANY)
ELEM_FIELDS = 16
META = COLS + 4 * ELEM_FIELDS
SEND_ROWS = META + 16
UNROLL = 4


def call(kernel, out_shape, in_specs, out_specs, scratch, flops, nbytes, vmem=40):
    return pl.pallas_call(
        kernel,
        out_shape=out_shape,
        in_specs=in_specs,
        out_specs=out_specs,
        scratch_shapes=scratch,
        compiler_params=pltpu.CompilerParams(vmem_limit_bytes=vmem * 1024 * 1024),
        cost_estimate=pl.CostEstimate(flops=flops, bytes_accessed=nbytes, transcendentals=0),
    )


def lanes(chunk):
    return slice(chunk * BLK, (chunk + 1) * BLK)


def halves(x):
    high = x.astype(BF16)
    return high, (x - high.astype(F32)).astype(BF16)


def start_all(pairs, sem):
    copies = [pltpu.make_async_copy(s, d, sem.at[i]) for i, (s, d) in enumerate(pairs)]
    for c in copies:
        c.start()
    return copies


def pack_kernel(grad_hbm, area_hbm, corner_hbm, rows_ref, cols_ref, probe_hbm, send_ref, grad_ref, area_ref, corner_ref, meta_ref, sem):
    copies = start_all(
        ((grad_hbm, grad_ref), (area_hbm, area_ref), (corner_hbm, corner_ref), (probe_hbm, send_ref.at[0:COLS])), sem
    )
    meta_ref[...] = jnp.zeros(meta_ref.shape, F32)
    for i, ref in enumerate((rows_ref, cols_ref)):
        meta_ref[2 * i : 2 * i + 1, 0:TILE_DEV] = (ref[...] >> 4).astype(F32)
        meta_ref[2 * i + 1 : 2 * i + 2, 0:TILE_DEV] = (ref[...] & 15).astype(F32)
    send_ref[META:, :] = meta_ref[...].astype(BF16)
    for c in copies:
        c.wait()
    for q in range(4):
        here = slice(q * 512, (q + 1) * 512)
        values = [grad_ref[i, j : j + 1, here] for i in range(2) for j in range(2)] + [area_ref[:, here]]
        fields = [half.astype(F32) for v in values for half in halves(v)]
        fields += [corner_ref[a, side : side + 1, here].astype(F32) for side in range(2) for a in range(3)]
        top = COLS + q * ELEM_FIELDS
        send_ref[top : top + ELEM_FIELDS, :] = jnp.concatenate(fields, axis=0).astype(BF16)


def route_kernel(
    cov_hbm, slot_hbm, w1_hbm, b1_hbm, w2_hbm, b2_ref,
    out_ref,
    cov_ref, slot_ref, w1_ref, b1_ref, w2_ref, hot_ref, rank_ref, val_ref, par_ref, sem,
):
    copies = start_all(
        ((slot_hbm, slot_ref), (w1_hbm, w1_ref), (b1_hbm, b1_ref), (w2_hbm, w2_ref), (cov_hbm, cov_ref)), sem
    )
    slab_iota = lax.broadcasted_iota(jnp.int32, (BLK, BLK), 0)
    lane_iota = lax.broadcasted_iota(jnp.int32, (BLK, BLK), 1)
    earlier = jnp.concatenate(
        [jnp.where(slab_iota < lane_iota, 1.0, 0.0).astype(BF16), jnp.ones((BLK, BLK), BF16)], axis=1
    )
    copies[0].wait()
    for chunk in range(CHUNKS):
        slab = slot_ref[0:1, lanes(chunk)] >> 2
        hot_ref[:, lanes(chunk)] = jnp.where(slab_iota == slab, 1.0, 0.0).astype(BF16)
    seen = jnp.zeros((BLK, BLK), F32)
    for chunk in range(CHUNKS):
        hot = hot_ref[:, lanes(chunk)]
        counts = jnp.dot(hot, earlier, preferred_element_type=F32)
        rank_ref[:, lanes(chunk)] = jnp.sum(
            hot.astype(F32) * (counts[:, :BLK] + seen), axis=0, keepdims=True
        )
        seen = seen + counts[:, BLK:]
    for c in copies[1:]:
        c.wait()
    rows = 256
    for part in range(cov_ref.shape[0] // rows):
        here = slice(part * rows, (part + 1) * rows)
        pre_act = jnp.dot(cov_ref[here, :], w1_ref[...], preferred_element_type=F32) + b1_ref[...]
        hidden = jax.nn.gelu(pre_act, approximate=True).astype(BF16)
        par_ref[:, here] = lax.dot_general(w2_ref[...], hidden, NT, preferred_element_type=F32)
    rank_iota = lax.broadcasted_iota(jnp.int32, (RANKS, BLK), 0).astype(F32)
    for chunk in range(CHUNKS):
        device = slot_ref[0:1, lanes(chunk)]
        place = slot_ref[1:2, lanes(chunk)]
        values = []
        for f in range(3):
            values += [half.astype(F32) for half in halves(par_ref[f : f + 1, lanes(chunk)] + b2_ref[f])]
        values += [((device & 3) * TILE_DEV + (place >> 7)).astype(F32), (place & 127).astype(F32)]
        mine = rank_iota == rank_ref[:, lanes(chunk)]
        val_ref[:, lanes(chunk)] = jnp.concatenate(
            [jnp.where(mine, v, 0.0).astype(BF16) for v in values], axis=0
        )
    out_ref[...] = lax.dot_general(hot_ref[...], val_ref[...], NT, preferred_element_type=F32)


def list_kernel(
    s0_hbm, s1_hbm, s2_hbm, s3_hbm,
    tid_ref, geo_ref, pos_ref, info_ref,
    all_ref, raw_ref, ints_ref, meta_ref, sem, meta_sem,
):
    me = lax.axis_index("sub")
    base = (lax.axis_index("slab") - 1) * (SUBS * BLK_DEV)
    copies = start_all([(s, all_ref.at[i]) for i, s in enumerate((s0_hbm, s1_hbm, s2_hbm, s3_hbm))], sem)
    tid_ref[...] = jnp.full(tid_ref.shape, -1.0, F32)
    raw_ref[...] = jnp.zeros(raw_ref.shape, F32)
    for n in range(SLOTS):
        info_ref[0, n] = 0
        info_ref[1, n] = SUBS * BLK_DEV
    for c in copies:
        c.wait()
    for v in range(SUBS):
        coded = all_ref[v, META : META + 16, 0:BLK].astype(F32)
        for i in range(2):
            whole = coded[2 * i : 2 * i + 1] * 16.0 + coded[2 * i + 1 : 2 * i + 2]
            ints_ref[4 * i + v : 4 * i + v + 1, :] = whole.astype(jnp.int32)
    copy = pltpu.make_async_copy(ints_ref, meta_ref, meta_sem.at[0])
    copy.start()
    copy.wait()

    def find(t, n):
        v, k = t // TILE_DEV, t % TILE_DEV
        row = meta_ref[v, k]
        owned = (row // BLK_DEV) % SUBS == me

        @pl.when(owned)
        def _():
            tile = (me - v) % SUBS * TILE_DEV + k
            col = meta_ref[4 + v, k] - base
            step, s, blk = col // (SUBS * BLK_DEV), col // BLK_DEV % SUBS, col % BLK_DEV
            info_ref[0, n] = row % BLK_DEV
            info_ref[1, n] = (step * SUBS + (me - s) % SUBS) * BLK_DEV + blk
            tid_ref[pl.ds(n, 1), :] = jnp.full((1, BLK), tile, jnp.int32).astype(F32)
            top = pl.ds(pl.multiple_of(COLS + (k // 4) * ELEM_FIELDS, 16), ELEM_FIELDS)
            here = pl.ds(pl.multiple_of((k % 4) * BLK, BLK), BLK)
            raw_ref[pl.ds(n, 1)] = all_ref[v, top, here].astype(F32)[None]

        return n + owned.astype(jnp.int32)

    info_ref[0, SLOTS] = lax.fori_loop(0, TILES_SLAB, find, jnp.int32(0))
    field = [raw_ref[:, f, :] for f in range(ELEM_FIELDS)]
    value = [field[2 * i] + field[2 * i + 1] for i in range(5)]
    grad_x = [value[0], value[1], -(value[0] + value[1])]
    grad_y = [value[2], value[3], -(value[2] + value[3])]
    for i, (a, b) in enumerate(PAIRS):
        geo_ref[i] = grad_x[a] * grad_x[b] + grad_y[a] * grad_y[b]
        geo_ref[6 + i] = grad_x[a] * grad_y[b] + grad_y[a] * grad_x[b]
    geo_ref[12] = value[4]
    for a in range(6):
        pos_ref[a] = field[10 + a].astype(jnp.int32)


def matrix_kernel(got_ref, tid_ref, geo_ref, k_ref, hot_ref, val_ref, turned_ref):
    lane_iota = lax.broadcasted_iota(jnp.int32, (BLK, BLK), 0).astype(F32).astype(BF16)
    one, zero = jnp.ones((), BF16), jnp.zeros((), BF16)
    tiles = tid_ref[...].astype(BF16)
    found = jnp.zeros((6 * SLOTS, BLK), F32)
    for u in range(SUBS):
        turned_ref[...] = got_ref[u].astype(F32).T
        for k in range(RANKS):
            rows = [
                jnp.broadcast_to(turned_ref[f * RANKS + k : f * RANKS + k + 1, :], (16, BLK)).astype(BF16)
                for f in range(FIELDS)
            ]
            twice = [jnp.concatenate([r, r], axis=0) for r in rows[:7]]
            mine = tiles == twice[6]
            val_ref[:, lanes(k)] = jnp.concatenate([jnp.where(mine, twice[f], zero) for f in range(6)], axis=0)
            hot_ref[:, lanes(k)] = jnp.where(lane_iota == jnp.concatenate([rows[7]] * 8, axis=0), one, zero)
        found = found + lax.dot_general(val_ref[...], hot_ref[...], NT, preferred_element_type=F32)
    params = [
        found[2 * f * SLOTS : (2 * f + 1) * SLOTS] + found[(2 * f + 1) * SLOTS : (2 * f + 2) * SLOTS]
        for f in range(3)
    ]
    kappa_sq = jnp.exp(params[0])
    scale = jnp.exp(params[1])
    coupling = 0.9 * jnp.tanh(params[2])
    area = geo_ref[12]
    for i, (a, b) in enumerate(PAIRS):
        mass = kappa_sq * (2.0 if a == b else 1.0)
        stiffness = scale * (geo_ref[i] + coupling * geo_ref[6 + i])
        k_ref[i] = (area * (stiffness + mass)).astype(BF16).astype(F32)


def apply_kernel(
    info_ref, k_ref, pos_ref, before_hbm, own_hbm, after_hbm,
    out_ref, x_ref, acc_ref, sem,
):
    copies = start_all(
        [(src, x_ref.at[SUBS * i : SUBS * (i + 1)]) for i, src in enumerate((before_hbm, own_hbm, after_hbm))], sem
    )
    lane_iota = lax.broadcasted_iota(jnp.int32, (BLK, BLK), 0).astype(F32).astype(BF16)
    one, zero = jnp.ones((), BF16), jnp.zeros((), BF16)
    acc_ref[...] = jnp.zeros(acc_ref.shape, F32)
    for c in copies:
        c.wait()

    def tile_part(n):
        col = info_ref[1, n]
        where = pl.ds(pl.multiple_of((col % BLK_DEV) * BLK, BLK), BLK)
        x = x_ref[col // BLK_DEV, :, where].astype(F32)
        k = [k_ref[i, pl.ds(n, 1), :] for i in range(6)]
        xs = [
            jnp.take_along_axis(x, jnp.broadcast_to(pos_ref[3 + b, pl.ds(n, 1), :], (COLS, BLK)), axis=1)
            for b in range(3)
        ]
        ys = []
        hots = []
        for a in range(3):
            y = k[PAIR_OF[a, 0]] * xs[0] + k[PAIR_OF[a, 1]] * xs[1] + k[PAIR_OF[a, 2]] * xs[2]
            ys.append(y.astype(BF16))
            row = jnp.broadcast_to(pos_ref[a, pl.ds(n, 1), :].astype(F32), (16, BLK)).astype(BF16)
            hots.append(jnp.where(lane_iota == jnp.concatenate([row] * 8, axis=0), one, zero))
        return lax.dot_general(
            jnp.concatenate(ys, axis=1), jnp.concatenate(hots, axis=1), NT, preferred_element_type=F32
        )

    def add(group, carry):
        done = [tile_part(group * UNROLL + i) for i in range(UNROLL)]
        for i in range(UNROLL):
            block = info_ref[0, group * UNROLL + i]
            acc_ref[block] = acc_ref[block] + done[i]
        return carry

    lax.fori_loop(0, (info_ref[0, SLOTS] + UNROLL - 1) // UNROLL, add, jnp.int32(0))
    for block in range(BLK_DEV):
        out_ref[:, lanes(block)] = acc_ref[block]


def shared(block):
    copies = jnp.broadcast_to(block[None], (SUBS, *block.shape))
    return lax.all_to_all(copies, "sub", split_axis=0, concat_axis=0, tiled=True)


def route(covariates, partition_slot, in_weight, in_bias, out_weight, out_bias):
    elements = partition_slot.shape[1]
    vm = pltpu.VMEM
    return call(
        route_kernel,
        jax.ShapeDtypeStruct((BLK, BLK), F32),
        [HBM] * 5 + [SMEM],
        VMEM,
        [
            vm(covariates.shape, BF16),
            vm(partition_slot.shape, jnp.int32),
            vm(in_weight.shape, BF16),
            vm((1, in_bias.shape[0]), F32),
            vm(out_weight.shape, BF16),
            vm((BLK, elements), BF16),
            vm((1, elements), F32),
            vm((BLK, elements), BF16),
            vm((3, elements), F32),
            pltpu.SemaphoreType.DMA((5,)),
        ],
        400_000_000,
        1_000_000,
        60,
    )(covariates, partition_slot, in_weight, in_bias[None], out_weight, out_bias)


def pack(gradients, areas, corners, tile_rows, tile_cols, probe):
    vm = pltpu.VMEM
    return call(
        pack_kernel,
        jax.ShapeDtypeStruct((SEND_ROWS, probe.shape[1]), BF16),
        [HBM] * 3 + [VMEM] * 2 + [HBM],
        VMEM,
        [
            vm(gradients.shape, F32),
            vm((1, areas.shape[0]), F32),
            vm((3, 2, areas.shape[0]), jnp.int32),
            vm((16, probe.shape[1]), F32),
            pltpu.SemaphoreType.DMA((4,)),
        ],
        1_000_000,
        1_000_000,
        60,
    )(gradients, areas[None], corners.transpose(1, 0, 2), tile_rows[None], tile_cols[None], probe)


def listed(sends):
    sds = jax.ShapeDtypeStruct
    vm = pltpu.VMEM
    return call(
        list_kernel,
        (
            sds((SLOTS, BLK), F32),
            sds((13, SLOTS, BLK), F32),
            sds((6, SLOTS, BLK), jnp.int32),
            sds((2, SLOTS + 1), jnp.int32),
        ),
        [ANY] * 4,
        (VMEM, VMEM, VMEM, SMEM),
        [
            vm((SUBS, *sends[0].shape), BF16),
            vm((SLOTS, ELEM_FIELDS, BLK), F32),
            vm((8, BLK), jnp.int32),
            pltpu.SMEM((8, BLK), jnp.int32),
            pltpu.SemaphoreType.DMA((4,)),
            pltpu.SemaphoreType.DMA((1,)),
        ],
        10_000_000,
        1_000_000,
    )(*sends)


def matrices(got, tid, geo):
    vm = pltpu.VMEM
    return call(
        matrix_kernel,
        jax.ShapeDtypeStruct((6, SLOTS, BLK), F32),
        [VMEM] * 3,
        VMEM,
        [
            vm((BLK, RANKS * BLK), BF16),
            vm((6 * SLOTS, RANKS * BLK), BF16),
            vm((BLK, BLK), F32),
        ],
        1_000_000_000,
        3_000_000,
    )(got, tid, geo)


def applied(info, k, pos, before, own, after):
    vm = pltpu.VMEM
    return call(
        apply_kernel,
        jax.ShapeDtypeStruct((COLS, own.shape[2]), F32),
        [SMEM] + [VMEM] * 2 + [ANY] * 3,
        VMEM,
        [
            vm((3 * SUBS, *own.shape[1:]), BF16),
            vm((BLK_DEV, COLS, BLK), F32),
            pltpu.SemaphoreType.DMA((3,)),
        ],
        1_000_000_000,
        3_000_000,
    )(info, k, pos, before, own, after)


def local(
    covariates,
    partition_slot,
    in_weight,
    in_bias,
    out_weight,
    out_bias,
    gradients,
    areas,
    corners,
    tile_rows,
    tile_cols,
    probe,
):
    slabs = lax.axis_size("slab")
    routed = route(covariates, partition_slot, in_weight, in_bias, out_weight, out_bias)
    arrived = lax.all_to_all(routed, "slab", split_axis=0, concat_axis=0, tiled=True)
    send = pack(gradients, areas, corners, tile_rows, tile_cols, probe)
    sends = [send] + [lax.ppermute(send, "sub", [(i, (i + k) % SUBS) for i in range(SUBS)]) for k in (1, 2, 3)]
    got = shared(arrived.astype(BF16))
    own = jnp.stack([s[:COLS] for s in sends])
    up = [(i, i + 1) for i in range(slabs - 1)]
    before = lax.ppermute(own, "slab", up)
    after = lax.ppermute(own, "slab", [(j, i) for i, j in up])
    tid, geo, pos, info = listed(sends)
    return applied(info, matrices(got, tid, geo), pos, before, own, after)


def solution(mesh):
    placed = (
        P(("slab", "sub"), None),
        P(None, ("slab", "sub")),
        P(),
        P(),
        P(),
        P(),
        P(None, None, ("slab", "sub")),
        P(("slab", "sub")),
        P(None, None, ("slab", "sub")),
        P(("slab", "sub")),
        P(("slab", "sub")),
        P(None, ("slab", "sub")),
    )
    return jax.shard_map(
        local, mesh=mesh, in_specs=placed, out_specs=P(None, ("slab", "sub")), check_vma=False
    )
```

time: 78.9 us -> 70.3 us (0.89)
  the two profiles are of different devices: /device:TPU:10 before, /device:TPU:2 now
where the time goes in v3:
time: 70.3 us; the launch traced here: 69.9 us
  starting transfers between devices  38 us (54%)
  Pallas kernels  18.4 us (26%)
  waiting for transfers between devices  12.5 us (18%)
    all_to_all x1, starting transfers between devices, local(): lax.all_to_all(routed, 'slab', split_axis=0, concat_axis=0, tiled=True)  16.7 us
    ppermute x3, starting transfers between devices, local(): lax.ppermute(send, 'sub', [(i, (i + k) % SUBS) for i in range(SUBS)])  13.7 us
    all_to_all x1, waiting for transfers between devices, local(): lax.all_to_all(routed, 'slab', split_axis=0, concat_axis=0, tiled=True)  12.5 us
    pallas_call x1, Pallas kernels, listed(): call(list_kernel, (sds((SLOTS, BLK), F32), sds((13, SLOTS, BLK), F32), sd...  5.06 us
    pallas_call x1, Pallas kernels, route(): call(route_kernel, jax.ShapeDtypeStruct((BLK, BLK), F32), [HBM] * 5 + [SM...  5.04 us
    all_to_all x1, starting transfers between devices, shared(): lax.all_to_all(copies, 'sub', split_axis=0, concat_axis=0, tiled=True)  4.72 us
    pallas_call x1, Pallas kernels, applied(): call(apply_kernel, jax.ShapeDtypeStruct((COLS, own.shape[2]), F32), [SMEM...  4.04 us
    pallas_call x1, Pallas kernels, pack(): call(pack_kernel, jax.ShapeDtypeStruct((SEND_ROWS, probe.shape[1]), BF16)...  2.39 us
  transfers between devices with their start and end apart: 7, of which 1 were waited for; matrix products, arithmetic and copies ran while one was open for 1% of the time, Pallas kernels for 17%

profile of v3, /device:TPU:2, one launch (start us, length us, event | category | flops | bytes accessed | tf_op | source)
XLA Modules:
  0.0 69.9 jit_solution(10302153639319461711)
XLA Ops:
  0.0 2.4 %shard_map.118.s0_hbm = bf16[144,512]{1,0:T(8,128)(2,1)} custom-call(f32[2,2,2048]{2,1,0:T(2,128)} %grad_hbm.1, f32[1,2048]{1,0:T(1,128)} %bitcast.22, s32[3,2,2048]{2,1,0:T(2,128)} %bitcast.21, s32[1,16]{1,0:T(1,128)} %bitcast.23, s32[1,16]{1,0:T(1,128)} %bitcast.24, bf16[64,512]{1,0:T(8,128)(2,1)} %probe_hbm.1), custom_call_target="tpu_custom_call" | custom-call | flops 1000000 | bytes 1000000 | tf_op jit(solution)/shard_map/pallas_call | solution.py:294
  2.4 3.4 %collective-permute-start = (bf16[144,512]{1,0:T(8,128)(2,1)}, bf16[144,512]{1,0:T(8,128)(2,1)S(1)}, u32[]{:S(2)}, u32[]{:S(2)}) collective-permute-start(bf16[144,512]{1,0:T(8,128)(2,1)} %shard_map.118.s0_hbm), channel_id=1, source_target_pairs={{0,1},{1,2},{2,3},{3,0},{4,5},{5,6},{6,7},{7,4},{8,9},{9,10},{10,1... | collective-permute-start | bytes 442376 | tf_op jit(solution)/shard_map/ppermute | solution.py:390
  5.8 8.4 %collective-permute-start.1 = (bf16[144,512]{1,0:T(8,128)(2,1)}, bf16[144,512]{1,0:T(8,128)(2,1)S(1)}, u32[]{:S(2)}, u32[]{:S(2)}) collective-permute-start(bf16[144,512]{1,0:T(8,128)(2,1)} %shard_map.118.s0_hbm), channel_id=1, source_target_pairs={{0,2},{1,3},{2,0},{3,1},{4,6},{5,7},{6,4},{7,5},{8,10},{9,11},{10,... | collective-permute-start | bytes 442376 | tf_op jit(solution)/shard_map/ppermute | solution.py:390
  14.2 1.9 %collective-permute-start.2 = (bf16[144,512]{1,0:T(8,128)(2,1)}, bf16[144,512]{1,0:T(8,128)(2,1)S(1)}, u32[]{:S(2)}, u32[]{:S(2)}) collective-permute-start(bf16[144,512]{1,0:T(8,128)(2,1)} %shard_map.118.s0_hbm), channel_id=1, source_target_pairs={{0,3},{1,0},{2,1},{3,2},{4,7},{5,4},{6,5},{7,6},{8,11},{9,8},{10,9... | collective-permute-start | bytes 442376 | tf_op jit(solution)/shard_map/ppermute | solution.py:390
  16.1 0.0 copy-start
  16.1 5.0 %shard_map.120 = f32[128,128]{1,0:T(8,128)} custom-call(bf16[2048,128]{1,0:T(8,128)(2,1)} %cov_hbm.1, s32[2,2048]{1,0:T(2,128)} %slot_hbm.1, bf16[128,256]{1,0:T(8,128)(2,1)} %w1_hbm.1, f32[1,256]{1,0:T(1,128)} %bitcast.25, bf16[3,256]{1,0:T(4,128)(2,1)} %w2_hbm.1, f32[3]{0:T(128)} %b2_ref.1), custom_call_target="tpu_custom_call" | custom-call | flops 400000000 | bytes 1000000 | tf_op jit(solution)/shard_map/pallas_call | solution.py:269
  21.2 16.7 %all-to-all-start = ((f32[128,1,128]{2,1,0:T(1,128)}), f32[128,1,128]{2,1,0:T(1,128)S(1)}, u32[]{:S(2)}, u32[]{:S(2)}) async-start(f32[128,1,128]{2,1,0:T(1,128)} %bitcast.20), calls=%async_computation | async-start | bytes 131072 | tf_op jit(solution)/shard_map/all_to_all | solution.py:388
  37.9 0.0 copy-done
  38.0 0.0 collective-permute-done.2.s3_hbm
  38.0 0.0 collective-permute-done.1.s2_hbm
  38.0 0.0 collective-permute-done.s1_hbm
  38.1 1.5 %collective-permute-start.3 = (bf16[4,64,512]{2,1,0:T(8,128)(2,1)S(1)}, bf16[4,64,512]{2,1,0:T(8,128)(2,1)S(1)}, u32[]{:S(2)}, u32[]{:S(2)}) collective-permute-start(bf16[4,64,512]{2,1,0:T(8,128)(2,1)S(1)} %pad_maximum_fusion.own_hbm), channel_id=1, source_target_pairs={{0,4},{4,8},{8,12},{12,16},{16,20},{20,24},{24,28},{28,32},{32,36}... | collective-permute-start | bytes 786440 | tf_op jit(solution)/shard_map/ppermute | solution.py:394
  39.6 1.3 %collective-permute-start.4 = (bf16[4,64,512]{2,1,0:T(8,128)(2,1)S(1)}, bf16[4,64,512]{2,1,0:T(8,128)(2,1)S(1)}, u32[]{:S(2)}, u32[]{:S(2)}) collective-permute-start(bf16[4,64,512]{2,1,0:T(8,128)(2,1)S(1)} %pad_maximum_fusion.own_hbm), channel_id=1, source_target_pairs={{4,0},{8,4},{12,8},{16,12},{20,16},{24,20},{28,24},{32,28},{36,32}... | collective-permute-start | bytes 786440 | tf_op jit(solution)/shard_map/ppermute | solution.py:395
  40.9 12.5 %all-to-all-done = f32[128,1,128]{2,1,0:T(1,128)S(1)} async-done(((f32[128,1,128]{2,1,0:T(1,128)}), f32[128,1,128]{2,1,0:T(1,128)S(1)}, u32[]{:S(2)}, u32[]{:S(2)}) %all-to-all-start) | async-done | bytes 65568 | tf_op jit(solution)/shard_map/all_to_all | solution.py:388
  53.4 0.7 broadcast_in_dim.22
  54.1 4.7 %all-to-all-start.1 = ((bf16[4,128,128]{2,1,0:T(8,128)(2,1)}), bf16[4,128,128]{2,1,0:T(8,128)(2,1)S(1)}, u32[]{:S(2)}, u32[]{:S(2)}) async-start(bf16[4,128,128]{2,1,0:T(8,128)(2,1)} %broadcast_in_dim.22), calls=%async_computation.1 | async-start | bytes 262144 | tf_op jit(solution)/shard_map/all_to_all | solution.py:263
  58.8 5.1 %shard_map.119 = (f32[32,128]{1,0:T(8,128)S(1)}, f32[13,32,128]{2,1,0:T(8,128)S(1)}, s32[6,32,128]{2,1,0:T(8,128)S(1)}, s32[2,33]{1,0:T(2,128)S(1)}) custom-call(bf16[144,512]{1,0:T(8,128)(2,1)S(1)} %copy-done, bf16[144,512]{1,0:T(8,128)(2,1)S(1)} %collective-permute-done.s1_hbm, bf16[144,512]{1,0:T(8,128)(2,1)S(1)} %collective-permute-done.1.s2_hbm, ...), custom_call_target="tpu_custom_call" | custom-call | flops 10000000 | bytes 1000000 | tf_op jit(solution)/shard_map/pallas_call | solution.py:315
  63.9 0.0 all-to-all-done.1.got_ref
  63.9 1.9 %shard_map.121.k_ref = f32[6,32,128]{2,1,0:T(8,128)S(1)} custom-call(bf16[4,128,128]{2,1,0:T(8,128)(2,1)S(1)} %all-to-all-done.1.got_ref, f32[32,128]{1,0:T(8,128)S(1)} %get-tuple-element.10.tid_ref, f32[13,32,128]{2,1,0:T(8,128)S(1)} %get-tuple-element.11.geo_ref), custom_call_target="tpu_custom_call" | custom-call | flops 1000000000 | bytes 3000000 | tf_op jit(solution)/shard_map/pallas_call | solution.py:340
  65.8 0.0 collective-permute-done.3.before_hbm
  65.8 0.0 collective-permute-done.4.after_hbm
  65.8 4.0 %shard_map.122 = f32[64,512]{1,0:T(8,128)} custom-call(s32[2,33]{1,0:T(2,128)S(1)} %get-tuple-element.9.info_ref, f32[6,32,128]{2,1,0:T(8,128)S(1)} %shard_map.121.k_ref, s32[6,32,128]{2,1,0:T(8,128)S(1)} %get-tuple-element.12.pos_ref, bf16[4,64,512]{2,1,0:T(8,128)(2,1)S(1)} %collective-permute-done.3.before_hbm, ...), custom_call_target="tpu_custom_call" | custom-call | flops 1000000000 | bytes 3000000 | tf_op jit(solution)/shard_map/pallas_call | solution.py:357
  (6 shorter events, 0.1 us)
Async XLA Ops:
  2.4 35.6 %collective-permute-start = (bf16[144,512]{1,0:T(8,128)(2,1)}, bf16[144,512]{1,0:T(8,128)(2,1)S(1)}, u32[]{:S(2)}, u32[]{:S(2)}) collective-permute-start(bf16[144,512]{1,0:T(8,128)(2,1)} %shard_map.118.s0_hbm), channel_id=1, source_target_pairs={{0,1},{1,2},{2,3},{3,0},{4,5},{5,6},{6,7},{7,4},{8,9},{9,10},{10,1... | collective-permute-start | bytes 442376 | tf_op jit(solution)/shard_map/ppermute | solution.py:390
  5.8 32.2 %collective-permute-start.1 = (bf16[144,512]{1,0:T(8,128)(2,1)}, bf16[144,512]{1,0:T(8,128)(2,1)S(1)}, u32[]{:S(2)}, u32[]{:S(2)}) collective-permute-start(bf16[144,512]{1,0:T(8,128)(2,1)} %shard_map.118.s0_hbm), channel_id=1, source_target_pairs={{0,2},{1,3},{2,0},{3,1},{4,6},{5,7},{6,4},{7,5},{8,10},{9,11},{10,... | collective-permute-start | bytes 442376 | tf_op jit(solution)/shard_map/ppermute | solution.py:390
  14.2 23.8 %collective-permute-start.2 = (bf16[144,512]{1,0:T(8,128)(2,1)}, bf16[144,512]{1,0:T(8,128)(2,1)S(1)}, u32[]{:S(2)}, u32[]{:S(2)}) collective-permute-start(bf16[144,512]{1,0:T(8,128)(2,1)} %shard_map.118.s0_hbm), channel_id=1, source_target_pairs={{0,3},{1,0},{2,1},{3,2},{4,7},{5,4},{6,5},{7,6},{8,11},{9,8},{10,9... | collective-permute-start | bytes 442376 | tf_op jit(solution)/shard_map/ppermute | solution.py:390
  16.1 21.8 %copy-start = (bf16[144,512]{1,0:T(8,128)(2,1)S(1)}, bf16[144,512]{1,0:T(8,128)(2,1)}, u32[]{:S(2)}) copy-start(bf16[144,512]{1,0:T(8,128)(2,1)} %shard_map.118.s0_hbm) | copy-start | bytes 442372
  21.2 32.2 %all-to-all-start = ((f32[128,1,128]{2,1,0:T(1,128)}), f32[128,1,128]{2,1,0:T(1,128)S(1)}, u32[]{:S(2)}, u32[]{:S(2)}) async-start(f32[128,1,128]{2,1,0:T(1,128)} %bitcast.20), calls=%async_computation | async-start | bytes 131072 | tf_op jit(solution)/shard_map/all_to_all | solution.py:388
  38.1 27.7 %collective-permute-start.3 = (bf16[4,64,512]{2,1,0:T(8,128)(2,1)S(1)}, bf16[4,64,512]{2,1,0:T(8,128)(2,1)S(1)}, u32[]{:S(2)}, u32[]{:S(2)}) collective-permute-start(bf16[4,64,512]{2,1,0:T(8,128)(2,1)S(1)} %pad_maximum_fusion.own_hbm), channel_id=1, source_target_pairs={{0,4},{4,8},{8,12},{12,16},{16,20},{20,24},{24,28},{28,32},{32,36}... | collective-permute-start | bytes 786440 | tf_op jit(solution)/shard_map/ppermute | solution.py:394
  39.6 26.2 %collective-permute-start.4 = (bf16[4,64,512]{2,1,0:T(8,128)(2,1)S(1)}, bf16[4,64,512]{2,1,0:T(8,128)(2,1)S(1)}, u32[]{:S(2)}, u32[]{:S(2)}) collective-permute-start(bf16[4,64,512]{2,1,0:T(8,128)(2,1)S(1)} %pad_maximum_fusion.own_hbm), channel_id=1, source_target_pairs={{4,0},{8,4},{12,8},{16,12},{20,16},{24,20},{28,24},{32,28},{36,32}... | collective-permute-start | bytes 786440 | tf_op jit(solution)/shard_map/ppermute | solution.py:395
  54.1 9.8 %all-to-all-start.1 = ((bf16[4,128,128]{2,1,0:T(8,128)(2,1)}), bf16[4,128,128]{2,1,0:T(8,128)(2,1)S(1)}, u32[]{:S(2)}, u32[]{:S(2)}) async-start(bf16[4,128,128]{2,1,0:T(8,128)(2,1)} %broadcast_in_dim.22), calls=%async_computation.1 | async-start | bytes 262144 | tf_op jit(solution)/shard_map/all_to_all | solution.py:263

commit v4 on v3

--- a/solution.py
+++ b/solution.py
@@ -25,7 +25,9 @@
 HBM = pl.BlockSpec(memory_space=pltpu.HBM)
 ANY = pl.BlockSpec(memory_space=pl.ANY)
 ELEM_FIELDS = 16
-META = COLS + 4 * ELEM_FIELDS
+ROUTED = 32
+ELEMS = ROUTED + COLS
+META = ELEMS + 4 * TILE_DEV
 SEND_ROWS = META + 16
 UNROLL = 4
 
@@ -58,34 +60,26 @@
     return copies
 
 
-def pack_kernel(grad_hbm, area_hbm, corner_hbm, rows_ref, cols_ref, probe_hbm, send_ref, grad_ref, area_ref, corner_ref, meta_ref, sem):
+def front_kernel(
+    cov_hbm, slot_hbm, w1_hbm, b1_hbm, w2_hbm, b2_ref, grad_hbm, area_hbm, corner_hbm, rows_ref, cols_ref, probe_hbm,
+    out_hbm,
+    cov_ref, slot_ref, w1_ref, b1_ref, w2_ref, grad_ref, area_ref, corner_ref, meta_ref,
+    hot_ref, rank_ref, val_ref, par_ref, send_ref, sem, out_sem,
+):
     copies = start_all(
-        ((grad_hbm, grad_ref), (area_hbm, area_ref), (corner_hbm, corner_ref), (probe_hbm, send_ref.at[0:COLS])), sem
+        (
+            (slot_hbm, slot_ref), (grad_hbm, grad_ref), (area_hbm, area_ref), (corner_hbm, corner_ref),
+            (probe_hbm, send_ref.at[ROUTED:ELEMS]),
+            (w1_hbm, w1_ref), (b1_hbm, b1_ref), (w2_hbm, w2_ref), (cov_hbm, cov_ref),
+        ),
+        sem,
     )
     meta_ref[...] = jnp.zeros(meta_ref.shape, F32)
     for i, ref in enumerate((rows_ref, cols_ref)):
         meta_ref[2 * i : 2 * i + 1, 0:TILE_DEV] = (ref[...] >> 4).astype(F32)
         meta_ref[2 * i + 1 : 2 * i + 2, 0:TILE_DEV] = (ref[...] & 15).astype(F32)
-    send_ref[META:, :] = meta_ref[...].astype(BF16)
-    for c in copies:
-        c.wait()
-    for q in range(4):
-        here = slice(q * 512, (q + 1) * 512)
-        values = [grad_ref[i, j : j + 1, here] for i in range(2) for j in range(2)] + [area_ref[:, here]]
-        fields = [half.astype(F32) for v in values for half in halves(v)]
-        fields += [corner_ref[a, side : side + 1, here].astype(F32) for side in range(2) for a in range(3)]
-        top = COLS + q * ELEM_FIELDS
-        send_ref[top : top + ELEM_FIELDS, :] = jnp.concatenate(fields, axis=0).astype(BF16)
-
-
-def route_kernel(
-    cov_hbm, slot_hbm, w1_hbm, b1_hbm, w2_hbm, b2_ref,
-    out_ref,
-    cov_ref, slot_ref, w1_ref, b1_ref, w2_ref, hot_ref, rank_ref, val_ref, par_ref, sem,
-):
-    copies = start_all(
-        ((slot_hbm, slot_ref), (w1_hbm, w1_ref), (b1_hbm, b1_ref), (w2_hbm, w2_ref), (cov_hbm, cov_ref)), sem
-    )
+    meta = pltpu.roll(meta_ref[...], lax.axis_index("sub") * TILE_DEV, 1).astype(BF16)
+    send_ref[META:, :] = jnp.concatenate([meta, jnp.zeros((16, 3 * BLK), BF16)], axis=1)
     slab_iota = lax.broadcasted_iota(jnp.int32, (BLK, BLK), 0)
     lane_iota = lax.broadcasted_iota(jnp.int32, (BLK, BLK), 1)
     earlier = jnp.concatenate(
@@ -103,7 +97,24 @@
             hot.astype(F32) * (counts[:, :BLK] + seen), axis=0, keepdims=True
         )
         seen = seen + counts[:, BLK:]
-    for c in copies[1:]:
+    for c in copies[1:5]:
+        c.wait()
+    for group in range(4):
+        for f in range(4):
+            field = 4 * group + f
+            if field < 10:
+                v = field // 2
+                row = area_ref[...] if v == 4 else grad_ref[v // 2, v % 2 : v % 2 + 1, :]
+                part = halves(row)[field % 2].astype(F32)
+            else:
+                a, side = (field - 10) % 3, (field - 10) // 3
+                part = corner_ref[a, side : side + 1, :].astype(F32)
+            top = ELEMS + group * TILE_DEV
+            send_ref[top : top + TILE_DEV, lanes(f)] = jnp.concatenate(
+                [part[:, lanes(k)] for k in range(TILE_DEV)], axis=0
+            ).astype(BF16)
+    outs = start_all([(send_ref.at[ROUTED:], out_hbm.at[i, ROUTED:]) for i in range(SUBS)], out_sem)
+    for c in copies[5:]:
         c.wait()
     rows = 256
     for part in range(cov_ref.shape[0] // rows):
@@ -123,54 +134,52 @@
         val_ref[:, lanes(chunk)] = jnp.concatenate(
             [jnp.where(mine, v, 0.0).astype(BF16) for v in values], axis=0
         )
-    out_ref[...] = lax.dot_general(hot_ref[...], val_ref[...], NT, preferred_element_type=F32)
-
-
-def list_kernel(
-    s0_hbm, s1_hbm, s2_hbm, s3_hbm,
-    tid_ref, geo_ref, pos_ref, info_ref,
-    all_ref, raw_ref, ints_ref, meta_ref, sem, meta_sem,
-):
+    routed = lax.dot_general(hot_ref[...], val_ref[...], NT, preferred_element_type=F32).astype(BF16)
+    for j in range(4):
+        send_ref[0:ROUTED, lanes(j)] = routed[j * ROUTED : (j + 1) * ROUTED]
+    outs += [pltpu.make_async_copy(send_ref.at[:ROUTED], out_hbm.at[i, :ROUTED], out_sem.at[SUBS + i]) for i in range(SUBS)]
+    for c in outs[SUBS:]:
+        c.start()
+    for c in outs:
+        c.wait()
+
+
+def list_kernel(all_ref, tid_ref, geo_ref, pos_ref, info_ref):
     me = lax.axis_index("sub")
     base = (lax.axis_index("slab") - 1) * (SUBS * BLK_DEV)
-    copies = start_all([(s, all_ref.at[i]) for i, s in enumerate((s0_hbm, s1_hbm, s2_hbm, s3_hbm))], sem)
-    tid_ref[...] = jnp.full(tid_ref.shape, -1.0, F32)
-    raw_ref[...] = jnp.zeros(raw_ref.shape, F32)
-    for n in range(SLOTS):
-        info_ref[0, n] = 0
-        info_ref[1, n] = SUBS * BLK_DEV
-    for c in copies:
-        c.wait()
-    for v in range(SUBS):
-        coded = all_ref[v, META : META + 16, 0:BLK].astype(F32)
-        for i in range(2):
-            whole = coded[2 * i : 2 * i + 1] * 16.0 + coded[2 * i + 1 : 2 * i + 2]
-            ints_ref[4 * i + v : 4 * i + v + 1, :] = whole.astype(jnp.int32)
-    copy = pltpu.make_async_copy(ints_ref, meta_ref, meta_sem.at[0])
-    copy.start()
-    copy.wait()
-
-    def find(t, n):
-        v, k = t // TILE_DEV, t % TILE_DEV
-        row = meta_ref[v, k]
-        owned = (row // BLK_DEV) % SUBS == me
-
-        @pl.when(owned)
-        def _():
-            tile = (me - v) % SUBS * TILE_DEV + k
-            col = meta_ref[4 + v, k] - base
-            step, s, blk = col // (SUBS * BLK_DEV), col // BLK_DEV % SUBS, col % BLK_DEV
-            info_ref[0, n] = row % BLK_DEV
-            info_ref[1, n] = (step * SUBS + (me - s) % SUBS) * BLK_DEV + blk
-            tid_ref[pl.ds(n, 1), :] = jnp.full((1, BLK), tile, jnp.int32).astype(F32)
-            top = pl.ds(pl.multiple_of(COLS + (k // 4) * ELEM_FIELDS, 16), ELEM_FIELDS)
-            here = pl.ds(pl.multiple_of((k % 4) * BLK, BLK), BLK)
-            raw_ref[pl.ds(n, 1)] = all_ref[v, top, here].astype(F32)[None]
-
-        return n + owned.astype(jnp.int32)
-
-    info_ref[0, SLOTS] = lax.fori_loop(0, TILES_SLAB, find, jnp.int32(0))
-    field = [raw_ref[:, f, :] for f in range(ELEM_FIELDS)]
+    coded = all_ref[0, META:, 0:BLK].astype(F32)
+    for u in range(1, SUBS):
+        coded = coded + all_ref[u, META:, 0:BLK].astype(F32)
+    row = (coded[0:1] * 16.0 + coded[1:2]).astype(jnp.int32)
+    col = (coded[2:3] * 16.0 + coded[3:4]).astype(jnp.int32) - base
+    tile = lax.broadcasted_iota(jnp.int32, (1, BLK), 1)
+    mine = (((row >> 2) & 3) == me) & (tile < TILES_SLAB)
+    mine = jnp.where(mine, 1.0, 0.0)
+    earlier = jnp.where(
+        lax.broadcasted_iota(jnp.int32, (BLK, BLK), 0) < lax.broadcasted_iota(jnp.int32, (BLK, BLK), 1), 1.0, 0.0
+    )
+    rank = jnp.dot(
+        jnp.broadcast_to(mine, (16, BLK)).astype(BF16), earlier.astype(BF16), preferred_element_type=F32
+    )[0:1]
+    slot_iota = lax.broadcasted_iota(jnp.int32, (SLOTS, BLK), 0).astype(F32)
+    pick = jnp.where((slot_iota == rank) & (mine > 0.0), 1.0, 0.0)
+    tiles = jnp.sum(pick * tile.astype(F32), axis=1, keepdims=True)
+    used = jnp.sum(pick, axis=1, keepdims=True)
+    tid_ref[...] = jnp.broadcast_to(jnp.where(used > 0.0, tiles, -1.0), (SLOTS, BLK))
+    count = jnp.broadcast_to(jnp.sum(mine, axis=1, keepdims=True), (1, BLK))
+    pick = pick.astype(BF16)
+    facts = jnp.concatenate(
+        [(row & 3).astype(F32), jnp.clip(col, 0, 47).astype(F32), jnp.zeros((14, BLK), F32)], axis=0
+    ).astype(BF16)
+    wide = jnp.concatenate([pick, jnp.zeros((BLK - SLOTS, BLK), BF16)], axis=0)
+    facts = lax.dot_general(facts, wide, NT, preferred_element_type=F32)
+    info_ref[...] = jnp.concatenate([facts[0:2], count, jnp.zeros((5, BLK), F32)], axis=0).astype(jnp.int32)
+    field = []
+    for group in range(4):
+        here = slice(ELEMS + group * TILE_DEV, ELEMS + (group + 1) * TILE_DEV)
+        stacked = jnp.concatenate([all_ref[u, here, :] for u in range(SUBS)], axis=0)
+        got = jnp.dot(pick[:, :TILES_SLAB], stacked, preferred_element_type=F32)
+        field += [got[:, lanes(f)] for f in range(4)]
     value = [field[2 * i] + field[2 * i + 1] for i in range(5)]
     grad_x = [value[0], value[1], -(value[0] + value[1])]
     grad_y = [value[2], value[3], -(value[2] + value[3])]
@@ -188,7 +197,7 @@
     tiles = tid_ref[...].astype(BF16)
     found = jnp.zeros((6 * SLOTS, BLK), F32)
     for u in range(SUBS):
-        turned_ref[...] = got_ref[u].astype(F32).T
+        turned_ref[...] = got_ref[lanes(u), :].astype(F32).T
         for k in range(RANKS):
             rows = [
                 jnp.broadcast_to(turned_ref[f * RANKS + k : f * RANKS + k + 1, :], (16, BLK)).astype(BF16)
@@ -253,86 +262,62 @@
             acc_ref[block] = acc_ref[block] + done[i]
         return carry
 
-    lax.fori_loop(0, (info_ref[0, SLOTS] + UNROLL - 1) // UNROLL, add, jnp.int32(0))
+    lax.fori_loop(0, (info_ref[2, 0] + UNROLL - 1) // UNROLL, add, jnp.int32(0))
     for block in range(BLK_DEV):
         out_ref[:, lanes(block)] = acc_ref[block]
 
 
-def shared(block):
-    copies = jnp.broadcast_to(block[None], (SUBS, *block.shape))
-    return lax.all_to_all(copies, "sub", split_axis=0, concat_axis=0, tiled=True)
-
-
-def route(covariates, partition_slot, in_weight, in_bias, out_weight, out_bias):
-    elements = partition_slot.shape[1]
+def front(covariates, partition_slot, in_weight, in_bias, out_weight, out_bias, gradients, areas, corners, tile_rows, tile_cols, probe):
+    elements = areas.shape[0]
     vm = pltpu.VMEM
     return call(
-        route_kernel,
-        jax.ShapeDtypeStruct((BLK, BLK), F32),
-        [HBM] * 5 + [SMEM],
-        VMEM,
+        front_kernel,
+        jax.ShapeDtypeStruct((SUBS, SEND_ROWS, probe.shape[1]), BF16),
+        [HBM] * 5 + [SMEM] + [HBM] * 3 + [VMEM] * 2 + [HBM],
+        HBM,
         [
             vm(covariates.shape, BF16),
             vm(partition_slot.shape, jnp.int32),
             vm(in_weight.shape, BF16),
             vm((1, in_bias.shape[0]), F32),
             vm(out_weight.shape, BF16),
+            vm(gradients.shape, F32),
+            vm((1, elements), F32),
+            vm((3, 2, elements), jnp.int32),
+            vm((16, BLK), F32),
             vm((BLK, elements), BF16),
             vm((1, elements), F32),
             vm((BLK, elements), BF16),
             vm((3, elements), F32),
-            pltpu.SemaphoreType.DMA((5,)),
+            vm((SEND_ROWS, probe.shape[1]), BF16),
+            pltpu.SemaphoreType.DMA((9,)),
+            pltpu.SemaphoreType.DMA((2 * SUBS,)),
         ],
         400_000_000,
         1_000_000,
         60,
-    )(covariates, partition_slot, in_weight, in_bias[None], out_weight, out_bias)
-
-
-def pack(gradients, areas, corners, tile_rows, tile_cols, probe):
-    vm = pltpu.VMEM
-    return call(
-        pack_kernel,
-        jax.ShapeDtypeStruct((SEND_ROWS, probe.shape[1]), BF16),
-        [HBM] * 3 + [VMEM] * 2 + [HBM],
-        VMEM,
-        [
-            vm(gradients.shape, F32),
-            vm((1, areas.shape[0]), F32),
-            vm((3, 2, areas.shape[0]), jnp.int32),
-            vm((16, probe.shape[1]), F32),
-            pltpu.SemaphoreType.DMA((4,)),
-        ],
-        1_000_000,
-        1_000_000,
-        60,
-    )(gradients, areas[None], corners.transpose(1, 0, 2), tile_rows[None], tile_cols[None], probe)
-
-
-def listed(sends):
+    )(
+        covariates, partition_slot, in_weight, in_bias[None], out_weight, out_bias,
+        gradients, areas[None], corners.transpose(1, 0, 2), tile_rows[None], tile_cols[None], probe,
+    )
+
+
+def listed(everything):
     sds = jax.ShapeDtypeStruct
-    vm = pltpu.VMEM
     return call(
         list_kernel,
         (
             sds((SLOTS, BLK), F32),
             sds((13, SLOTS, BLK), F32),
             sds((6, SLOTS, BLK), jnp.int32),
-            sds((2, SLOTS + 1), jnp.int32),
+            sds((8, BLK), jnp.int32),
         ),
-        [ANY] * 4,
-        (VMEM, VMEM, VMEM, SMEM),
-        [
-            vm((SUBS, *sends[0].shape), BF16),
-            vm((SLOTS, ELEM_FIELDS, BLK), F32),
-            vm((8, BLK), jnp.int32),
-            pltpu.SMEM((8, BLK), jnp.int32),
-            pltpu.SemaphoreType.DMA((4,)),
-            pltpu.SemaphoreType.DMA((1,)),
-        ],
+        [VMEM],
+        (VMEM,) * 4,
+        (),
         10_000_000,
         1_000_000,
-    )(*sends)
+    )(everything)
 
 
 def matrices(got, tid, geo):
@@ -384,17 +369,21 @@
     probe,
 ):
     slabs = lax.axis_size("slab")
-    routed = route(covariates, partition_slot, in_weight, in_bias, out_weight, out_bias)
-    arrived = lax.all_to_all(routed, "slab", split_axis=0, concat_axis=0, tiled=True)
-    send = pack(gradients, areas, corners, tile_rows, tile_cols, probe)
-    sends = [send] + [lax.ppermute(send, "sub", [(i, (i + k) % SUBS) for i in range(SUBS)]) for k in (1, 2, 3)]
-    got = shared(arrived.astype(BF16))
-    own = jnp.stack([s[:COLS] for s in sends])
+    send = front(
+        covariates, partition_slot, in_weight, in_bias, out_weight, out_bias,
+        gradients, areas, corners, tile_rows, tile_cols, probe,
+    )
+    everything = lax.all_to_all(send, "sub", split_axis=0, concat_axis=0, tiled=True)
+    routed = everything[:, :ROUTED].reshape(SUBS, ROUTED, 4, BLK).transpose(2, 1, 0, 3)
+    routed = routed.reshape(4 * ROUTED, SUBS, BLK)
+    got = lax.all_to_all(routed, "slab", split_axis=0, concat_axis=0, tiled=True)
+    own = everything[:, ROUTED:ELEMS]
     up = [(i, i + 1) for i in range(slabs - 1)]
     before = lax.ppermute(own, "slab", up)
     after = lax.ppermute(own, "slab", [(j, i) for i, j in up])
-    tid, geo, pos, info = listed(sends)
-    return applied(info, matrices(got, tid, geo), pos, before, own, after)
+    tid, geo, pos, info = listed(everything)
+    k = matrices(got.reshape(-1, BLK), tid, geo)
+    return applied(info, k, pos, before, own, after)
 
 
 def solution(mesh):

time: 70.3 us -> 65.2 us (0.927)
  the two profiles are of different devices: /device:TPU:2 before, /device:TPU:32 now
where the time goes in v4:
time: 65.2 us; the launch traced here: 64.8 us
  starting transfers between devices  23.5 us (36%)
  blocking collectives  15.9 us (24%)
  waiting for transfers between devices  13.1 us (20%)
  Pallas kernels  11.5 us (18%)
  local copies, waits for them, and re-layouts  0.8 us (1%)
    all_to_all x1, starting transfers between devices, local(): lax.all_to_all(routed, 'slab', split_axis=0, concat_axis=0, tiled=True)  19.2 us
    all_to_all x1, blocking collectives, local(): lax.all_to_all(send, 'sub', split_axis=0, concat_axis=0, tiled=True)  15.9 us
    all_to_all x1, waiting for transfers between devices, local(): lax.all_to_all(routed, 'slab', split_axis=0, concat_axis=0, tiled=True)  13.1 us
    pallas_call x1, Pallas kernels, front(): call(front_kernel, jax.ShapeDtypeStruct((SUBS, SEND_ROWS, probe.shape[1])...  5.2 us
    pallas_call x1, Pallas kernels, applied(): call(apply_kernel, jax.ShapeDtypeStruct((COLS, own.shape[2]), F32), [SMEM...  4.09 us
    ppermute x1, starting transfers between devices, local(): before = lax.ppermute(own, 'slab', up)  2.3 us
    ppermute x1, starting transfers between devices, local(): after = lax.ppermute(own, 'slab', [(j, i) for i, j in up])  2.02 us
    pallas_call x1, Pallas kernels, matrices(): call(matrix_kernel, jax.ShapeDtypeStruct((6, SLOTS, BLK), F32), [VMEM] *...  1.9 us
  transfers between devices with their start and end apart: 3, of which 1 were waited for; matrix products, arithmetic and copies ran while one was open for 0% of the time, Pallas kernels for 3%

profile of v4, /device:TPU:32, one launch (start us, length us, event | category | flops | bytes accessed | tf_op | source)
XLA Modules:
  0.0 64.8 jit_solution(7578948648510626149)
XLA Ops:
  0.0 5.2 %shard_map.118 = bf16[4,176,512]{2,1,0:T(8,128)(2,1)} custom-call(bf16[2048,128]{1,0:T(8,128)(2,1)} %cov_hbm.1, s32[2,2048]{1,0:T(2,128)} %slot_hbm.1, bf16[128,256]{1,0:T(8,128)(2,1)} %w1_hbm.1, f32[1,256]{1,0:T(1,128)} %bitcast.18, bf16[3,256]{1,0:T(4,128)(2,1)} %w2_hbm.1, f32[3]{0:T(128)} %b2_ref.1, f32[2,2,2048]{2,1,0:T(2,128)} %grad_hbm.1, ...), custom_call_target="tpu_custom_call" | custom-call | flops 400000000 | bytes 1000000 | tf_op jit(solution)/shard_map/pallas_call | solution.py:273
  5.2 15.9 %all_to_all.10.all_ref = bf16[4,176,512]{2,1,0:T(8,128)(2,1)S(1)} all-to-all(bf16[4,176,512]{2,1,0:T(8,128)(2,1)} %shard_map.118), channel_id=1, replica_groups=mesh['slab'=128,'sub'=4] {'sub'}, dimensions={0} | all-to-all | bytes 1441792 | tf_op jit(solution)/shard_map/all_to_all | solution.py:376
  21.1 0.8 %copy.16 = bf16[128,4,128]{2,1,0:T(4,128)(2,1)} copy(bf16[128,4,128]{2,0,1:T(8,128)(2,1)S(1)} %bitcast.15) | data formatting | bytes 262144 | tf_op jit(solution)/shard_map/reshape | solution.py:378
  21.9 19.2 %all-to-all-start.1 = ((bf16[128,4,128]{2,1,0:T(4,128)(2,1)}), bf16[128,4,128]{2,1,0:T(4,128)(2,1)S(1)}, u32[]{:S(2)}, u32[]{:S(2)}) async-start(bf16[128,4,128]{2,1,0:T(4,128)(2,1)} %copy.16), calls=%async_computation.1 | async-start | bytes 262144 | tf_op jit(solution)/shard_map/all_to_all | solution.py:379
  41.1 2.0 %collective-permute-start.1 = (bf16[4,64,512]{2,1,0:T(8,128)(2,1)S(1)}, bf16[4,64,512]{2,1,0:T(8,128)(2,1)S(1)}, u32[]{:S(2)}, u32[]{:S(2)}) collective-permute-start(bf16[4,64,512]{2,1,0:T(8,128)(2,1)S(1)} %slice.9.own_hbm), channel_id=1, source_target_pairs={{4,0},{8,4},{12,8},{16,12},{20,16},{24,20},{28,24},{32,28},{36,32}... | collective-permute-start | bytes 786440 | tf_op jit(solution)/shard_map/ppermute | solution.py:383
  43.1 2.3 %collective-permute-start = (bf16[4,64,512]{2,1,0:T(8,128)(2,1)S(1)}, bf16[4,64,512]{2,1,0:T(8,128)(2,1)S(1)}, u32[]{:S(2)}, u32[]{:S(2)}) collective-permute-start(bf16[4,64,512]{2,1,0:T(8,128)(2,1)S(1)} %slice.9.own_hbm), channel_id=1, source_target_pairs={{0,4},{4,8},{8,12},{12,16},{16,20},{20,24},{24,28},{28,32},{32,36}... | collective-permute-start | bytes 786440 | tf_op jit(solution)/shard_map/ppermute | solution.py:382
  45.4 0.3 shard_map.119
  45.7 13.1 %all-to-all-done.1 = bf16[128,4,128]{2,1,0:T(4,128)(2,1)S(1)} async-done(((bf16[128,4,128]{2,1,0:T(4,128)(2,1)}), bf16[128,4,128]{2,1,0:T(4,128)(2,1)S(1)}, u32[]{:S(2)}, u32[]{:S(2)}) %all-to-all-start.1) | async-done | bytes 131104 | tf_op jit(solution)/shard_map/all_to_all | solution.py:379
  58.8 1.9 %shard_map.120.k_ref = f32[6,32,128]{2,1,0:T(8,128)S(1)} custom-call(bf16[512,128]{1,0:T(8,128)(2,1)S(1)} %bitcast.14, f32[32,128]{1,0:T(8,128)S(1)} %get-tuple-element.10.tid_ref, f32[13,32,128]{2,1,0:T(8,128)S(1)} %get-tuple-element.11.geo_ref), custom_call_target="tpu_custom_call" | custom-call | flops 1000000000 | bytes 3000000 | tf_op jit(solution)/shard_map/pallas_call | solution.py:325
  60.7 0.0 collective-permute-done.1.after_hbm
  60.7 0.0 collective-permute-done.before_hbm
  60.7 4.1 %shard_map.121 = f32[64,512]{1,0:T(8,128)} custom-call(s32[8,128]{1,0:T(8,128)S(1)} %get-tuple-element.9.info_ref, f32[6,32,128]{2,1,0:T(8,128)S(1)} %shard_map.120.k_ref, s32[6,32,128]{2,1,0:T(8,128)S(1)} %get-tuple-element.12.pos_ref, bf16[4,64,512]{2,1,0:T(8,128)(2,1)S(1)} %collective-permute-done.before_hbm, bf16[4,64,512]{2,1,0:T(8,128)(2,1)S(1)} %slice.9.own_hbm, ...), custom_call_target="tpu_custom_call" | custom-call | flops 1000000000 | bytes 3000000 | tf_op jit(solution)/shard_map/pallas_call | solution.py:342
  (2 shorter events, 0.0 us)
Async XLA Ops:
  21.9 36.9 %all-to-all-start.1 = ((bf16[128,4,128]{2,1,0:T(4,128)(2,1)}), bf16[128,4,128]{2,1,0:T(4,128)(2,1)S(1)}, u32[]{:S(2)}, u32[]{:S(2)}) async-start(bf16[128,4,128]{2,1,0:T(4,128)(2,1)} %copy.16), calls=%async_computation.1 | async-start | bytes 262144 | tf_op jit(solution)/shard_map/all_to_all | solution.py:379
  41.1 19.6 %collective-permute-start.1 = (bf16[4,64,512]{2,1,0:T(8,128)(2,1)S(1)}, bf16[4,64,512]{2,1,0:T(8,128)(2,1)S(1)}, u32[]{:S(2)}, u32[]{:S(2)}) collective-permute-start(bf16[4,64,512]{2,1,0:T(8,128)(2,1)S(1)} %slice.9.own_hbm), channel_id=1, source_target_pairs={{4,0},{8,4},{12,8},{16,12},{20,16},{24,20},{28,24},{32,28},{36,32}... | collective-permute-start | bytes 786440 | tf_op jit(solution)/shard_map/ppermute | solution.py:383
  43.1 17.6 %collective-permute-start = (bf16[4,64,512]{2,1,0:T(8,128)(2,1)S(1)}, bf16[4,64,512]{2,1,0:T(8,128)(2,1)S(1)}, u32[]{:S(2)}, u32[]{:S(2)}) collective-permute-start(bf16[4,64,512]{2,1,0:T(8,128)(2,1)S(1)} %slice.9.own_hbm), channel_id=1, source_target_pairs={{0,4},{4,8},{8,12},{12,16},{16,20},{20,24},{24,28},{28,32},{32,36}... | collective-permute-start | bytes 786440 | tf_op jit(solution)/shard_map/ppermute | solution.py:382

commit v5 on v4

v5 whole, which is shorter than its diff:
```python
import jax
import jax.numpy as jnp
from jax import lax
from jax.experimental import pallas as pl
from jax.experimental.pallas import tpu as pltpu
from jax.sharding import PartitionSpec as P

BLK = 128
CHUNKS = 16
RANKS = 16
FIELDS = 8
SLOTS = 32
TILE_DEV = 16
SUBS = 4
BLK_DEV = 4
COLS = 64
PAIRS = ((0, 0), (0, 1), (0, 2), (1, 1), (1, 2), (2, 2))
PAIR_OF = {(a, b): PAIRS.index((min(a, b), max(a, b))) for a in range(3) for b in range(3)}
NT = (((1,), (1,)), ((), ()))
VMEM = pl.BlockSpec(memory_space=pltpu.VMEM)
SMEM = pl.BlockSpec(memory_space=pltpu.SMEM)
F32 = jnp.float32
BF16 = jnp.bfloat16
HBM = pl.BlockSpec(memory_space=pltpu.HBM)
ANY = pl.BlockSpec(memory_space=pl.ANY)
OWNED = 8
ELEM_FIELDS = 18
PROBE = BLK
ELEMS = PROBE + BLK_DEV * COLS
SEND_ROWS = ELEMS + ELEM_FIELDS * OWNED
UNROLL = 4


def call(kernel, out_shape, in_specs, out_specs, scratch, flops, nbytes, vmem=40):
    return pl.pallas_call(
        kernel,
        out_shape=out_shape,
        in_specs=in_specs,
        out_specs=out_specs,
        scratch_shapes=scratch,
        compiler_params=pltpu.CompilerParams(vmem_limit_bytes=vmem * 1024 * 1024),
        cost_estimate=pl.CostEstimate(flops=flops, bytes_accessed=nbytes, transcendentals=0),
    )


def lanes(chunk):
    return slice(chunk * BLK, (chunk + 1) * BLK)


def halves(x):
    high = x.astype(BF16)
    return high, (x - high.astype(F32)).astype(BF16)


def start_all(pairs, sem):
    copies = [pltpu.make_async_copy(s, d, sem.at[i]) for i, (s, d) in enumerate(pairs)]
    for c in copies:
        c.start()
    return copies


def front_kernel(
    cov_hbm, slot_hbm, w1_hbm, b1_hbm, w2_hbm, b2_ref, grad_hbm, area_hbm, corner_hbm, rows_ref, cols_ref, probe_hbm,
    out_hbm,
    cov_ref, slot_ref, w1_ref, b1_ref, w2_ref, grad_ref, area_ref, corner_ref, tile_ref,
    hot_ref, rank_ref, val_ref, par_ref, send_ref, elem_ref, sem, out_sem,
):
    copies = start_all(
        (
            (slot_hbm, slot_ref), (grad_hbm, grad_ref), (area_hbm, area_ref), (corner_hbm, corner_ref),
            (w1_hbm, w1_ref), (b1_hbm, b1_ref), (w2_hbm, w2_ref), (cov_hbm, cov_ref),
            *(
                (probe_hbm.at[:, lanes(b)], send_ref.at[PROBE + b * COLS : PROBE + (b + 1) * COLS])
                for b in range(BLK_DEV)
            ),
        ),
        sem,
    )
    slab_iota = lax.broadcasted_iota(jnp.int32, (BLK, BLK), 0)
    lane_iota = lax.broadcasted_iota(jnp.int32, (BLK, BLK), 1)
    before = jnp.where(slab_iota < lane_iota, 1.0, 0.0).astype(BF16)
    earlier = jnp.concatenate([before, jnp.ones((BLK, BLK), BF16)], axis=1)
    tile_ref[...] = jnp.full(tile_ref.shape, -1.0, F32)
    tile_ref[0:1, 0:TILE_DEV] = rows_ref[...].astype(F32)
    tile_ref[1:2, 0:TILE_DEV] = cols_ref[...].astype(F32)
    row = tile_ref[0:1, :].astype(jnp.int32)
    col = tile_ref[1:2, :].astype(jnp.int32)
    real = lane_iota[0:1] < TILE_DEV
    owner = (row >> 2) & (SUBS - 1)
    mine = jnp.concatenate(
        [jnp.where(real & (owner == d), 1.0, 0.0) for d in range(SUBS)] + [jnp.zeros((12, BLK), F32)], axis=0
    )
    place = jnp.dot(mine.astype(BF16), before, preferred_element_type=F32)
    slot_iota = slab_iota[0:OWNED].astype(F32)
    pick = jnp.concatenate(
        [
            jnp.where((slot_iota == place[d : d + 1]) & (mine[d : d + 1] > 0.0), 1.0, 0.0)
            for d in range(SUBS)
        ],
        axis=0,
    ).astype(BF16)[:, :TILE_DEV]
    facts = [
        (lane_iota[0:1] + (lax.axis_index("sub") * TILE_DEV + 1)).astype(F32),
        (row & (BLK_DEV - 1)).astype(F32),
        (col >> 4).astype(F32),
        (col & 15).astype(F32),
    ]
    facts = jnp.concatenate([jnp.where(real, f, 0.0) for f in facts] + [jnp.zeros((BLK - 4, BLK), F32)], axis=0).T
    copies[0].wait()
    for chunk in range(CHUNKS):
        slab = slot_ref[0:1, lanes(chunk)] >> 2
        hot_ref[:, lanes(chunk)] = jnp.where(slab_iota == slab, 1.0, 0.0).astype(BF16)
    seen = jnp.zeros((BLK, BLK), F32)
    for chunk in range(CHUNKS):
        hot = hot_ref[:, lanes(chunk)]
        counts = jnp.dot(hot, earlier, preferred_element_type=F32)
        rank_ref[:, lanes(chunk)] = jnp.sum(
            hot.astype(F32) * (counts[:, :BLK] + seen), axis=0, keepdims=True
        )
        seen = seen + counts[:, BLK:]
    for c in copies[1:4]:
        c.wait()
    fields = []
    for v in range(5):
        value = area_ref[...] if v == 4 else grad_ref[v // 2, v % 2 : v % 2 + 1, :]
        fields += [half.astype(F32) for half in halves(value)]
    for side in range(2):
        for a in range(3):
            fields.append(corner_ref[a, side : side + 1, :].astype(F32))
    fields = [jnp.concatenate([f[:, lanes(k)] for k in range(TILE_DEV)], axis=0) for f in fields]
    fields += [facts[:TILE_DEV], jnp.zeros((TILE_DEV, BLK), F32)]
    picked = jnp.dot(pick, jnp.concatenate(fields, axis=1).astype(BF16), preferred_element_type=F32)
    for d in range(SUBS):
        elem_ref[d] = jnp.concatenate(
            [picked[d * OWNED : (d + 1) * OWNED, lanes(f)] for f in range(ELEM_FIELDS)], axis=0
        ).astype(BF16)
    for c in copies[8:]:
        c.wait()
    outs = start_all(
        [(send_ref.at[PROBE:], out_hbm.at[d, PROBE:ELEMS]) for d in range(SUBS)]
        + [(elem_ref.at[d], out_hbm.at[d, ELEMS:]) for d in range(SUBS)],
        out_sem,
    )
    for c in copies[4:8]:
        c.wait()
    rows = 256
    for part in range(cov_ref.shape[0] // rows):
        here = slice(part * rows, (part + 1) * rows)
        pre_act = jnp.dot(cov_ref[here, :], w1_ref[...], preferred_element_type=F32) + b1_ref[...]
        hidden = jax.nn.gelu(pre_act, approximate=True).astype(BF16)
        par_ref[:, here] = lax.dot_general(w2_ref[...], hidden, NT, preferred_element_type=F32)
    rank_iota = lax.broadcasted_iota(jnp.int32, (RANKS, BLK), 0).astype(F32)
    for chunk in range(CHUNKS):
        device = slot_ref[0:1, lanes(chunk)]
        place = slot_ref[1:2, lanes(chunk)]
        values = []
        for f in range(3):
            values += [half.astype(F32) for half in halves(par_ref[f : f + 1, lanes(chunk)] + b2_ref[f])]
        values += [((device & 3) * TILE_DEV + (place >> 7)).astype(F32), (place & 127).astype(F32)]
        ranked = rank_iota == rank_ref[:, lanes(chunk)]
        val_ref[:, lanes(chunk)] = jnp.concatenate(
            [jnp.where(ranked, v, 0.0).astype(BF16) for v in values], axis=0
        )
    send_ref[0:PROBE, :] = lax.dot_general(
        hot_ref[...], val_ref[...], NT, preferred_element_type=F32
    ).astype(BF16)
    last = [
        pltpu.make_async_copy(send_ref.at[:PROBE], out_hbm.at[d, :PROBE], out_sem.at[2 * SUBS + d])
        for d in range(SUBS)
    ]
    for c in last:
        c.start()
    for c in outs + last:
        c.wait()


def list_kernel(all_ref, tid_ref, geo_ref, pos_ref, info_ref):
    base = (lax.axis_index("slab") - 1) * (SUBS * BLK_DEV)
    sent = [all_ref[u, ELEMS:, :].astype(F32) for u in range(SUBS)]
    field = [
        jnp.concatenate([e[f * OWNED : (f + 1) * OWNED] for e in sent], axis=0) for f in range(ELEM_FIELDS - 1)
    ]
    facts = jnp.concatenate([field[16], jnp.zeros((BLK - SLOTS, BLK), F32)], axis=0)
    tid_ref[...] = jnp.broadcast_to(facts[:SLOTS, 0:1] - 1.0, (SLOTS, BLK))
    facts = facts.T
    col = (facts[2:3] * 16.0 + facts[3:4]).astype(jnp.int32) - base
    col = jnp.where(facts[0:1] > 0.0, col, SUBS * BLK_DEV)
    info_ref[...] = jnp.concatenate(
        [facts[1:2].astype(jnp.int32), col, jnp.zeros((6, BLK), jnp.int32)], axis=0
    )
    value = [field[2 * i] + field[2 * i + 1] for i in range(5)]
    grad_x = [value[0], value[1], -(value[0] + value[1])]
    grad_y = [value[2], value[3], -(value[2] + value[3])]
    for i, (a, b) in enumerate(PAIRS):
        geo_ref[i] = grad_x[a] * grad_x[b] + grad_y[a] * grad_y[b]
        geo_ref[6 + i] = grad_x[a] * grad_y[b] + grad_y[a] * grad_x[b]
    geo_ref[12] = value[4]
    for a in range(6):
        pos_ref[a] = field[10 + a].astype(jnp.int32)


def finish_kernel(
    info_ref, got_ref, tid_ref, geo_ref, pos_ref, before_hbm, own_hbm, after_hbm,
    out_ref, hot_ref, val_ref, turned_ref, k_ref, x_ref, acc_ref, sem,
):
    blocks = SUBS * BLK_DEV
    copies = start_all(
        [(src, x_ref.at[blocks * i : blocks * (i + 1)]) for i, src in enumerate((before_hbm, own_hbm, after_hbm))], sem
    )
    lane_iota = lax.broadcasted_iota(jnp.int32, (BLK, BLK), 0).astype(F32).astype(BF16)
    one, zero = jnp.ones((), BF16), jnp.zeros((), BF16)
    tiles = tid_ref[...].astype(BF16)
    found = jnp.zeros((6 * SLOTS, BLK), F32)
    for u in range(SUBS):
        turned_ref[...] = got_ref[lanes(u), :].astype(F32).T
        for k in range(RANKS):
            rows = [
                jnp.broadcast_to(turned_ref[f * RANKS + k : f * RANKS + k + 1, :], (16, BLK)).astype(BF16)
                for f in range(FIELDS)
            ]
            twice = [jnp.concatenate([r, r], axis=0) for r in rows[:7]]
            mine = tiles == twice[6]
            val_ref[:, lanes(k)] = jnp.concatenate([jnp.where(mine, twice[f], zero) for f in range(6)], axis=0)
            hot_ref[:, lanes(k)] = jnp.where(lane_iota == jnp.concatenate([rows[7]] * 8, axis=0), one, zero)
        found = found + lax.dot_general(val_ref[...], hot_ref[...], NT, preferred_element_type=F32)
    params = [
        found[2 * f * SLOTS : (2 * f + 1) * SLOTS] + found[(2 * f + 1) * SLOTS : (2 * f + 2) * SLOTS]
        for f in range(3)
    ]
    kappa_sq = jnp.exp(params[0])
    scale = jnp.exp(params[1])
    coupling = 0.9 * jnp.tanh(params[2])
    area = geo_ref[12]
    for i, (a, b) in enumerate(PAIRS):
        mass = kappa_sq * (2.0 if a == b else 1.0)
        stiffness = scale * (geo_ref[i] + coupling * geo_ref[6 + i])
        k_ref[i] = (area * (stiffness + mass)).astype(BF16).astype(F32)
    acc_ref[...] = jnp.zeros(acc_ref.shape, F32)
    for c in copies:
        c.wait()

    def tile_part(n):
        x = x_ref[info_ref[1, n]].astype(F32)
        k = [k_ref[i, pl.ds(n, 1), :] for i in range(6)]
        xs = [
            jnp.take_along_axis(x, jnp.broadcast_to(pos_ref[3 + b, pl.ds(n, 1), :], (COLS, BLK)), axis=1)
            for b in range(3)
        ]
        ys = []
        hots = []
        for a in range(3):
            y = k[PAIR_OF[a, 0]] * xs[0] + k[PAIR_OF[a, 1]] * xs[1] + k[PAIR_OF[a, 2]] * xs[2]
            ys.append(y.astype(BF16))
            row = jnp.broadcast_to(pos_ref[a, pl.ds(n, 1), :].astype(F32), (16, BLK)).astype(BF16)
            hots.append(jnp.where(lane_iota == jnp.concatenate([row] * 8, axis=0), one, zero))
        return lax.dot_general(
            jnp.concatenate(ys, axis=1), jnp.concatenate(hots, axis=1), NT, preferred_element_type=F32
        )

    def add(group, carry):
        done = [tile_part(group * UNROLL + i) for i in range(UNROLL)]
        for i in range(UNROLL):
            block = info_ref[0, group * UNROLL + i]
            acc_ref[block] = acc_ref[block] + done[i]
        return carry

    lax.fori_loop(0, SLOTS // UNROLL, add, jnp.int32(0))
    for block in range(BLK_DEV):
        out_ref[:, lanes(block)] = acc_ref[block]


def front(covariates, partition_slot, in_weight, in_bias, out_weight, out_bias, gradients, areas, corners, tile_rows, tile_cols, probe):
    elements = areas.shape[0]
    vm = pltpu.VMEM
    return call(
        front_kernel,
        jax.ShapeDtypeStruct((SUBS, SEND_ROWS, BLK), BF16),
        [HBM] * 5 + [SMEM] + [HBM] * 3 + [VMEM] * 2 + [HBM],
        HBM,
        [
            vm(covariates.shape, BF16),
            vm(partition_slot.shape, jnp.int32),
            vm(in_weight.shape, BF16),
            vm((1, in_bias.shape[0]), F32),
            vm(out_weight.shape, BF16),
            vm(gradients.shape, F32),
            vm((1, elements), F32),
            vm((3, 2, elements), jnp.int32),
            vm((8, BLK), F32),
            vm((BLK, elements), BF16),
            vm((1, elements), F32),
            vm((BLK, elements), BF16),
            vm((3, elements), F32),
            vm((ELEMS, BLK), BF16),
            vm((SUBS, ELEM_FIELDS * OWNED, BLK), BF16),
            pltpu.SemaphoreType.DMA((8 + BLK_DEV,)),
            pltpu.SemaphoreType.DMA((3 * SUBS,)),
        ],
        400_000_000,
        1_000_000,
        60,
    )(
        covariates, partition_slot, in_weight, in_bias[None], out_weight, out_bias,
        gradients, areas[None], corners.transpose(1, 0, 2), tile_rows[None], tile_cols[None], probe,
    )


def listed(everything):
    sds = jax.ShapeDtypeStruct
    return call(
        list_kernel,
        (
            sds((SLOTS, BLK), F32),
            sds((13, SLOTS, BLK), F32),
            sds((6, SLOTS, BLK), jnp.int32),
            sds((8, BLK), jnp.int32),
        ),
        [VMEM],
        (VMEM,) * 4,
        (),
        10_000_000,
        1_000_000,
    )(everything)


def finished(info, got, tid, geo, pos, before, own, after):
    vm = pltpu.VMEM
    return call(
        finish_kernel,
        jax.ShapeDtypeStruct((COLS, BLK_DEV * BLK), F32),
        [SMEM] + [VMEM] * 4 + [ANY] * 3,
        VMEM,
        [
            vm((BLK, RANKS * BLK), BF16),
            vm((6 * SLOTS, RANKS * BLK), BF16),
            vm((BLK, BLK), F32),
            vm((6, SLOTS, BLK), F32),
            vm((3 * SUBS * BLK_DEV, COLS, BLK), BF16),
            vm((BLK_DEV, COLS, BLK), F32),
            pltpu.SemaphoreType.DMA((3,)),
        ],
        1_000_000_000,
        3_000_000,
    )(info, got, tid, geo, pos, before, own, after)


def local(
    covariates,
    partition_slot,
    in_weight,
    in_bias,
    out_weight,
    out_bias,
    gradients,
    areas,
    corners,
    tile_rows,
    tile_cols,
    probe,
):
    slabs = lax.axis_size("slab")
    send = front(
        covariates, partition_slot, in_weight, in_bias, out_weight, out_bias,
        gradients, areas, corners, tile_rows, tile_cols, probe,
    )
    everything = lax.all_to_all(send, "sub", split_axis=0, concat_axis=0, tiled=True)
    routed = everything[:, :PROBE].transpose(1, 0, 2)
    got = lax.all_to_all(routed, "slab", split_axis=0, concat_axis=0, tiled=True)
    own = everything[:, PROBE:ELEMS].reshape(SUBS * BLK_DEV, COLS, BLK)
    up = [(i, i + 1) for i in range(slabs - 1)]
    before = lax.ppermute(own, "slab", up)
    after = lax.ppermute(own, "slab", [(j, i) for i, j in up])
    tid, geo, pos, info = listed(everything)
    return finished(info, got.reshape(-1, BLK), tid, geo, pos, before, own, after)


def solution(mesh):
    placed = (
        P(("slab", "sub"), None),
        P(None, ("slab", "sub")),
        P(),
        P(),
        P(),
        P(),
        P(None, None, ("slab", "sub")),
        P(("slab", "sub")),
        P(None, None, ("slab", "sub")),
        P(("slab", "sub")),
        P(("slab", "sub")),
        P(None, ("slab", "sub")),
    )
    return jax.shard_map(
        local, mesh=mesh, in_specs=placed, out_specs=P(None, ("slab", "sub")), check_vma=False
    )
```

time: 65.2 us -> 63.6 us (0.975)
  the two profiles are of different devices: /device:TPU:32 before, /device:TPU:1 now
where the time goes in v5:
time: 63.6 us; the launch traced here: 63.3 us
  starting transfers between devices  28.2 us (44%)
  blocking collectives  11.9 us (19%)
  waiting for transfers between devices  11.7 us (18%)
  Pallas kernels  10.7 us (17%)
  local copies, waits for them, and re-layouts  0.79 us (1%)
    all_to_all x1, starting transfers between devices, local(): lax.all_to_all(routed, 'slab', split_axis=0, concat_axis=0, tiled=True)  22.7 us
    all_to_all x1, blocking collectives, local(): lax.all_to_all(send, 'sub', split_axis=0, concat_axis=0, tiled=True)  11.9 us
    all_to_all x1, waiting for transfers between devices, local(): lax.all_to_all(routed, 'slab', split_axis=0, concat_axis=0, tiled=True)  6.95 us
    pallas_call x1, Pallas kernels, finished(): call(finish_kernel, jax.ShapeDtypeStruct((COLS, BLK_DEV * BLK), F32), [SM...  5.91 us
    ppermute x1, waiting for transfers between devices, local(): after = lax.ppermute(own, 'slab', [(j, i) for i, j in up])  4.72 us
    pallas_call x1, Pallas kernels, front(): call(front_kernel, jax.ShapeDtypeStruct((SUBS, SEND_ROWS, BLK), BF16), [H...  4.65 us
    ppermute x1, starting transfers between devices, local(): after = lax.ppermute(own, 'slab', [(j, i) for i, j in up])  2.8 us
    ppermute x1, starting transfers between devices, local(): before = lax.ppermute(own, 'slab', up)  2.76 us
  transfers between devices with their start and end apart: 3, of which 2 were waited for; matrix products, arithmetic and copies ran while one was open for 0% of the time, Pallas kernels for 0%

profile of v5, /device:TPU:1, one launch (start us, length us, event | category | flops | bytes accessed | tf_op | source)
XLA Modules:
  0.0 63.3 jit_solution(10902684697347997408)
XLA Ops:
  0.0 4.6 %shard_map.118 = bf16[4,528,128]{2,1,0:T(8,128)(2,1)} custom-call(bf16[2048,128]{1,0:T(8,128)(2,1)} %cov_hbm.1, s32[2,2048]{1,0:T(2,128)} %slot_hbm.1, bf16[128,256]{1,0:T(8,128)(2,1)} %w1_hbm.1, f32[1,256]{1,0:T(1,128)} %bitcast.15, bf16[3,256]{1,0:T(4,128)(2,1)} %w2_hbm.1, f32[3]{0:T(128)} %b2_ref.1, f32[2,2,2048]{2,1,0:T(2,128)} %grad_hbm.1, ...), custom_call_target="tpu_custom_call" | custom-call | flops 400000000 | bytes 1000000 | tf_op jit(solution)/shard_map/pallas_call | solution.py:275
  4.7 11.9 %all_to_all.10.all_ref = bf16[4,528,128]{2,1,0:T(8,128)(2,1)S(1)} all-to-all(bf16[4,528,128]{2,1,0:T(8,128)(2,1)} %shard_map.118), channel_id=1, replica_groups=mesh['slab'=128,'sub'=4] {'sub'}, dimensions={0} | all-to-all | bytes 1081344 | tf_op jit(solution)/shard_map/all_to_all | solution.py:366
  16.5 0.8 %copy.14 = bf16[128,4,128]{2,1,0:T(4,128)(2,1)} copy(bf16[128,4,128]{2,0,1:T(8,128)(2,1)S(1)} %slice_bitcast_fusion) | data formatting | bytes 262144 | tf_op jit(solution)/shard_map/transpose | solution.py:367
  17.3 22.7 %all-to-all-start.1 = ((bf16[128,4,128]{2,1,0:T(4,128)(2,1)}), bf16[128,4,128]{2,1,0:T(4,128)(2,1)S(1)}, u32[]{:S(2)}, u32[]{:S(2)}) async-start(bf16[128,4,128]{2,1,0:T(4,128)(2,1)} %copy.14), calls=%async_computation.1 | async-start | bytes 262144 | tf_op jit(solution)/shard_map/all_to_all | solution.py:368
  40.0 2.8 %collective-permute-start.1 = (bf16[16,64,128]{2,1,0:T(8,128)(2,1)S(1)}, bf16[16,64,128]{2,1,0:T(8,128)(2,1)S(1)}, u32[]{:S(2)}, u32[]{:S(2)}) collective-permute-start(bf16[16,64,128]{2,1,0:T(8,128)(2,1)S(1)} %bitcast.9), channel_id=1, source_target_pairs={{4,0},{8,4},{12,8},{16,12},{20,16},{24,20},{28,24},{32,28},{36,32}... | collective-permute-start | bytes 786440 | tf_op jit(solution)/shard_map/ppermute | solution.py:372
  42.8 2.8 %collective-permute-start = (bf16[16,64,128]{2,1,0:T(8,128)(2,1)S(1)}, bf16[16,64,128]{2,1,0:T(8,128)(2,1)S(1)}, u32[]{:S(2)}, u32[]{:S(2)}) collective-permute-start(bf16[16,64,128]{2,1,0:T(8,128)(2,1)S(1)} %bitcast.10), channel_id=1, source_target_pairs={{0,4},{4,8},{8,12},{12,16},{16,20},{20,24},{24,28},{28,32},{32,36}... | collective-permute-start | bytes 786440 | tf_op jit(solution)/shard_map/ppermute | solution.py:371
  45.6 0.1 shard_map.119
  45.7 4.7 %collective-permute-done.1.after_hbm = bf16[16,64,128]{2,1,0:T(8,128)(2,1)S(1)} collective-permute-done((bf16[16,64,128]{2,1,0:T(8,128)(2,1)S(1)}, bf16[16,64,128]{2,1,0:T(8,128)(2,1)S(1)}, u32[]{:S(2)}, u32[]{:S(2)}) %collective-permute-start.1) | collective-permute-done | bytes 262176 | tf_op jit(solution)/shard_map/ppermute | solution.py:372
  50.4 0.0 collective-permute-done.before_hbm
  50.4 7.0 %all-to-all-done.1 = bf16[128,4,128]{2,1,0:T(4,128)(2,1)S(1)} async-done(((bf16[128,4,128]{2,1,0:T(4,128)(2,1)}), bf16[128,4,128]{2,1,0:T(4,128)(2,1)S(1)}, u32[]{:S(2)}, u32[]{:S(2)}) %all-to-all-start.1) | async-done | bytes 131104 | tf_op jit(solution)/shard_map/all_to_all | solution.py:368
  57.4 5.9 %shard_map.120 = f32[64,512]{1,0:T(8,128)} custom-call(s32[8,128]{1,0:T(8,128)S(1)} %get-tuple-element.9.info_ref, bf16[512,128]{1,0:T(8,128)(2,1)S(1)} %bitcast.12, f32[32,128]{1,0:T(8,128)S(1)} %get-tuple-element.10.tid_ref, f32[13,32,128]{2,1,0:T(8,128)S(1)} %get-tuple-element.11.geo_ref, s32[6,32,128]{2,1,0:T(8,128)S(1)} %get-tuple-element.12.pos_ref, ...), custom_call_target="tpu_custom_call" | custom-call | flops 1000000000 | bytes 3000000 | tf_op jit(solution)/shard_map/pallas_call | solution.py:328
  (2 shorter events, 0.0 us)
Async XLA Ops:
  17.3 40.1 %all-to-all-start.1 = ((bf16[128,4,128]{2,1,0:T(4,128)(2,1)}), bf16[128,4,128]{2,1,0:T(4,128)(2,1)S(1)}, u32[]{:S(2)}, u32[]{:S(2)}) async-start(bf16[128,4,128]{2,1,0:T(4,128)(2,1)} %copy.14), calls=%async_computation.1 | async-start | bytes 262144 | tf_op jit(solution)/shard_map/all_to_all | solution.py:368
  40.0 10.4 %collective-permute-start.1 = (bf16[16,64,128]{2,1,0:T(8,128)(2,1)S(1)}, bf16[16,64,128]{2,1,0:T(8,128)(2,1)S(1)}, u32[]{:S(2)}, u32[]{:S(2)}) collective-permute-start(bf16[16,64,128]{2,1,0:T(8,128)(2,1)S(1)} %bitcast.9), channel_id=1, source_target_pairs={{4,0},{8,4},{12,8},{16,12},{20,16},{24,20},{28,24},{32,28},{36,32}... | collective-permute-start | bytes 786440 | tf_op jit(solution)/shard_map/ppermute | solution.py:372
  42.8 7.6 %collective-permute-start = (bf16[16,64,128]{2,1,0:T(8,128)(2,1)S(1)}, bf16[16,64,128]{2,1,0:T(8,128)(2,1)S(1)}, u32[]{:S(2)}, u32[]{:S(2)}) collective-permute-start(bf16[16,64,128]{2,1,0:T(8,128)(2,1)S(1)} %bitcast.10), channel_id=1, source_target_pairs={{0,4},{4,8},{8,12},{12,16},{16,20},{20,24},{24,28},{28,32},{32,36}... | collective-permute-start | bytes 786440 | tf_op jit(solution)/shard_map/ppermute | solution.py:371

commit v6 on v5

--- a/solution.py
+++ b/solution.py
@@ -22,13 +22,12 @@
 F32 = jnp.float32
 BF16 = jnp.bfloat16
 HBM = pl.BlockSpec(memory_space=pltpu.HBM)
-ANY = pl.BlockSpec(memory_space=pl.ANY)
 OWNED = 8
 ELEM_FIELDS = 18
 PROBE = BLK
 ELEMS = PROBE + BLK_DEV * COLS
 SEND_ROWS = ELEMS + ELEM_FIELDS * OWNED
-UNROLL = 4
+UNROLL = 16
 
 
 def call(kernel, out_shape, in_specs, out_specs, scratch, flops, nbytes, vmem=40):
@@ -143,7 +142,7 @@
     )
     for c in copies[4:8]:
         c.wait()
-    rows = 256
+    rows = 512
     for part in range(cov_ref.shape[0] // rows):
         here = slice(part * rows, (part + 1) * rows)
         pre_act = jnp.dot(cov_ref[here, :], w1_ref[...], preferred_element_type=F32) + b1_ref[...]
@@ -200,29 +199,26 @@
 
 
 def finish_kernel(
-    info_ref, got_ref, tid_ref, geo_ref, pos_ref, before_hbm, own_hbm, after_hbm,
-    out_ref, hot_ref, val_ref, turned_ref, k_ref, x_ref, acc_ref, sem,
+    info_ref, got_ref, tid_ref, geo_ref, pos_ref, before_ref, own_ref, after_ref,
+    out_ref, hot_ref, val_ref, turned_ref, k_ref, acc_ref,
 ):
     blocks = SUBS * BLK_DEV
-    copies = start_all(
-        [(src, x_ref.at[blocks * i : blocks * (i + 1)]) for i, src in enumerate((before_hbm, own_hbm, after_hbm))], sem
-    )
     lane_iota = lax.broadcasted_iota(jnp.int32, (BLK, BLK), 0).astype(F32).astype(BF16)
     one, zero = jnp.ones((), BF16), jnp.zeros((), BF16)
     tiles = tid_ref[...].astype(BF16)
     found = jnp.zeros((6 * SLOTS, BLK), F32)
     for u in range(SUBS):
-        turned_ref[...] = got_ref[lanes(u), :].astype(F32).T
+        turned_ref[u] = got_ref[lanes(u), :].astype(F32).T
         for k in range(RANKS):
             rows = [
-                jnp.broadcast_to(turned_ref[f * RANKS + k : f * RANKS + k + 1, :], (16, BLK)).astype(BF16)
+                jnp.broadcast_to(turned_ref[u, f * RANKS + k : f * RANKS + k + 1, :], (16, BLK)).astype(BF16)
                 for f in range(FIELDS)
             ]
             twice = [jnp.concatenate([r, r], axis=0) for r in rows[:7]]
             mine = tiles == twice[6]
-            val_ref[:, lanes(k)] = jnp.concatenate([jnp.where(mine, twice[f], zero) for f in range(6)], axis=0)
-            hot_ref[:, lanes(k)] = jnp.where(lane_iota == jnp.concatenate([rows[7]] * 8, axis=0), one, zero)
-        found = found + lax.dot_general(val_ref[...], hot_ref[...], NT, preferred_element_type=F32)
+            val_ref[u, :, lanes(k)] = jnp.concatenate([jnp.where(mine, twice[f], zero) for f in range(6)], axis=0)
+            hot_ref[u, :, lanes(k)] = jnp.where(lane_iota == jnp.concatenate([rows[7]] * 8, axis=0), one, zero)
+        found = found + lax.dot_general(val_ref[u], hot_ref[u], NT, preferred_element_type=F32)
     params = [
         found[2 * f * SLOTS : (2 * f + 1) * SLOTS] + found[(2 * f + 1) * SLOTS : (2 * f + 2) * SLOTS]
         for f in range(3)
@@ -236,11 +232,15 @@
         stiffness = scale * (geo_ref[i] + coupling * geo_ref[6 + i])
         k_ref[i] = (area * (stiffness + mass)).astype(BF16).astype(F32)
     acc_ref[...] = jnp.zeros(acc_ref.shape, F32)
-    for c in copies:
-        c.wait()
 
     def tile_part(n):
-        x = x_ref[info_ref[1, n]].astype(F32)
+        col = info_ref[1, n]
+        at = col & (blocks - 1)
+        x = jnp.where(
+            col < blocks,
+            before_ref[at].astype(F32),
+            jnp.where(col < 2 * blocks, own_ref[at].astype(F32), after_ref[at].astype(F32)),
+        )
         k = [k_ref[i, pl.ds(n, 1), :] for i in range(6)]
         xs = [
             jnp.take_along_axis(x, jnp.broadcast_to(pos_ref[3 + b, pl.ds(n, 1), :], (COLS, BLK)), axis=1)
@@ -328,16 +328,14 @@
     return call(
         finish_kernel,
         jax.ShapeDtypeStruct((COLS, BLK_DEV * BLK), F32),
-        [SMEM] + [VMEM] * 4 + [ANY] * 3,
+        [SMEM] + [VMEM] * 7,
         VMEM,
         [
-            vm((BLK, RANKS * BLK), BF16),
-            vm((6 * SLOTS, RANKS * BLK), BF16),
-            vm((BLK, BLK), F32),
+            vm((SUBS, BLK, RANKS * BLK), BF16),
+            vm((SUBS, 6 * SLOTS, RANKS * BLK), BF16),
+            vm((SUBS, BLK, BLK), F32),
             vm((6, SLOTS, BLK), F32),
-            vm((3 * SUBS * BLK_DEV, COLS, BLK), BF16),
             vm((BLK_DEV, COLS, BLK), F32),
-            pltpu.SemaphoreType.DMA((3,)),
         ],
         1_000_000_000,
         3_000_000,

time: 63.6 us -> 62 us (0.975)
  Pallas kernels: 10.7 us -> 9.04 us
    pallas_call x1, Pallas kernels: 5.91 us -> 4.46 us  [finished(): call(finish_kernel, jax.ShapeDtypeStruct((COLS, BLK_DEV * BLK), F32), [SM...]
where the time goes in v6:
time: 62 us; the launch traced here: 61.6 us
  starting transfers between devices  28.2 us (45%)
  blocking collectives  11.9 us (19%)
  waiting for transfers between devices  11.7 us (19%)
  Pallas kernels  9.04 us (15%)
  local copies, waits for them, and re-layouts  0.79 us (1%)
    all_to_all x1, starting transfers between devices, local(): lax.all_to_all(routed, 'slab', split_axis=0, concat_axis=0, tiled=True)  22.6 us
    all_to_all x1, blocking collectives, local(): lax.all_to_all(send, 'sub', split_axis=0, concat_axis=0, tiled=True)  11.9 us
    all_to_all x1, waiting for transfers between devices, local(): lax.all_to_all(routed, 'slab', split_axis=0, concat_axis=0, tiled=True)  6.95 us
    ppermute x1, waiting for transfers between devices, local(): after = lax.ppermute(own, 'slab', [(j, i) for i, j in up])  4.72 us
    pallas_call x1, Pallas kernels, finished(): call(finish_kernel, jax.ShapeDtypeStruct((COLS, BLK_DEV * BLK), F32), [SM...  4.46 us
    pallas_call x1, Pallas kernels, front(): call(front_kernel, jax.ShapeDtypeStruct((SUBS, SEND_ROWS, BLK), BF16), [H...  4.45 us
    ppermute x1, starting transfers between devices, local(): after = lax.ppermute(own, 'slab', [(j, i) for i, j in up])  2.8 us
    ppermute x1, starting transfers between devices, local(): before = lax.ppermute(own, 'slab', up)  2.76 us
  transfers between devices with their start and end apart: 3, of which 2 were waited for; matrix products, arithmetic and copies ran while one was open for 0% of the time, Pallas kernels for 0%

profile of v6, /device:TPU:1, one launch (start us, length us, event | category | flops | bytes accessed | tf_op | source)
XLA Modules:
  0.0 61.6 jit_solution(6324610580570037505)
XLA Ops:
  0.0 4.5 %shard_map.118 = bf16[4,528,128]{2,1,0:T(8,128)(2,1)} custom-call(bf16[2048,128]{1,0:T(8,128)(2,1)} %cov_hbm.1, s32[2,2048]{1,0:T(2,128)} %slot_hbm.1, bf16[128,256]{1,0:T(8,128)(2,1)} %w1_hbm.1, f32[1,256]{1,0:T(1,128)} %bitcast.15, bf16[3,256]{1,0:T(4,128)(2,1)} %w2_hbm.1, f32[3]{0:T(128)} %b2_ref.1, f32[2,2,2048]{2,1,0:T(2,128)} %grad_hbm.1, ...), custom_call_target="tpu_custom_call" | custom-call | flops 400000000 | bytes 1000000 | tf_op jit(solution)/shard_map/pallas_call | solution.py:275
  4.5 11.9 %all_to_all.10.all_ref = bf16[4,528,128]{2,1,0:T(8,128)(2,1)S(1)} all-to-all(bf16[4,528,128]{2,1,0:T(8,128)(2,1)} %shard_map.118), channel_id=1, replica_groups=mesh['slab'=128,'sub'=4] {'sub'}, dimensions={0} | all-to-all | bytes 1081344 | tf_op jit(solution)/shard_map/all_to_all | solution.py:364
  16.3 0.8 %copy.14 = bf16[128,4,128]{2,1,0:T(4,128)(2,1)} copy(bf16[128,4,128]{2,0,1:T(8,128)(2,1)S(1)} %slice_bitcast_fusion) | data formatting | bytes 262144 | tf_op jit(solution)/shard_map/transpose | solution.py:365
  17.1 22.6 %all-to-all-start.1 = ((bf16[128,4,128]{2,1,0:T(4,128)(2,1)}), bf16[128,4,128]{2,1,0:T(4,128)(2,1)S(1)}, u32[]{:S(2)}, u32[]{:S(2)}) async-start(bf16[128,4,128]{2,1,0:T(4,128)(2,1)} %copy.14), calls=%async_computation.1 | async-start | bytes 262144 | tf_op jit(solution)/shard_map/all_to_all | solution.py:366
  39.8 2.8 %collective-permute-start.1 = (bf16[16,64,128]{2,1,0:T(8,128)(2,1)S(1)}, bf16[16,64,128]{2,1,0:T(8,128)(2,1)S(1)}, u32[]{:S(2)}, u32[]{:S(2)}) collective-permute-start(bf16[16,64,128]{2,1,0:T(8,128)(2,1)S(1)} %bitcast.9), channel_id=1, source_target_pairs={{4,0},{8,4},{12,8},{16,12},{20,16},{24,20},{28,24},{32,28},{36,32}... | collective-permute-start | bytes 786440 | tf_op jit(solution)/shard_map/ppermute | solution.py:370
  42.6 2.8 %collective-permute-start = (bf16[16,64,128]{2,1,0:T(8,128)(2,1)S(1)}, bf16[16,64,128]{2,1,0:T(8,128)(2,1)S(1)}, u32[]{:S(2)}, u32[]{:S(2)}) collective-permute-start(bf16[16,64,128]{2,1,0:T(8,128)(2,1)S(1)} %bitcast.10), channel_id=1, source_target_pairs={{0,4},{4,8},{8,12},{12,16},{16,20},{20,24},{24,28},{28,32},{32,36}... | collective-permute-start | bytes 786440 | tf_op jit(solution)/shard_map/ppermute | solution.py:369
  45.4 0.1 shard_map.119
  45.5 4.7 %collective-permute-done.1.after_ref = bf16[16,64,128]{2,1,0:T(8,128)(2,1)S(1)} collective-permute-done((bf16[16,64,128]{2,1,0:T(8,128)(2,1)S(1)}, bf16[16,64,128]{2,1,0:T(8,128)(2,1)S(1)}, u32[]{:S(2)}, u32[]{:S(2)}) %collective-permute-start.1) | collective-permute-done | bytes 262176 | tf_op jit(solution)/shard_map/ppermute | solution.py:370
  50.2 0.0 collective-permute-done.before_ref
  50.2 7.0 %all-to-all-done.1 = bf16[128,4,128]{2,1,0:T(4,128)(2,1)S(1)} async-done(((bf16[128,4,128]{2,1,0:T(4,128)(2,1)}), bf16[128,4,128]{2,1,0:T(4,128)(2,1)S(1)}, u32[]{:S(2)}, u32[]{:S(2)}) %all-to-all-start.1) | async-done | bytes 131104 | tf_op jit(solution)/shard_map/all_to_all | solution.py:366
  57.2 4.5 %shard_map.120 = f32[64,512]{1,0:T(8,128)} custom-call(s32[8,128]{1,0:T(8,128)S(1)} %get-tuple-element.9.info_ref, bf16[512,128]{1,0:T(8,128)(2,1)S(1)} %bitcast.12, f32[32,128]{1,0:T(8,128)S(1)} %get-tuple-element.10.tid_ref, f32[13,32,128]{2,1,0:T(8,128)S(1)} %get-tuple-element.11.geo_ref, s32[6,32,128]{2,1,0:T(8,128)S(1)} %get-tuple-element.12.pos_ref, ...), custom_call_target="tpu_custom_call" | custom-call | flops 1000000000 | bytes 3000000 | tf_op jit(solution)/shard_map/pallas_call | solution.py:328
  (2 shorter events, 0.0 us)
Async XLA Ops:
  17.1 40.1 %all-to-all-start.1 = ((bf16[128,4,128]{2,1,0:T(4,128)(2,1)}), bf16[128,4,128]{2,1,0:T(4,128)(2,1)S(1)}, u32[]{:S(2)}, u32[]{:S(2)}) async-start(bf16[128,4,128]{2,1,0:T(4,128)(2,1)} %copy.14), calls=%async_computation.1 | async-start | bytes 262144 | tf_op jit(solution)/shard_map/all_to_all | solution.py:366
  39.8 10.4 %collective-permute-start.1 = (bf16[16,64,128]{2,1,0:T(8,128)(2,1)S(1)}, bf16[16,64,128]{2,1,0:T(8,128)(2,1)S(1)}, u32[]{:S(2)}, u32[]{:S(2)}) collective-permute-start(bf16[16,64,128]{2,1,0:T(8,128)(2,1)S(1)} %bitcast.9), channel_id=1, source_target_pairs={{4,0},{8,4},{12,8},{16,12},{20,16},{24,20},{28,24},{32,28},{36,32}... | collective-permute-start | bytes 786440 | tf_op jit(solution)/shard_map/ppermute | solution.py:370
  42.6 7.6 %collective-permute-start = (bf16[16,64,128]{2,1,0:T(8,128)(2,1)S(1)}, bf16[16,64,128]{2,1,0:T(8,128)(2,1)S(1)}, u32[]{:S(2)}, u32[]{:S(2)}) collective-permute-start(bf16[16,64,128]{2,1,0:T(8,128)(2,1)S(1)} %bitcast.10), channel_id=1, source_target_pairs={{0,4},{4,8},{8,12},{12,16},{16,20},{20,24},{24,28},{28,32},{32,36}... | collective-permute-start | bytes 786440 | tf_op jit(solution)/shard_map/ppermute | solution.py:369

commit v7 on v6

--- a/solution.py
+++ b/solution.py
@@ -60,16 +60,17 @@
 
 def front_kernel(
     cov_hbm, slot_hbm, w1_hbm, b1_hbm, w2_hbm, b2_ref, grad_hbm, area_hbm, corner_hbm, rows_ref, cols_ref, probe_hbm,
-    out_hbm,
+    out_ref,
     cov_ref, slot_ref, w1_ref, b1_ref, w2_ref, grad_ref, area_ref, corner_ref, tile_ref,
-    hot_ref, rank_ref, val_ref, par_ref, send_ref, elem_ref, sem, out_sem,
+    hot_ref, rank_ref, val_ref, par_ref, sem,
 ):
     copies = start_all(
         (
             (slot_hbm, slot_ref), (grad_hbm, grad_ref), (area_hbm, area_ref), (corner_hbm, corner_ref),
             (w1_hbm, w1_ref), (b1_hbm, b1_ref), (w2_hbm, w2_ref), (cov_hbm, cov_ref),
             *(
-                (probe_hbm.at[:, lanes(b)], send_ref.at[PROBE + b * COLS : PROBE + (b + 1) * COLS])
+                (probe_hbm.at[:, lanes(b)], out_ref.at[d, PROBE + b * COLS : PROBE + (b + 1) * COLS])
+                for d in range(SUBS)
                 for b in range(BLK_DEV)
             ),
         ),
@@ -130,16 +131,9 @@
     fields += [facts[:TILE_DEV], jnp.zeros((TILE_DEV, BLK), F32)]
     picked = jnp.dot(pick, jnp.concatenate(fields, axis=1).astype(BF16), preferred_element_type=F32)
     for d in range(SUBS):
-        elem_ref[d] = jnp.concatenate(
+        out_ref[d, ELEMS:, :] = jnp.concatenate(
             [picked[d * OWNED : (d + 1) * OWNED, lanes(f)] for f in range(ELEM_FIELDS)], axis=0
         ).astype(BF16)
-    for c in copies[8:]:
-        c.wait()
-    outs = start_all(
-        [(send_ref.at[PROBE:], out_hbm.at[d, PROBE:ELEMS]) for d in range(SUBS)]
-        + [(elem_ref.at[d], out_hbm.at[d, ELEMS:]) for d in range(SUBS)],
-        out_sem,
-    )
     for c in copies[4:8]:
         c.wait()
     rows = 512
@@ -160,16 +154,10 @@
         val_ref[:, lanes(chunk)] = jnp.concatenate(
             [jnp.where(ranked, v, 0.0).astype(BF16) for v in values], axis=0
         )
-    send_ref[0:PROBE, :] = lax.dot_general(
-        hot_ref[...], val_ref[...], NT, preferred_element_type=F32
-    ).astype(BF16)
-    last = [
-        pltpu.make_async_copy(send_ref.at[:PROBE], out_hbm.at[d, :PROBE], out_sem.at[2 * SUBS + d])
-        for d in range(SUBS)
-    ]
-    for c in last:
-        c.start()
-    for c in outs + last:
+    routed = lax.dot_general(hot_ref[...], val_ref[...], NT, preferred_element_type=F32).astype(BF16)
+    for d in range(SUBS):
+        out_ref[d, 0:PROBE, :] = routed
+    for c in copies[8:]:
         c.wait()
 
 
@@ -276,7 +264,7 @@
         front_kernel,
         jax.ShapeDtypeStruct((SUBS, SEND_ROWS, BLK), BF16),
         [HBM] * 5 + [SMEM] + [HBM] * 3 + [VMEM] * 2 + [HBM],
-        HBM,
+        VMEM,
         [
             vm(covariates.shape, BF16),
             vm(partition_slot.shape, jnp.int32),
@@ -291,10 +279,7 @@
             vm((1, elements), F32),
             vm((BLK, elements), BF16),
             vm((3, elements), F32),
-            vm((ELEMS, BLK), BF16),
-            vm((SUBS, ELEM_FIELDS * OWNED, BLK), BF16),
-            pltpu.SemaphoreType.DMA((8 + BLK_DEV,)),
-            pltpu.SemaphoreType.DMA((3 * SUBS,)),
+            pltpu.SemaphoreType.DMA((8 + SUBS * BLK_DEV,)),
         ],
         400_000_000,
         1_000_000,

time: 62 us -> 62.1 us (level)
  no operation moved by 1% of the time
where the time goes in v7:
time: 62.1 us; the launch traced here: 61.8 us
  starting transfers between devices  28.2 us (45%)
  blocking collectives  11.9 us (19%)
  waiting for transfers between devices  11.7 us (19%)
  Pallas kernels  9.18 us (15%)
  local copies, waits for them, and re-layouts  0.79 us (1%)
    all_to_all x1, starting transfers between devices, local(): lax.all_to_all(routed, 'slab', split_axis=0, concat_axis=0, tiled=True)  22.7 us
    all_to_all x1, blocking collectives, local(): lax.all_to_all(send, 'sub', split_axis=0, concat_axis=0, tiled=True)  11.9 us
    all_to_all x1, waiting for transfers between devices, local(): lax.all_to_all(routed, 'slab', split_axis=0, concat_axis=0, tiled=True)  6.95 us
    ppermute x1, waiting for transfers between devices, local(): after = lax.ppermute(own, 'slab', [(j, i) for i, j in up])  4.72 us
    pallas_call x1, Pallas kernels, front(): call(front_kernel, jax.ShapeDtypeStruct((SUBS, SEND_ROWS, BLK), BF16), [H...  4.6 us
    pallas_call x1, Pallas kernels, finished(): call(finish_kernel, jax.ShapeDtypeStruct((COLS, BLK_DEV * BLK), F32), [SM...  4.45 us
    ppermute x1, starting transfers between devices, local(): after = lax.ppermute(own, 'slab', [(j, i) for i, j in up])  2.8 us
    ppermute x1, starting transfers between devices, local(): before = lax.ppermute(own, 'slab', up)  2.76 us
  transfers between devices with their start and end apart: 3, of which 2 were waited for; matrix products, arithmetic and copies ran while one was open for 0% of the time, Pallas kernels for 0%

profile of v7, /device:TPU:1, one launch (start us, length us, event | category | flops | bytes accessed | tf_op | source)
XLA Modules:
  0.0 61.8 jit_solution(861893967854188752)
XLA Ops:
  0.0 4.6 %shard_map.118 = bf16[4,528,128]{2,1,0:T(8,128)(2,1)} custom-call(bf16[2048,128]{1,0:T(8,128)(2,1)} %cov_hbm.1, s32[2,2048]{1,0:T(2,128)} %slot_hbm.1, bf16[128,256]{1,0:T(8,128)(2,1)} %w1_hbm.1, f32[1,256]{1,0:T(1,128)} %bitcast.15, bf16[3,256]{1,0:T(4,128)(2,1)} %w2_hbm.1, f32[3]{0:T(128)} %b2_ref.1, f32[2,2,2048]{2,1,0:T(2,128)} %grad_hbm.1, ...), custom_call_target="tpu_custom_call" | custom-call | flops 400000000 | bytes 1000000 | tf_op jit(solution)/shard_map/pallas_call | solution.py:263
  4.6 11.9 %all_to_all.10.all_ref = bf16[4,528,128]{2,1,0:T(8,128)(2,1)S(1)} all-to-all(bf16[4,528,128]{2,1,0:T(8,128)(2,1)} %shard_map.118), channel_id=1, replica_groups=mesh['slab'=128,'sub'=4] {'sub'}, dimensions={0} | all-to-all | bytes 1081344 | tf_op jit(solution)/shard_map/all_to_all | solution.py:349
  16.5 0.8 %copy.14 = bf16[128,4,128]{2,1,0:T(4,128)(2,1)} copy(bf16[128,4,128]{2,0,1:T(8,128)(2,1)S(1)} %slice_bitcast_fusion) | data formatting | bytes 262144 | tf_op jit(solution)/shard_map/transpose | solution.py:350
  17.3 22.7 %all-to-all-start.1 = ((bf16[128,4,128]{2,1,0:T(4,128)(2,1)}), bf16[128,4,128]{2,1,0:T(4,128)(2,1)S(1)}, u32[]{:S(2)}, u32[]{:S(2)}) async-start(bf16[128,4,128]{2,1,0:T(4,128)(2,1)} %copy.14), calls=%async_computation.1 | async-start | bytes 262144 | tf_op jit(solution)/shard_map/all_to_all | solution.py:351
  40.0 2.8 %collective-permute-start.1 = (bf16[16,64,128]{2,1,0:T(8,128)(2,1)S(1)}, bf16[16,64,128]{2,1,0:T(8,128)(2,1)S(1)}, u32[]{:S(2)}, u32[]{:S(2)}) collective-permute-start(bf16[16,64,128]{2,1,0:T(8,128)(2,1)S(1)} %bitcast.9), channel_id=1, source_target_pairs={{4,0},{8,4},{12,8},{16,12},{20,16},{24,20},{28,24},{32,28},{36,32}... | collective-permute-start | bytes 786440 | tf_op jit(solution)/shard_map/ppermute | solution.py:355
  42.8 2.8 %collective-permute-start = (bf16[16,64,128]{2,1,0:T(8,128)(2,1)S(1)}, bf16[16,64,128]{2,1,0:T(8,128)(2,1)S(1)}, u32[]{:S(2)}, u32[]{:S(2)}) collective-permute-start(bf16[16,64,128]{2,1,0:T(8,128)(2,1)S(1)} %bitcast.10), channel_id=1, source_target_pairs={{0,4},{4,8},{8,12},{12,16},{16,20},{20,24},{24,28},{28,32},{32,36}... | collective-permute-start | bytes 786440 | tf_op jit(solution)/shard_map/ppermute | solution.py:354
  45.5 0.1 shard_map.119
  45.7 4.7 %collective-permute-done.1.after_ref = bf16[16,64,128]{2,1,0:T(8,128)(2,1)S(1)} collective-permute-done((bf16[16,64,128]{2,1,0:T(8,128)(2,1)S(1)}, bf16[16,64,128]{2,1,0:T(8,128)(2,1)S(1)}, u32[]{:S(2)}, u32[]{:S(2)}) %collective-permute-start.1) | collective-permute-done | bytes 262176 | tf_op jit(solution)/shard_map/ppermute | solution.py:355
  50.4 0.0 collective-permute-done.before_ref
  50.4 7.0 %all-to-all-done.1 = bf16[128,4,128]{2,1,0:T(4,128)(2,1)S(1)} async-done(((bf16[128,4,128]{2,1,0:T(4,128)(2,1)}), bf16[128,4,128]{2,1,0:T(4,128)(2,1)S(1)}, u32[]{:S(2)}, u32[]{:S(2)}) %all-to-all-start.1) | async-done | bytes 131104 | tf_op jit(solution)/shard_map/all_to_all | solution.py:351
  57.3 4.5 %shard_map.120 = f32[64,512]{1,0:T(8,128)} custom-call(s32[8,128]{1,0:T(8,128)S(1)} %get-tuple-element.9.info_ref, bf16[512,128]{1,0:T(8,128)(2,1)S(1)} %bitcast.12, f32[32,128]{1,0:T(8,128)S(1)} %get-tuple-element.10.tid_ref, f32[13,32,128]{2,1,0:T(8,128)S(1)} %get-tuple-element.11.geo_ref, s32[6,32,128]{2,1,0:T(8,128)S(1)} %get-tuple-element.12.pos_ref, ...), custom_call_target="tpu_custom_call" | custom-call | flops 1000000000 | bytes 3000000 | tf_op jit(solution)/shard_map/pallas_call | solution.py:313
  (2 shorter events, 0.0 us)
Async XLA Ops:
  17.3 40.1 %all-to-all-start.1 = ((bf16[128,4,128]{2,1,0:T(4,128)(2,1)}), bf16[128,4,128]{2,1,0:T(4,128)(2,1)S(1)}, u32[]{:S(2)}, u32[]{:S(2)}) async-start(bf16[128,4,128]{2,1,0:T(4,128)(2,1)} %copy.14), calls=%async_computation.1 | async-start | bytes 262144 | tf_op jit(solution)/shard_map/all_to_all | solution.py:351
  40.0 10.4 %collective-permute-start.1 = (bf16[16,64,128]{2,1,0:T(8,128)(2,1)S(1)}, bf16[16,64,128]{2,1,0:T(8,128)(2,1)S(1)}, u32[]{:S(2)}, u32[]{:S(2)}) collective-permute-start(bf16[16,64,128]{2,1,0:T(8,128)(2,1)S(1)} %bitcast.9), channel_id=1, source_target_pairs={{4,0},{8,4},{12,8},{16,12},{20,16},{24,20},{28,24},{32,28},{36,32}... | collective-permute-start | bytes 786440 | tf_op jit(solution)/shard_map/ppermute | solution.py:355
  42.8 7.6 %collective-permute-start = (bf16[16,64,128]{2,1,0:T(8,128)(2,1)S(1)}, bf16[16,64,128]{2,1,0:T(8,128)(2,1)S(1)}, u32[]{:S(2)}, u32[]{:S(2)}) collective-permute-start(bf16[16,64,128]{2,1,0:T(8,128)(2,1)S(1)} %bitcast.10), channel_id=1, source_target_pairs={{0,4},{4,8},{8,12},{12,16},{16,20},{20,24},{24,28},{28,32},{32,36}... | collective-permute-start | bytes 786440 | tf_op jit(solution)/shard_map/ppermute | solution.py:354
